TPU v7x, 32 devices: a whole 2x2x4 slice. The times are simulated.
32 devices in a mesh: ctx: 8 (over z, core), wsh: 4 (over y, x).
Axes of the slice: x: 2, y: 2, z: 4, core: 2. Of those that a mesh axis runs over, the one named last changes fastest.
Arguments:
- tokens: bfloat16 [16, 2048, 1536], P('wsh', 'ctx'), may hold values from -6 to 6
- cotangent: bfloat16 [16, 2048, 1536], P('wsh', 'ctx'), may hold values from -6 to 6
- group_slot: int32 [12], replicated, may hold values from 0 to 15, as said below
- group_adapter: int32 [12], replicated, may hold values from 0 to 7
- attn_gain: bfloat16 [1536], replicated, may hold values from 0.5 to 1.5
- mlp_gain: bfloat16 [1536], replicated, may hold values from 0.5 to 1.5
- w_query: bfloat16 [1536, 1536], P('wsh', 'ctx'), may hold values from -0.15625 to 0.15625
- w_key: bfloat16 [1536, 256], P('wsh', 'ctx'), may hold values from -0.15625 to 0.15625
- w_value: bfloat16 [1536, 256], P('wsh', 'ctx'), may hold values from -0.15625 to 0.15625
- w_output: bfloat16 [1536, 1536], P('wsh', 'ctx'), may hold values from -1.25 to 1.25
- w_gate: bfloat16 [1536, 8960], P('wsh', 'ctx'), may hold values from -0.15625 to 0.15625
- w_up: bfloat16 [1536, 8960], P('wsh', 'ctx'), may hold values from -0.15625 to 0.15625
- w_down: bfloat16 [8960, 1536], P('wsh', 'ctx'), may hold values from -0.0625 to 0.0625
- query_bias: bfloat16 [1536], replicated, may hold values from -3 to 3
- key_bias: bfloat16 [256], replicated, may hold values from -3 to 3
- value_bias: bfloat16 [256], replicated, may hold values from -3 to 3
- adapt_query_in: bfloat16 [8, 16, 1536], replicated, may hold values from -0.15625 to 0.15625
- adapt_query_out: bfloat16 [8, 16, 1536], replicated, may hold values from -1.5 to 1.5
- adapt_key_in: bfloat16 [8, 16, 1536], replicated, may hold values from -0.15625 to 0.15625
- adapt_key_out: bfloat16 [8, 16, 256], replicated, may hold values from -1.5 to 1.5
- adapt_value_in: bfloat16 [8, 16, 1536], replicated, may hold values from -0.15625 to 0.15625
- adapt_value_out: bfloat16 [8, 16, 256], replicated, may hold values from -1.5 to 1.5
- adapt_output_in: bfloat16 [8, 16, 1536], replicated, may hold values from -1.25 to 1.25
- adapt_output_out: bfloat16 [8, 16, 1536], replicated, may hold values from -1.5 to 1.5
- adapt_gate_in: bfloat16 [8, 16, 1536], replicated, may hold values from -0.15625 to 0.15625
- adapt_gate_out: bfloat16 [8, 16, 8960], replicated, may hold values from -1.5 to 1.5
- adapt_up_in: bfloat16 [8, 16, 1536], replicated, may hold values from -0.15625 to 0.15625
- adapt_up_out: bfloat16 [8, 16, 8960], replicated, may hold values from -1.5 to 1.5
- adapt_down_in: bfloat16 [8, 16, 8960], replicated, may hold values from -0.0625 to 0.0625
- adapt_down_out: bfloat16 [8, 16, 1536], replicated, may hold values from -1.5 to 1.5
Outputs:
- layer_out: bfloat16 [16, 2048, 1536], P('wsh', 'ctx')
- input_grad: bfloat16 [16, 2048, 1536], P('wsh', 'ctx')
- grad_query_in: float32 [8, 16, 1536], replicated
- grad_query_out: float32 [8, 16, 1536], replicated
- grad_key_in: float32 [8, 16, 1536], replicated
- grad_key_out: float32 [8, 16, 256], replicated
- grad_value_in: float32 [8, 16, 1536], replicated
- grad_value_out: float32 [8, 16, 256], replicated
- grad_output_in: float32 [8, 16, 1536], replicated
- grad_output_out: float32 [8, 16, 1536], replicated
- grad_gate_in: float32 [8, 16, 1536], replicated
- grad_gate_out: float32 [8, 16, 8960], replicated
- grad_up_in: float32 [8, 16, 1536], replicated
- grad_up_out: float32 [8, 16, 8960], replicated
- grad_down_in: float32 [8, 16, 8960], replicated
- grad_down_out: float32 [8, 16, 1536], replicated
Inputs may be any that keep to these rules, and one draw needn't show every extreme that they name: 12 distinct slot numbers; group g fills slot group_slot[g], which weight shard group_slot[g] // 4 holds; slots that no group names are empty.
All inputs are finite; a program needn't handle non-finite values.
Results may differ from a plain program's by a relative error of at most 0.023.
Values may be sent and summed in bfloat16 or wider, within the bound.
No kernel may reach another device: no remote copies, remote signals or barrier semaphores. Data moves between devices by JAX's collectives and lax.ppermute only.
A program may use at most 512 MiB of HBM per device.

v0:
```python
import jax
import jax.numpy as jnp
from jax import lax
from jax.sharding import PartitionSpec as P

HEAD_DIM = 128
PROMPT = 1024
CONTS = 4
CONT = 256


norm_eps = 1e-06
adapter_scale = 0.5
rope_base = 1000000.0
masked_score = -1e30


def passed_along(array, axis, by):
    peers = lax.axis_size(axis)
    return lax.ppermute(array, axis, [(i, (i + by) % peers) for i in range(peers)])


def token_layout(token_index):
    cont_tokens = CONTS * CONT
    in_prompt = token_index >= cont_tokens
    segment = jnp.where(in_prompt, 0, 1 + token_index // CONT)
    position = jnp.where(in_prompt, token_index - cont_tokens, PROMPT + token_index % CONT)
    return (segment, position)


def visible(query_index, query_segment, source, block_len):
    key_index = source * block_len + jnp.arange(block_len, dtype=jnp.int32)
    key_segment, key_position = token_layout(key_index)
    same_part = (key_index[None, :] <= query_index[:, None]) & (
        key_segment[None, :] == query_segment[:, None]
    )
    return same_part | (key_segment[None, :] == 0) & (query_segment[:, None] != 0)


def rotate(values, position, direction):
    half_dim = values.shape[-1] // 2
    frequency = rope_base ** (-(jnp.arange(half_dim, dtype=jnp.float32) * 2.0) / values.shape[-1])
    angles = position.astype(jnp.float32)[:, None] * frequency[None, :]
    cosine_table = jnp.concatenate([jnp.cos(angles), jnp.cos(angles)], axis=-1)
    sine_table = direction * jnp.concatenate([jnp.sin(angles), jnp.sin(angles)], axis=-1)
    turned = jnp.concatenate([-values[..., half_dim:], values[..., :half_dim]], axis=-1)
    layout = (position.shape[0],) + (1,) * (values.ndim - 3) + (values.shape[-1],)
    return values * cosine_table.reshape(layout) + turned * sine_table.reshape(layout)


def rms_forward(hidden, gain_vec):
    return (
        hidden * lax.rsqrt(jnp.mean(hidden * hidden, axis=-1, keepdims=True) + norm_eps) * gain_vec
    )


def rms_backward(hidden, gain_vec, grad_normed):
    scaled = grad_normed * gain_vec
    inverse = lax.rsqrt(jnp.mean(hidden * hidden, axis=-1, keepdims=True) + norm_eps)
    return inverse * scaled - hidden * inverse**3 * jnp.mean(
        scaled * hidden, axis=-1, keepdims=True
    )


def project(input_rows, weight):
    return jnp.einsum("sbi,io->sbo", input_rows, weight, preferred_element_type=jnp.float32)


def project_back(incoming_gradient, weight):
    return jnp.einsum("sbo,io->sbi", incoming_gradient, weight, preferred_element_type=jnp.float32)


def adapter_forward(input_rows, selected_down_weight, selected_up_weight):
    projected_rank_rows = jnp.einsum(
        "ehn,ekn->ehk", input_rows, selected_down_weight, preferred_element_type=jnp.float32
    ).astype(jnp.bfloat16)
    return (
        projected_rank_rows,
        adapter_scale
        * jnp.einsum(
            "ivu,iup->ivp",
            projected_rank_rows,
            selected_up_weight,
            preferred_element_type=jnp.float32,
        ),
    )


def adapter_backward(
    incoming_gradient, input_rows, projected_rank_rows, selected_down_weight, selected_up_weight
):
    rank_space_gradient = (
        adapter_scale
        * jnp.einsum(
            "wdn,wxn->wdx",
            incoming_gradient,
            selected_up_weight,
            preferred_element_type=jnp.float32,
        )
    ).astype(jnp.bfloat16)
    back_to_input = jnp.einsum(
        "pec,pcn->pen",
        rank_space_gradient,
        selected_down_weight,
        preferred_element_type=jnp.float32,
    )
    down_weight_gradient = jnp.einsum(
        "jgq,jgu->jqu", rank_space_gradient, input_rows, preferred_element_type=jnp.float32
    )
    grad_up = adapter_scale * jnp.einsum(
        "yct,yca->yta", projected_rank_rows, incoming_gradient, preferred_element_type=jnp.float32
    )
    return (back_to_input, down_weight_gradient, grad_up)


def cycle_attend(queries, key_value, query_index, query_segment, cycle_place, cycle_size):
    slot_count, block_len, kv_heads, group_size, head_dim = queries.shape
    score_scale = head_dim ** (-0.5)

    def cycle_step(cycle_state, cycle_turn):
        moving, running_max, running_sum, accumulated = cycle_state
        allowed = visible(
            query_index, query_segment, (cycle_place - cycle_turn) % cycle_size, block_len
        )
        scores = (
            jnp.einsum("sbkgd,stkd->skgbt", queries, moving[0], preferred_element_type=jnp.float32)
            * score_scale
        )
        scores = jnp.where(allowed, scores, masked_score)
        new_max = jnp.maximum(running_max, jnp.max(scores, axis=-1))
        weights = jnp.where(allowed, jnp.exp(scores - new_max[..., None]), 0.0)
        factor = jnp.exp(running_max - new_max)
        running_sum = running_sum * factor + jnp.sum(weights, axis=-1)
        accumulated = accumulated * jnp.transpose(factor, (0, 3, 1, 2))[..., None] + jnp.einsum(
            "skgbt,stkd->sbkgd",
            weights.astype(jnp.bfloat16),
            moving[1],
            preferred_element_type=jnp.float32,
        )
        moving = passed_along(moving, "ctx", 1)
        return ((moving, new_max, running_sum, accumulated), None)

    stat_shape = (slot_count, kv_heads, group_size, block_len)
    start_state = (
        key_value,
        jnp.full(stat_shape, masked_score, jnp.float32),
        jnp.zeros(stat_shape, jnp.float32),
        jnp.zeros(queries.shape, jnp.float32),
    )
    final_state, unused = lax.scan(cycle_step, start_state, jnp.arange(cycle_size, dtype=jnp.int32))
    running_max, running_sum, accumulated = (final_state[1], final_state[2], final_state[3])
    mixed = accumulated / jnp.transpose(running_sum, (0, 3, 1, 2))[..., None]
    return (mixed, running_max + jnp.log(running_sum))


def cycle_attend_back(
    queries,
    key_value,
    grad_mixed,
    log_total,
    delta_rows,
    query_index,
    query_segment,
    cycle_place,
    cycle_size,
):
    slot_count, block_len, kv_heads, group_size, head_dim = queries.shape
    score_scale = head_dim ** (-0.5)

    def cycle_step(cycle_state, cycle_turn):
        moving, moving_grads, grad_query = cycle_state
        allowed = visible(
            query_index, query_segment, (cycle_place - cycle_turn) % cycle_size, block_len
        )
        scores = (
            jnp.einsum("sbkgd,stkd->skgbt", queries, moving[0], preferred_element_type=jnp.float32)
            * score_scale
        )
        scores = jnp.where(allowed, scores, masked_score)
        probs_now = jnp.where(allowed, jnp.exp(scores - log_total[..., None]), 0.0)
        grad_value = jnp.einsum(
            "skgbt,sbkgd->stkd",
            probs_now.astype(jnp.bfloat16),
            grad_mixed,
            preferred_element_type=jnp.float32,
        )
        grad_probs = jnp.einsum(
            "sbkgd,stkd->skgbt", grad_mixed, moving[1], preferred_element_type=jnp.float32
        )
        grad_scores = (probs_now * (grad_probs - delta_rows[..., None])).astype(jnp.bfloat16)
        grad_query = grad_query + score_scale * jnp.einsum(
            "skgbt,stkd->sbkgd", grad_scores, moving[0], preferred_element_type=jnp.float32
        )
        grad_key = score_scale * jnp.einsum(
            "skgbt,sbkgd->stkd", grad_scores, queries, preferred_element_type=jnp.float32
        )
        moving_grads = moving_grads + jnp.stack([grad_key, grad_value])
        moving = passed_along(moving, "ctx", 1)
        moving_grads = passed_along(moving_grads.astype(jnp.bfloat16), "ctx", 1).astype(
            moving_grads.dtype
        )
        return ((moving, moving_grads, grad_query), None)

    start_state = (
        key_value,
        jnp.zeros(key_value.shape, jnp.float32),
        jnp.zeros(queries.shape, jnp.float32),
    )
    final_state, unused = lax.scan(cycle_step, start_state, jnp.arange(cycle_size, dtype=jnp.int32))
    return (final_state[2], final_state[1])


def local(
    tokens,
    cotangent,
    group_slot,
    group_adapter,
    attn_gain,
    mlp_gain,
    w_query,
    w_key,
    w_value,
    w_output,
    w_gate,
    w_up,
    w_down,
    query_bias,
    key_bias,
    value_bias,
    adapt_query_in,
    adapt_query_out,
    adapt_key_in,
    adapt_key_out,
    adapt_value_in,
    adapt_value_out,
    adapt_output_in,
    adapt_output_out,
    adapt_gate_in,
    adapt_gate_out,
    adapt_up_in,
    adapt_up_out,
    adapt_down_in,
    adapt_down_out,
):
    slot_count, block_len, width = tokens.shape
    cycle_size = lax.axis_size("ctx")
    cycle_place = lax.axis_index("ctx")
    shard_place = lax.axis_index("wsh")
    slot_ids = shard_place * slot_count + jnp.arange(slot_count, dtype=jnp.int32)
    matches = group_slot[None, :] == slot_ids[:, None]
    live_slot = jnp.any(matches, axis=1).astype(jnp.float32)
    adapter_of = jnp.sum(jnp.where(matches, group_adapter[None, :], 0), axis=1)
    adapter_count = adapt_query_in.shape[0]
    choose = (adapter_of[:, None] == jnp.arange(adapter_count, dtype=jnp.int32)[None, :]).astype(
        jnp.float32
    ) * live_slot[:, None]
    live_rows = live_slot[:, None, None]
    query_index = cycle_place * block_len + jnp.arange(block_len, dtype=jnp.int32)
    query_segment, position = token_layout(query_index)
    shards = (w_query, w_key, w_value, w_output, w_gate, w_up, w_down)
    full_rows = (
        lax.all_gather(shards[0], "wsh", axis=0, tiled=True),
        lax.all_gather(shards[1], "wsh", axis=0, tiled=True),
        lax.all_gather(shards[2], "wsh", axis=0, tiled=True),
        lax.all_gather(shards[3], "wsh", axis=0, tiled=True),
        lax.all_gather(shards[4], "wsh", axis=0, tiled=True),
        lax.all_gather(shards[5], "wsh", axis=0, tiled=True),
        lax.all_gather(shards[6], "wsh", axis=0, tiled=True),
    )
    weights_now = (
        lax.all_gather(full_rows[0], "ctx", axis=1, tiled=True),
        lax.all_gather(full_rows[1], "ctx", axis=1, tiled=True),
        lax.all_gather(full_rows[2], "ctx", axis=1, tiled=True),
        lax.all_gather(full_rows[3], "ctx", axis=1, tiled=True),
        lax.all_gather(full_rows[4], "ctx", axis=1, tiled=True),
        lax.all_gather(full_rows[5], "ctx", axis=1, tiled=True),
        lax.all_gather(full_rows[6], "ctx", axis=1, tiled=True),
    )
    query_full, key_full, value_full, output_full, gate_full, up_full, down_full = weights_now
    adapter_pairs = (
        (adapt_query_in, adapt_query_out),
        (adapt_key_in, adapt_key_out),
        (adapt_value_in, adapt_value_out),
        (adapt_output_in, adapt_output_out),
        (adapt_gate_in, adapt_gate_out),
        (adapt_up_in, adapt_up_out),
        (adapt_down_in, adapt_down_out),
    )
    picked = [
        (jnp.take(pair_in, adapter_of, axis=0), jnp.take(pair_out, adapter_of, axis=0))
        for pair_in, pair_out in adapter_pairs
    ]
    kv_heads = key_full.shape[1] // HEAD_DIM
    group_size = width // HEAD_DIM // kv_heads
    gain_one = attn_gain.astype(jnp.float32)
    gain_two = mlp_gain.astype(jnp.float32)
    hidden = tokens.astype(jnp.float32)
    normed = rms_forward(hidden, gain_one).astype(jnp.bfloat16)
    rank_query, extra_query = adapter_forward(normed, picked[0][0], picked[0][1])
    rank_key, extra_key = adapter_forward(normed, picked[1][0], picked[1][1])
    rank_value, extra_value = adapter_forward(normed, picked[2][0], picked[2][1])
    query_lin = project(normed, query_full) + query_bias.astype(jnp.float32) + extra_query
    key_lin = project(normed, key_full) + key_bias.astype(jnp.float32) + extra_key
    value_lin = project(normed, value_full) + value_bias.astype(jnp.float32) + extra_value
    queries = rotate(
        query_lin.reshape(slot_count, block_len, kv_heads, group_size, HEAD_DIM), position, 1.0
    ).astype(jnp.bfloat16)
    keys_local = rotate(
        key_lin.reshape(slot_count, block_len, kv_heads, HEAD_DIM), position, 1.0
    ).astype(jnp.bfloat16)
    values_local = value_lin.reshape(slot_count, block_len, kv_heads, HEAD_DIM).astype(jnp.bfloat16)
    key_value = jnp.stack([keys_local, values_local])
    mixed, log_total = cycle_attend(
        queries, key_value, query_index, query_segment, cycle_place, cycle_size
    )
    context = mixed.reshape(slot_count, block_len, width).astype(jnp.bfloat16)
    rank_output, extra_output = adapter_forward(context, picked[3][0], picked[3][1])
    middle = hidden + project(context, output_full) + extra_output
    normed2 = rms_forward(middle, gain_two).astype(jnp.bfloat16)
    rank_gate, extra_gate = adapter_forward(normed2, picked[4][0], picked[4][1])
    rank_up, extra_up = adapter_forward(normed2, picked[5][0], picked[5][1])
    gate_lin = project(normed2, gate_full) + extra_gate
    up_lin = project(normed2, up_full) + extra_up
    sigmoid_gate = jax.nn.sigmoid(gate_lin)
    act_rows = (gate_lin * sigmoid_gate * up_lin).astype(jnp.bfloat16)
    rank_down, extra_down = adapter_forward(act_rows, picked[6][0], picked[6][1])
    result = middle + project(act_rows, down_full) + extra_down
    layer_out = (result * live_rows).astype(jnp.bfloat16)
    again_rows = (
        lax.all_gather(shards[0], "wsh", axis=0, tiled=True),
        lax.all_gather(shards[1], "wsh", axis=0, tiled=True),
        lax.all_gather(shards[2], "wsh", axis=0, tiled=True),
        lax.all_gather(shards[3], "wsh", axis=0, tiled=True),
        lax.all_gather(shards[4], "wsh", axis=0, tiled=True),
        lax.all_gather(shards[5], "wsh", axis=0, tiled=True),
        lax.all_gather(shards[6], "wsh", axis=0, tiled=True),
    )
    back_weights = (
        lax.all_gather(again_rows[0], "ctx", axis=1, tiled=True),
        lax.all_gather(again_rows[1], "ctx", axis=1, tiled=True),
        lax.all_gather(again_rows[2], "ctx", axis=1, tiled=True),
        lax.all_gather(again_rows[3], "ctx", axis=1, tiled=True),
        lax.all_gather(again_rows[4], "ctx", axis=1, tiled=True),
        lax.all_gather(again_rows[5], "ctx", axis=1, tiled=True),
        lax.all_gather(again_rows[6], "ctx", axis=1, tiled=True),
    )
    query_back, key_back, value_back, output_back, gate_back, up_back, down_back = back_weights
    grad_out = cotangent * live_rows.astype(jnp.bfloat16)
    to_act, g_down_in, g_down_out = adapter_backward(
        grad_out, act_rows, rank_down, picked[6][0], picked[6][1]
    )
    d_act = project_back(grad_out, down_back) + to_act
    d_gate = (d_act * up_lin * sigmoid_gate * (1.0 + gate_lin * (1.0 - sigmoid_gate))).astype(
        jnp.bfloat16
    )
    d_up = (d_act * gate_lin * sigmoid_gate).astype(jnp.bfloat16)
    to_gate, g_gate_in, g_gate_out = adapter_backward(
        d_gate, normed2, rank_gate, picked[4][0], picked[4][1]
    )
    to_up, g_up_in, g_up_out = adapter_backward(d_up, normed2, rank_up, picked[5][0], picked[5][1])
    d_normed2 = project_back(d_gate, gate_back) + to_gate + project_back(d_up, up_back) + to_up
    d_middle = grad_out.astype(jnp.float32) + rms_backward(middle, gain_two, d_normed2)
    d_branch = d_middle.astype(jnp.bfloat16)
    to_context, g_output_in, g_output_out = adapter_backward(
        d_branch, context, rank_output, picked[3][0], picked[3][1]
    )
    d_context = (project_back(d_branch, output_back) + to_context).astype(jnp.bfloat16)
    d_mixed = d_context.reshape(slot_count, block_len, kv_heads, group_size, HEAD_DIM)
    delta_rows = jnp.transpose(jnp.sum(d_mixed.astype(jnp.float32) * mixed, axis=-1), (0, 2, 3, 1))
    grad_query, grad_pair = cycle_attend_back(
        queries,
        key_value,
        d_mixed,
        log_total,
        delta_rows,
        query_index,
        query_segment,
        cycle_place,
        cycle_size,
    )
    d_query = (
        rotate(grad_query, position, -1.0)
        .reshape(slot_count, block_len, width)
        .astype(jnp.bfloat16)
    )
    d_key = (
        rotate(grad_pair[0], position, -1.0).reshape(slot_count, block_len, -1).astype(jnp.bfloat16)
    )
    d_value = grad_pair[1].reshape(slot_count, block_len, -1).astype(jnp.bfloat16)
    to_query, g_query_in, g_query_out = adapter_backward(
        d_query, normed, rank_query, picked[0][0], picked[0][1]
    )
    to_key, g_key_in, g_key_out = adapter_backward(
        d_key, normed, rank_key, picked[1][0], picked[1][1]
    )
    to_value, g_value_in, g_value_out = adapter_backward(
        d_value, normed, rank_value, picked[2][0], picked[2][1]
    )
    d_normed = (
        project_back(d_query, query_back)
        + project_back(d_key, key_back)
        + project_back(d_value, value_back)
        + to_query
        + to_key
        + to_value
    )
    d_hidden = d_middle + rms_backward(hidden, gain_one, d_normed)
    input_grad = (d_hidden * live_rows).astype(jnp.bfloat16)

    def by_adapter(per_slot):
        return jnp.einsum("sa,sri->ari", choose, per_slot)

    summed = lax.psum(
        (
            by_adapter(g_query_in),
            by_adapter(g_query_out),
            by_adapter(g_key_in),
            by_adapter(g_key_out),
            by_adapter(g_value_in),
            by_adapter(g_value_out),
            by_adapter(g_output_in),
            by_adapter(g_output_out),
            by_adapter(g_gate_in),
            by_adapter(g_gate_out),
            by_adapter(g_up_in),
            by_adapter(g_up_out),
            by_adapter(g_down_in),
            by_adapter(g_down_out),
        ),
        ("ctx", "wsh"),
    )
    return (
        layer_out,
        input_grad,
        summed[0],
        summed[1],
        summed[2],
        summed[3],
        summed[4],
        summed[5],
        summed[6],
        summed[7],
        summed[8],
        summed[9],
        summed[10],
        summed[11],
        summed[12],
        summed[13],
    )


def solution(mesh):
    return jax.shard_map(
        local,
        mesh=mesh,
        in_specs=(
            P("wsh", "ctx", None),
            P("wsh", "ctx", None),
            P(),
            P(),
            P(),
            P(),
            P("wsh", "ctx"),
            P("wsh", "ctx"),
            P("wsh", "ctx"),
            P("wsh", "ctx"),
            P("wsh", "ctx"),
            P("wsh", "ctx"),
            P("wsh", "ctx"),
            P(),
            P(),
            P(),
            P(),
            P(),
            P(),
            P(),
            P(),
            P(),
            P(),
            P(),
            P(),
            P(),
            P(),
            P(),
            P(),
            P(),
        ),
        out_specs=(
            P("wsh", "ctx", None),
            P("wsh", "ctx", None),
            P(),
            P(),
            P(),
            P(),
            P(),
            P(),
            P(),
            P(),
            P(),
            P(),
            P(),
            P(),
            P(),
            P(),
        ),
        check_vma=False,
    )
```

profile of v0, /device:TPU:0, one launch (start us, length us, event | category | flops | bytes accessed | tf_op | source)
XLA Modules:
  0.0 2599.1 jit_solution(2822389648553072899)
XLA Ops:
  9.5 18.0 all_gather.60
  27.6 13.4 all_gather.62
  41.0 20.0 all-gather.18.cloned.1.call-done
  61.1 49.1 %all-gather.24.cloned.1.call-done = bf16[4,2240,192]{1,2,0:T(8,128)(2,1)} async-done(((bf16[1,2240,192]{1,2,0:T(8,128)(2,1)}), bf16[4,2240,192]{1,2,0:T(8,128)(2,1)}) %all-gather.24.cloned.1.call-update) | async-done | bytes 3440656 | tf_op jit(solution)/shard_map/all_gather | solution.py:268
  141.7 16.2 all_gather.57
  183.4 20.3 all_gather.59
  270.9 329.2 %while.40 = (s32[]{:T(128)}, bf16[2,4,256,2,128]{4,2,3,1,0:T(8,128)(2,1)S(1)}, f32[4,2,6,256]{3,2,1,0:T(8,128)S(1)}, f32[4,2,6,256]{3,2,1,0:T(8,128)S(1)}, f32[4...) while((s32[]{:T(128)}, ...), condition=%wide.region_5.8_spmd.clone.clone.clone, body=%wide.region_2.7_spmd.clone.clone.clone.sunk | while | flops 1656647168 | bytes 112239984 | solution.py:150
  282.9 11.3 bitcast_add_fusion.4
  304.0 10.6 bitcast_add_fusion.4
  314.7 18.1 collective-permute-done
  342.7 10.6 bitcast_add_fusion.4
  353.3 18.1 collective-permute-done
  381.3 10.6 bitcast_add_fusion.4
  391.9 18.2 collective-permute-done
  420.0 10.8 bitcast_add_fusion.4
  430.8 30.3 %collective-permute-done = bf16[2,4,256,2,128]{4,2,3,1,0:T(8,128)(2,1)S(1)} collective-permute-done((bf16[2,4,256,2,128]{4,2,3,1,0:T(8,128)(2,1)S(1)}, bf16[2,4,256,2,128]{4,2,3,1,0:T(8,128)(2,1)S(1)}, u32[]{:S(2)}, u32[]{:S(2)}) %collective-permute-start) | collective-permute-done | bytes 1048608 | tf_op jit(solution)/shard_map/while/body/eval_jaxpr/ppermute | solution.py:20
  471.1 10.8 bitcast_add_fusion.4
  481.8 40.2 %collective-permute-done = bf16[2,4,256,2,128]{4,2,3,1,0:T(8,128)(2,1)S(1)} collective-permute-done((bf16[2,4,256,2,128]{4,2,3,1,0:T(8,128)(2,1)S(1)}, bf16[2,4,256,2,128]{4,2,3,1,0:T(8,128)(2,1)S(1)}, u32[]{:S(2)}, u32[]{:S(2)}) %collective-permute-start) | collective-permute-done | bytes 1048608 | tf_op jit(solution)/shard_map/while/body/eval_jaxpr/ppermute | solution.py:20
  534.1 10.7 bitcast_add_fusion.4
  544.9 31.1 %collective-permute-done = bf16[2,4,256,2,128]{4,2,3,1,0:T(8,128)(2,1)S(1)} collective-permute-done((bf16[2,4,256,2,128]{4,2,3,1,0:T(8,128)(2,1)S(1)}, bf16[2,4,256,2,128]{4,2,3,1,0:T(8,128)(2,1)S(1)}, u32[]{:S(2)}, u32[]{:S(2)}) %collective-permute-start) | collective-permute-done | bytes 1048608 | tf_op jit(solution)/shard_map/while/body/eval_jaxpr/ppermute | solution.py:20
  587.8 12.3 bitcast_add_fusion.4
  628.3 36.3 %fusion.61 = f32[4,256,8960]{2,1,0:T(8,128)} fusion(bf16[4,256,1536]{2,1,0:T(8,128)(2,1)} %copy-done.10, bf16[1536,8960]{0,1:T(8,128)(2,1)} %all-gather.20.cloned.1.call-done), kind=kOutput, calls=%fused_computation.113 | convolution fusion | flops 28185722880 | bytes 67371008 | tf_op jit(solution)/shard_map/sbi,io->sbo/dot_general | solution.py:66
  664.6 27.1 %multiply_add_fusion = f32[4,256,8960]{2,1,0:T(8,128)} fusion(f32[4,256,8960]{2,1,0:T(8,128)} %fusion.61, bf16[4,256,16]{1,2,0:T(8,128)(2,1)S(1)} %convolution_convert_fusion.1, bf16[4,16,8960]{2,1,0:T(8,128)(2,1)S(1)} %copy-done.31, pred[4]{0:T(512)(128)(4,1)S(1)} %compare_and_fusion), kind=kOutput, calls=%fused_computation.104 | convolution fusion | flops 312524800 | bytes 74579968 | tf_op jit(solution)/shard_map/ivu,iup->ivp/dot_general | solution.py:80
  691.6 124.3 %all-gather.22.cloned.1.call-done = bf16[8960,1536]{0,1:T(8,128)(2,1)} async-done(((bf16[8960,192]{0,1:T(8,128)(2,1)}), bf16[8960,1536]{0,1:T(8,128)(2,1)}) %all-gather.22.cloned.1.call-update) | async-done | bytes 27525136 | tf_op jit(solution)/shard_map/all_gather | solution.py:277
  816.0 36.3 %fusion.55 = f32[4,256,8960]{2,1,0:T(8,128)} fusion(bf16[8960,1536]{0,1:T(8,128)(2,1)} %all-gather.22.cloned.1.call-done, bf16[4,256,1536]{2,1,0:T(8,128)(2,1)} %param.41, bf16[4]{0:T(256)(128)(2,1)S(1)} %copy-done.127), kind=kOutput, calls=%fused_computation.107 | convolution fusion | flops 28187295744 | bytes 67371016 | tf_op jit(solution)/shard_map/sbo,io->sbi/dot_general | solution.py:70
  852.3 27.1 %convolution_add_fusion = f32[4,256,8960]{2,1,0:T(8,128)} fusion(f32[4,256,8960]{2,1,0:T(8,128)} %fusion.55, bf16[4,256,16]{1,2,0:T(8,128)(2,1)S(1)} %copy-done.61, bf16[4,16,8960]{2,1,0:T(8,128)(2,1)S(1)} %copy-done.29, pred[4]{0:T(512)(128)(4,1)S(1)} %compare_and_fusion), kind=kOutput, calls=%fused_computation.119 | convolution fusion | flops 303349760 | bytes 74579968 | tf_op jit(solution)/shard_map/pec,pcn->pen/dot_general | solution.py:101
  879.4 185.0 %all-gather.16.cloned.1.call-done = bf16[1536,8960]{0,1:T(8,128)(2,1)} async-done(((bf16[1536,1120]{0,1:T(8,128)(2,1)}), bf16[1536,8960]{0,1:T(8,128)(2,1)}) %all-gather.16.cloned.1.call-update) | async-done | bytes 27525136 | tf_op jit(solution)/shard_map/all_gather | solution.py:275
  1064.4 35.9 %fusion.65 = f32[4,256,8960]{2,1,0:T(8,128)} fusion(bf16[4,256,1536]{2,1,0:T(8,128)(2,1)} %copy-done.10, bf16[1536,8960]{0,1:T(8,128)(2,1)} %all-gather.16.cloned.1.call-done), kind=kOutput, calls=%fused_computation.117 | convolution fusion | flops 28185722880 | bytes 67371008 | tf_op jit(solution)/shard_map/sbi,io->sbo/dot_general | solution.py:66
  1100.3 56.3 %multiply_convert_fusion.1 = (bf16[4,256,8960]{2,1,0:T(8,128)(2,1)}, bf16[4,256,8960]{2,1,0:T(8,128)(2,1)}, bf16[4,256,8960]{2,1,0:T(8,128)(2,1)}) fusion(f32[4,256,8960]{2,1,0:T(8,128)} %convolution_add_fusion, f32[4,256,8960]{2,1,0:T(8,128)} %multiply_add_fusion, f32[4,256,8960]{2,1,0:T(8,128)} %fusion.65, bf16[4,256,16]{1,2,0:T(8,128)(2,1)S(1)} %copy-done.63, ...), kind=kOutput, calls=%fused_computation.102 | convolution fusion | flops 459325440 | bytes 166330368 | tf_op jit(solution)/shard_map/ivu,iup->ivp/dot_general | solution.py:80
  1156.6 9.8 convolution_multiply_fusion
  1175.1 9.7 convolution_multiply_fusion.1
  1197.2 35.9 %fusion.59 = f32[4,256,1536]{2,1,0:T(8,128)} fusion(bf16[4,256,8960]{2,1,0:T(8,128)(2,1)} %get-tuple-element.696, bf16[1536,8960]{0,1:T(8,128)(2,1)} %all-gather.20.cloned.1.call-done), kind=kOutput, calls=%fused_computation.111 | convolution fusion | flops 28185722880 | bytes 52166656 | tf_op jit(solution)/shard_map/sbo,io->sbi/dot_general | solution.py:70
  1233.1 36.0 %fusion.63 = f32[4,256,1536]{2,1,0:T(8,128)} fusion(bf16[4,256,8960]{2,1,0:T(8,128)(2,1)} %get-tuple-element.694, bf16[1536,8960]{0,1:T(8,128)(2,1)} %all-gather.16.cloned.1.call-done), kind=kOutput, calls=%fused_computation.115 | convolution fusion | flops 28185722880 | bytes 52166656 | tf_op jit(solution)/shard_map/sbo,io->sbi/dot_general | solution.py:70
  1311.7 392.7 %while.41 = (s32[]{:T(128)}, bf16[2,4,256,2,128]{4,2,3,1,0:T(8,128)(2,1)S(1)}, f32[2,4,256,2,128]{4,2,3,1,0:T(8,128)}, f32[4,256,2,6,128]{4,1,3,2,0:T(8,128)}, s...) while((s32[]{:T(128)}, ...), condition=%wide.region_11.15_spmd.clone.clone.clone, body=%wide.region_10.14_spmd.clone.clone.clone.sunk | while | flops 4072230400 | bytes 213771824 | solution.py:209
  1351.2 9.7 collective-permute-done.1
  1400.2 9.7 collective-permute-done.1
  1431.5 9.6 bitcast_add_fusion.5
  1449.2 9.7 collective-permute-done.1
  1480.5 9.6 bitcast_add_fusion.5
  1498.2 9.7 collective-permute-done.1
  1547.2 9.7 collective-permute-done.1
  1596.2 9.7 collective-permute-done.1
  1627.5 9.6 bitcast_add_fusion.5
  1645.3 9.7 collective-permute-done.1
  1694.3 9.7 collective-permute-done.1
  1791.1 20.7 fusion.76
  1811.8 34.0 %fusion.57 = f32[4,256,1536]{2,1,0:T(8,128)S(1)} fusion(bf16[4,256,8960]{2,1,0:T(8,128)(2,1)} %get-tuple-element.695, bf16[8960,1536]{0,1:T(8,128)(2,1)} %all-gather.22.cloned.1.call-done), kind=kOutput, calls=%fused_computation.109 | convolution fusion | flops 28185722880 | bytes 52166656 | tf_op jit(solution)/shard_map/sbi,io->sbo/dot_general | solution.py:66
  1856.2 709.1 %all-reduce.3.cloned.1.call-done = (f32[8,16,1536]{2,0,1:T(8,128)}, f32[8,16,1536]{2,0,1:T(8,128)}, f32[8,16,1536]{2,0,1:T(8,128)}, f32[8,16,256]{2,0,1:T(8,128)...) async-done(((f32[8,16,1536]{2,0,1:T(8,128)}, ...) | async-done | bytes 21102608 | tf_op jit(solution)/shard_map/psum | solution.py:413
  (792 shorter events, 699.6 us)
Async XLA Ops:
  7.2 213.6 %copy-start = (bf16[8,16,8960]{2,1,0:T(8,128)(2,1)S(1)}, bf16[8,16,8960]{2,1,0:T(8,128)(2,1)}, u32[]{:S(2)}) copy-start(bf16[8,16,8960]{2,1,0:T(8,128)(2,1)} %param.67) | copy-start | bytes 6881284
  7.2 53.9 %all-gather.18.cloned.1.call-start = ((), (), s32[]{:S(2)}) async-start(), calls=%async_computation.4 | async-start | bytes 4300800 | tf_op jit(solution)/shard_map/all_gather | solution.py:267
  7.9 102.3 %all-gather.24.cloned.1.call-start = ((), (), s32[]{:S(2)}) async-start(), calls=%async_computation.7 | async-start | bytes 4423680 | tf_op jit(solution)/shard_map/all_gather | solution.py:268
  8.7 231.7 %all-gather.14.cloned.1.call-start = ((), (), s32[]{:S(2)}) async-start(), calls=%async_computation.2 | async-start | bytes 4300800 | tf_op jit(solution)/shard_map/all_gather | solution.py:266
  9.4 231.0 %all-gather.10.cloned.1.call-start = ((), (), s32[]{:S(2)}) async-start(), calls=%async_computation | async-start | bytes 5308416 | tf_op jit(solution)/shard_map/all_gather | solution.py:271
  27.5 585.1 %all-gather.12.cloned.1.call-start = ((), (), s32[]{:S(2)}) async-start(), calls=%async_computation.1 | async-start | bytes 5308416 | tf_op jit(solution)/shard_map/all_gather | solution.py:274
  41.0 587.3 %all-gather.20.cloned.1.call-start = ((), (), s32[]{:S(2)}) async-start(), calls=%async_computation.5 | async-start | bytes 30965760 | tf_op jit(solution)/shard_map/all_gather | solution.py:276
  61.1 754.9 %all-gather.22.cloned.1.call-start = ((), (), s32[]{:S(2)}) async-start(), calls=%async_computation.6 | async-start | bytes 30965760 | tf_op jit(solution)/shard_map/all_gather | solution.py:277
  123.6 940.8 %all-gather.16.cloned.1.call-start = ((), (), s32[]{:S(2)}) async-start(), calls=%async_computation.3 | async-start | bytes 30965760 | tf_op jit(solution)/shard_map/all_gather | solution.py:275
  123.7 116.8 %copy-start.94 = (f32[1536]{0:T(1024)}, f32[1536]{0:T(1024)S(1)}, u32[]{:S(2)}) copy-start(f32[1536]{0:T(1024)S(1)} %convert_element_type.202) | copy-start | bytes 18436
  138.3 1148.5 %copy-start.85 = (pred[4]{0:T(512)(128)(4,1)}, pred[4]{0:T(512)(128)(4,1)S(1)}, u32[]{:S(2)}) copy-start(pred[4]{0:T(512)(128)(4,1)S(1)} %compare_and_fusion) | copy-start | bytes 16
  141.6 98.8 %copy-start.121 = (f32[4,256]{1,0:T(4,128)}, f32[4,256]{1,0:T(4,128)S(1)}, u32[]{:S(2)}) copy-start(f32[4,256]{1,0:T(4,128)S(1)} %get-tuple-element.710) | copy-start | bytes 12292
  218.5 405.8 %copy-start.112 = (f32[1536]{0:T(1024)}, f32[1536]{0:T(1024)S(1)}, u32[]{:S(2)}) copy-start(f32[1536]{0:T(1024)S(1)} %convert_element_type.218) | copy-start | bytes 18436
  240.4 2325.0 %all-reduce.3.cloned.1.call-start = ((), (), s32[]{:S(2)}) async-start(), calls=%async_computation.8 | async-start | bytes 42205184 | tf_op jit(solution)/shard_map/psum | solution.py:413
  271.0 23.2 collective-permute-start
  294.3 38.6 %collective-permute-start = (bf16[2,4,256,2,128]{4,2,3,1,0:T(8,128)(2,1)S(1)}, bf16[2,4,256,2,128]{4,2,3,1,0:T(8,128)(2,1)S(1)}, u32[]{:S(2)}, u32[]{:S(2)}) collective-permute-start(bf16[2,4,256,2,128]{4,2,3,1,0:T(8,128)(2,1)S(1)} %copy.280), channel_id=1, source_target_pairs={{0,4},{4,8},{8,12},{12,16},{16,20},{20,24},{24,28},{28,0},{1,5},{5... | collective-permute-start | bytes 3145736 | tf_op jit(solution)/shard_map/while/body/eval_jaxpr/ppermute | solution.py:20
  332.9 38.5 %collective-permute-start = (bf16[2,4,256,2,128]{4,2,3,1,0:T(8,128)(2,1)S(1)}, bf16[2,4,256,2,128]{4,2,3,1,0:T(8,128)(2,1)S(1)}, u32[]{:S(2)}, u32[]{:S(2)}) collective-permute-start(bf16[2,4,256,2,128]{4,2,3,1,0:T(8,128)(2,1)S(1)} %copy.280), channel_id=1, source_target_pairs={{0,4},{4,8},{8,12},{12,16},{16,20},{20,24},{24,28},{28,0},{1,5},{5... | collective-permute-start | bytes 3145736 | tf_op jit(solution)/shard_map/while/body/eval_jaxpr/ppermute | solution.py:20
  371.5 38.6 %collective-permute-start = (bf16[2,4,256,2,128]{4,2,3,1,0:T(8,128)(2,1)S(1)}, bf16[2,4,256,2,128]{4,2,3,1,0:T(8,128)(2,1)S(1)}, u32[]{:S(2)}, u32[]{:S(2)}) collective-permute-start(bf16[2,4,256,2,128]{4,2,3,1,0:T(8,128)(2,1)S(1)} %copy.280), channel_id=1, source_target_pairs={{0,4},{4,8},{8,12},{12,16},{16,20},{20,24},{24,28},{28,0},{1,5},{5... | collective-permute-start | bytes 3145736 | tf_op jit(solution)/shard_map/while/body/eval_jaxpr/ppermute | solution.py:20
  410.2 51.0 %collective-permute-start = (bf16[2,4,256,2,128]{4,2,3,1,0:T(8,128)(2,1)S(1)}, bf16[2,4,256,2,128]{4,2,3,1,0:T(8,128)(2,1)S(1)}, u32[]{:S(2)}, u32[]{:S(2)}) collective-permute-start(bf16[2,4,256,2,128]{4,2,3,1,0:T(8,128)(2,1)S(1)} %copy.280), channel_id=1, source_target_pairs={{0,4},{4,8},{8,12},{12,16},{16,20},{20,24},{24,28},{28,0},{1,5},{5... | collective-permute-start | bytes 3145736 | tf_op jit(solution)/shard_map/while/body/eval_jaxpr/ppermute | solution.py:20
  461.3 60.8 %collective-permute-start = (bf16[2,4,256,2,128]{4,2,3,1,0:T(8,128)(2,1)S(1)}, bf16[2,4,256,2,128]{4,2,3,1,0:T(8,128)(2,1)S(1)}, u32[]{:S(2)}, u32[]{:S(2)}) collective-permute-start(bf16[2,4,256,2,128]{4,2,3,1,0:T(8,128)(2,1)S(1)} %copy.280), channel_id=1, source_target_pairs={{0,4},{4,8},{8,12},{12,16},{16,20},{20,24},{24,28},{28,0},{1,5},{5... | collective-permute-start | bytes 3145736 | tf_op jit(solution)/shard_map/while/body/eval_jaxpr/ppermute | solution.py:20
  522.2 53.8 %collective-permute-start = (bf16[2,4,256,2,128]{4,2,3,1,0:T(8,128)(2,1)S(1)}, bf16[2,4,256,2,128]{4,2,3,1,0:T(8,128)(2,1)S(1)}, u32[]{:S(2)}, u32[]{:S(2)}) collective-permute-start(bf16[2,4,256,2,128]{4,2,3,1,0:T(8,128)(2,1)S(1)} %copy.280), channel_id=1, source_target_pairs={{0,4},{4,8},{8,12},{12,16},{16,20},{20,24},{24,28},{28,0},{1,5},{5... | collective-permute-start | bytes 3145736 | tf_op jit(solution)/shard_map/while/body/eval_jaxpr/ppermute | solution.py:20
  576.1 24.0 collective-permute-start
  664.5 151.4 %copy-start.127 = (bf16[4]{0:T(256)(128)(2,1)S(1)}, bf16[4]{0:T(256)(128)(2,1)}, u32[]{:S(2)}) copy-start(bf16[4]{0:T(256)(128)(2,1)} %copy-done.126) | copy-start | bytes 28
  691.6 160.6 %copy-start.29 = (bf16[4,16,8960]{2,1,0:T(8,128)(2,1)S(1)}, bf16[4,16,8960]{2,1,0:T(8,128)(2,1)}, u32[]{:S(2)}) copy-start(bf16[4,16,8960]{2,1,0:T(8,128)(2,1)} %gather_fusion.12) | copy-start | bytes 3440644
  691.6 160.6 %copy-start.61 = (bf16[4,256,16]{1,2,0:T(8,128)(2,1)S(1)}, bf16[4,256,16]{1,2,0:T(8,128)(2,1)}, u32[]{:S(2)}) copy-start(bf16[4,256,16]{1,2,0:T(8,128)(2,1)} %fusion.115) | copy-start | bytes 98308
  879.4 220.9 %copy-start.33 = (bf16[4,16,8960]{2,1,0:T(8,128)(2,1)S(1)}, bf16[4,16,8960]{2,1,0:T(8,128)(2,1)}, u32[]{:S(2)}) copy-start(bf16[4,16,8960]{2,1,0:T(8,128)(2,1)} %gather_fusion.9) | copy-start | bytes 3440644
  879.4 220.9 %copy-start.63 = (bf16[4,256,16]{1,2,0:T(8,128)(2,1)S(1)}, bf16[4,256,16]{1,2,0:T(8,128)(2,1)}, u32[]{:S(2)}) copy-start(bf16[4,256,16]{1,2,0:T(8,128)(2,1)} %convolution_convert_fusion.2) | copy-start | bytes 98308
  1100.3 56.3 %copy-start.57 = (bf16[4,256,16]{1,2,0:T(8,128)(2,1)S(1)}, bf16[4,256,16]{1,2,0:T(8,128)(2,1)}, u32[]{:S(2)}) copy-start(bf16[4,256,16]{1,2,0:T(8,128)(2,1)} %copy-done.56) | copy-start | bytes 98308
  1197.2 71.9 %slice-start = ((s8[6291456]{0:T(1024)(128)(4,1)}), s8[4194304]{0:T(1024)(128)(4,1)S(1)}, s32[]{:S(2)}) async-start(s8[6291456]{0:T(1024)(128)(4,1)} %bitcast.297), calls=%async_computation.9 | async-start | bytes 8388608
  1197.2 84.5 %slice-start.8 = ((s8[4718592]{0:T(1024)(128)(4,1)}), s8[4194304]{0:T(1024)(128)(4,1)S(1)}, s32[]{:S(2)}) async-start(s8[4718592]{0:T(1024)(128)(4,1)} %bitcast.326), calls=%async_computation.17 | async-start | bytes 8388608
  1233.1 48.7 %slice-start.9 = ((s8[4718592]{0:T(1024)(128)(4,1)}), s8[524288]{0:T(1024)(128)(4,1)S(1)}, s32[]{:S(2)}) async-start(s8[4718592]{0:T(1024)(128)(4,1)} %bitcast.326), calls=%async_computation.18 | async-start | bytes 1048576
  1333.4 16.2 collective-permute-start.2
  1333.7 27.2 %collective-permute-start.1 = (bf16[2,4,256,2,128]{4,2,3,1,0:T(8,128)(2,1)S(1)}, bf16[2,4,256,2,128]{4,2,3,1,0:T(8,128)(2,1)S(1)}, u32[]{:S(2)}, u32[]{:S(2)}) collective-permute-start(bf16[2,4,256,2,128]{4,2,3,1,0:T(8,128)(2,1)S(1)} %copy.294), channel_id=1, source_target_pairs={{0,4},{4,8},{8,12},{12,16},{16,20},{20,24},{24,28},{28,0},{1,5},{5... | collective-permute-start | bytes 3145736 | tf_op jit(solution)/shard_map/while/body/eval_jaxpr/ppermute | solution.py:20
  1382.4 16.2 collective-permute-start.2
  1382.4 27.5 %collective-permute-start.1 = (bf16[2,4,256,2,128]{4,2,3,1,0:T(8,128)(2,1)S(1)}, bf16[2,4,256,2,128]{4,2,3,1,0:T(8,128)(2,1)S(1)}, u32[]{:S(2)}, u32[]{:S(2)}) collective-permute-start(bf16[2,4,256,2,128]{4,2,3,1,0:T(8,128)(2,1)S(1)} %copy.294), channel_id=1, source_target_pairs={{0,4},{4,8},{8,12},{12,16},{16,20},{20,24},{24,28},{28,0},{1,5},{5... | collective-permute-start | bytes 3145736 | tf_op jit(solution)/shard_map/while/body/eval_jaxpr/ppermute | solution.py:20
  1431.4 16.2 collective-permute-start.2
  1431.4 27.5 %collective-permute-start.1 = (bf16[2,4,256,2,128]{4,2,3,1,0:T(8,128)(2,1)S(1)}, bf16[2,4,256,2,128]{4,2,3,1,0:T(8,128)(2,1)S(1)}, u32[]{:S(2)}, u32[]{:S(2)}) collective-permute-start(bf16[2,4,256,2,128]{4,2,3,1,0:T(8,128)(2,1)S(1)} %copy.294), channel_id=1, source_target_pairs={{0,4},{4,8},{8,12},{12,16},{16,20},{20,24},{24,28},{28,0},{1,5},{5... | collective-permute-start | bytes 3145736 | tf_op jit(solution)/shard_map/while/body/eval_jaxpr/ppermute | solution.py:20
  1480.5 16.2 collective-permute-start.2
  1480.5 27.5 %collective-permute-start.1 = (bf16[2,4,256,2,128]{4,2,3,1,0:T(8,128)(2,1)S(1)}, bf16[2,4,256,2,128]{4,2,3,1,0:T(8,128)(2,1)S(1)}, u32[]{:S(2)}, u32[]{:S(2)}) collective-permute-start(bf16[2,4,256,2,128]{4,2,3,1,0:T(8,128)(2,1)S(1)} %copy.294), channel_id=1, source_target_pairs={{0,4},{4,8},{8,12},{12,16},{16,20},{20,24},{24,28},{28,0},{1,5},{5... | collective-permute-start | bytes 3145736 | tf_op jit(solution)/shard_map/while/body/eval_jaxpr/ppermute | solution.py:20
  1529.5 16.2 collective-permute-start.2
  1529.5 27.5 %collective-permute-start.1 = (bf16[2,4,256,2,128]{4,2,3,1,0:T(8,128)(2,1)S(1)}, bf16[2,4,256,2,128]{4,2,3,1,0:T(8,128)(2,1)S(1)}, u32[]{:S(2)}, u32[]{:S(2)}) collective-permute-start(bf16[2,4,256,2,128]{4,2,3,1,0:T(8,128)(2,1)S(1)} %copy.294), channel_id=1, source_target_pairs={{0,4},{4,8},{8,12},{12,16},{16,20},{20,24},{24,28},{28,0},{1,5},{5... | collective-permute-start | bytes 3145736 | tf_op jit(solution)/shard_map/while/body/eval_jaxpr/ppermute | solution.py:20
  1578.5 16.2 collective-permute-start.2
  1578.5 27.5 %collective-permute-start.1 = (bf16[2,4,256,2,128]{4,2,3,1,0:T(8,128)(2,1)S(1)}, bf16[2,4,256,2,128]{4,2,3,1,0:T(8,128)(2,1)S(1)}, u32[]{:S(2)}, u32[]{:S(2)}) collective-permute-start(bf16[2,4,256,2,128]{4,2,3,1,0:T(8,128)(2,1)S(1)} %copy.294), channel_id=1, source_target_pairs={{0,4},{4,8},{8,12},{12,16},{16,20},{20,24},{24,28},{28,0},{1,5},{5... | collective-permute-start | bytes 3145736 | tf_op jit(solution)/shard_map/while/body/eval_jaxpr/ppermute | solution.py:20
  1627.5 16.2 collective-permute-start.2
  1627.5 27.5 %collective-permute-start.1 = (bf16[2,4,256,2,128]{4,2,3,1,0:T(8,128)(2,1)S(1)}, bf16[2,4,256,2,128]{4,2,3,1,0:T(8,128)(2,1)S(1)}, u32[]{:S(2)}, u32[]{:S(2)}) collective-permute-start(bf16[2,4,256,2,128]{4,2,3,1,0:T(8,128)(2,1)S(1)} %copy.294), channel_id=1, source_target_pairs={{0,4},{4,8},{8,12},{12,16},{16,20},{20,24},{24,28},{28,0},{1,5},{5... | collective-permute-start | bytes 3145736 | tf_op jit(solution)/shard_map/while/body/eval_jaxpr/ppermute | solution.py:20
  1676.5 16.2 collective-permute-start.2
  1676.5 27.5 %collective-permute-start.1 = (bf16[2,4,256,2,128]{4,2,3,1,0:T(8,128)(2,1)S(1)}, bf16[2,4,256,2,128]{4,2,3,1,0:T(8,128)(2,1)S(1)}, u32[]{:S(2)}, u32[]{:S(2)}) collective-permute-start(bf16[2,4,256,2,128]{4,2,3,1,0:T(8,128)(2,1)S(1)} %copy.294), channel_id=1, source_target_pairs={{0,4},{4,8},{8,12},{12,16},{16,20},{20,24},{24,28},{28,0},{1,5},{5... | collective-permute-start | bytes 3145736 | tf_op jit(solution)/shard_map/while/body/eval_jaxpr/ppermute | solution.py:20
  1791.1 54.7 %slice-start.2 = ((s8[6291456]{0:T(1024)(128)(4,1)}), s8[2097152]{0:T(1024)(128)(4,1)S(1)}, s32[]{:S(2)}) async-start(s8[6291456]{0:T(1024)(128)(4,1)} %bitcast.299), calls=%async_computation.11 | async-start | bytes 4194304
  (171 other events, 1629.2 us)
Sparse Core Ops, SparseCore 0:
  9.8 51.1 all-gather.17
  62.9 47.2 all-gather.23
  112.0 46.2 all-gather.13
  159.8 57.8 all-gather.9
  219.2 50.5 all-gather.11
  271.3 302.0 all-gather.19
  575.7 240.2 all-gather.21
  817.6 246.7 all-gather.15
  1782.5 782.7 all-reduce.2
where the time goes:
time: 2610 us; the launch traced here: 2600 us
  waiting for transfers between devices  1380 us (53%)
  matrix products  845 us (32%)
  local copies, waits for them, and re-layouts  167 us (6%)
  other arithmetic  92.3 us (4%)
  blocking collectives  84.5 us (3%)
    psum x1, waiting for transfers between devices, local(): lax.psum((by_adapter(g_query_in), by_adapter(g_query_out), by_adapter(g_k...  709 us
    ppermute x24, waiting for transfers between devices, passed_along(): lax.ppermute(array, axis, [(i, (i + by) % peers) for i in range(peers)])  288 us
    all_gather x1, waiting for transfers between devices, local(): lax.all_gather(full_rows[4], 'ctx', axis=1, tiled=True)  185 us
    dot_general x7, matrix products, project_back(): jnp.einsum('sbo,io->sbi', incoming_gradient, weight, preferred_element_ty...  141 us
    dot_general x7, matrix products, project(): jnp.einsum('sbi,io->sbo', input_rows, weight, preferred_element_type=jnp....  125 us
    all_gather x1, waiting for transfers between devices, local(): lax.all_gather(full_rows[6], 'ctx', axis=1, tiled=True)  124 us
    dot_general x7, matrix products, adapter_forward(): jnp.einsum('ivu,iup->ivp', projected_rank_rows, selected_up_weight, prefe...  94 us
    dot_general x8, matrix products, cycle_step(): jnp.einsum('skgbt,stkd->sbkgd', weights.astype(jnp.bfloat16), moving[1],...  87.7 us
  transfers between devices with their start and end apart: 33, of which 27 were waited for; matrix products, arithmetic and copies ran while one was open for 22% of the time, Pallas kernels for 0%

commit v1 on v0

v1 whole, which is shorter than its diff:
```python
import functools
import math

import jax
import jax.numpy as jnp
from jax import lax
from jax.experimental import pallas as pl
from jax.experimental.pallas import tpu as pltpu
from jax.sharding import PartitionSpec as P

HEAD_DIM = 128
PROMPT = 1024
CONTS = 4
CONT = 256
RANK = 16

norm_eps = 1e-06
adapter_scale = 0.5
rope_base = 1000000.0
masked_score = -1e30
score_scale = HEAD_DIM ** (-0.5)
score_to_log2 = score_scale * math.log2(math.e)

f32 = jnp.float32
bf16 = jnp.bfloat16
VMEM_LIMIT = 60 * 2**20
PIECE = 256


def nt(left, right):
    return lax.dot_general(left, right, (((1,), (1,)), ((), ())), preferred_element_type=f32)


def nn(left, right):
    return lax.dot_general(left, right, (((1,), (0,)), ((), ())), preferred_element_type=f32)


def tn(left, right):
    return lax.dot_general(left, right, (((0,), (0,)), ((), ())), preferred_element_type=f32)


def along_line(array, pairs):
    return lax.ppermute(array, "ctx", [(2 * a + c, 2 * b + c) for a, b in pairs for c in (0, 1)])


def swap_cores(array):
    size = lax.axis_size("ctx")
    return lax.ppermute(array, "ctx", [(i, i ^ 1) for i in range(size)])


def hold_kernel(*refs):
    pass


def hold(arrays, *after):
    anywhere = pl.BlockSpec(memory_space=pl.ANY)
    count = len(arrays)
    return pl.pallas_call(
        hold_kernel,
        in_specs=[anywhere] * (count + len(after)),
        out_specs=[anywhere] * count,
        out_shape=[jax.ShapeDtypeStruct(a.shape, a.dtype) for a in arrays],
        input_output_aliases={i: i for i in range(count)},
        name="hold",
    )(*arrays, *after)


def line_gather(piece, place, line, after=()):
    came = [
        along_line(piece, [(i, (i + by) % line) for i in range(line)]) for by in range(1, line)
    ]
    if after:
        came = hold(came, *after)
    out = jnp.zeros((line,) + piece.shape, piece.dtype)
    out = lax.dynamic_update_index_in_dim(out, piece, place, 0)
    for by in range(1, line):
        out = lax.dynamic_update_index_in_dim(out, came[by - 1], (place - by) % line, 0)
    return out


def shard_gather(lined):
    return lax.all_gather(lined, "wsh", axis=0, tiled=False)


def add_up(arrays):
    return functools.reduce(jnp.add, [a.astype(f32) for a in arrays]).astype(bf16)


def reduce_ctx(parts, place, core, line):
    pairs = parts.reshape((line, 2) + parts.shape[1:])
    keep = lax.dynamic_index_in_dim(pairs, core, 1, False)
    give = lax.dynamic_index_in_dim(pairs, 1 - core, 1, False)
    mine = add_up([keep, swap_cores(give)])
    terms = [lax.dynamic_index_in_dim(mine, place, 0, False)]
    for by in range(1, line):
        out = lax.dynamic_index_in_dim(mine, (place + by) % line, 0, False)
        terms.append(along_line(out, [(i, (i + by) % line) for i in range(line)]))
    return add_up(terms)


def across(array, by):
    size = lax.axis_size("wsh")
    return lax.ppermute(array, "wsh", [(i, i ^ by) for i in range(size)])


def reduce_wsh(parts, shard):
    terms = [lax.dynamic_index_in_dim(parts, shard, 0, False)]
    for by in range(1, parts.shape[0]):
        terms.append(across(lax.dynamic_index_in_dim(parts, shard ^ by, 0, False), by))
    return add_up(terms)


def gather_all(piece, place, core, shard, line):
    own = line_gather(piece, place, line)
    shards = lax.axis_size("wsh")
    all_own = jnp.zeros((shards,) + own.shape, own.dtype)
    all_own = lax.dynamic_update_index_in_dim(all_own, own, shard, 0)
    for by in range(1, shards):
        all_own = lax.dynamic_update_index_in_dim(all_own, across(own, by), shard ^ by, 0)
    other = swap_cores(all_own)
    pair = jnp.stack([jnp.where(core == 0, all_own, other), jnp.where(core == 0, other, all_own)])
    return jnp.moveaxis(pair, 2, 0)


def params(**more):
    return pltpu.CompilerParams(
        dimension_semantics=("arbitrary",), vmem_limit_bytes=VMEM_LIMIT, **more
    )


def whole(array):
    return pl.BlockSpec(array.shape, lambda s, *pre: (0,) * array.ndim)


def by_slot(array):
    return pl.BlockSpec((1,) + array.shape[1:], lambda s, *pre: (s,) + (0,) * (array.ndim - 1))


def second_by_slot(array):
    return pl.BlockSpec(
        (array.shape[0], 1) + array.shape[2:], lambda s, *pre: (0, s) + (0,) * (array.ndim - 2)
    )


def cost(flops, bytes_accessed, exps=0):
    return pl.CostEstimate(flops=int(flops), bytes_accessed=int(bytes_accessed), transcendentals=int(exps))


def slot_lanes(adapter, block, ranks):
    lane = lax.broadcasted_iota(jnp.int32, (block, ranks), 1)
    return lane // RANK == adapter[pl.program_id(0)]


def picked(mask, values):
    return jnp.where(mask, values, 0.0).astype(bf16)


def struct(shape, dtype):
    return jax.ShapeDtypeStruct(shape, dtype)


def turn(u, cos, sin):
    return u * cos + pltpu.roll(u, HEAD_DIM // 2, 1) * sin


def turn_back(u, cos, sin):
    return u * cos - pltpu.roll(u, HEAD_DIM // 2, 1) * sin


def key_value_kernel(
    adapter, tok, gain, weight, bias, in_k, in_v, out_k, out_v, cosine, sine,
    normed_ref, rank_k_ref, rank_v_ref, kv_ref,
):
    hidden = tok[0].astype(f32)
    inverse = lax.rsqrt(jnp.mean(hidden * hidden, axis=-1, keepdims=True) + norm_eps)
    normed = (hidden * inverse * gain[...]).astype(bf16)
    normed_ref[0] = normed
    mask = slot_lanes(adapter, normed.shape[0], in_k.shape[0])
    kv_width = kv_ref.shape[-1] // 2
    lin = nt(normed, weight[...]) + bias[...]
    rank_k = picked(mask, nt(normed, in_k[...]))
    rank_v = picked(mask, nt(normed, in_v[...]))
    rank_k_ref[0], rank_v_ref[0] = rank_k, rank_v
    key = lin[:, :kv_width] + adapter_scale * nn(rank_k, out_k[...])
    value = lin[:, kv_width:] + adapter_scale * nn(rank_v, out_v[...])
    cos, sin = cosine[...], sine[...]
    for h in range(kv_width // HEAD_DIM):
        part = slice(h * HEAD_DIM, (h + 1) * HEAD_DIM)
        kv_ref[0, :, part] = turn(key[:, part], cos, sin).astype(bf16)
    kv_ref[0, :, kv_width:] = value.astype(bf16)


def key_value_side(adapter_of, tokens, gain, weight, bias, adapters, cosine, sine):
    slots, block, width = tokens.shape
    shared = (gain, weight, bias, *adapters, cosine, sine)
    ranks = struct((slots, block, adapters[0].shape[0]), bf16)
    outs = (struct(tokens.shape, bf16), ranks, ranks, struct((slots, block, weight.shape[0]), bf16))
    return pl.pallas_call(
        key_value_kernel,
        grid_spec=pltpu.PrefetchScalarGridSpec(
            num_scalar_prefetch=1,
            grid=(slots,),
            in_specs=[by_slot(tokens)] + [whole(a) for a in shared],
            out_specs=[by_slot(o) for o in outs],
        ),
        out_shape=outs,
        compiler_params=params(),
        cost_estimate=cost(3 * slots * block * width * weight.shape[0], 12e6),
        name="key_value_side",
    )(adapter_of, tokens, *shared)


def query_kernel(adapter, normed, weight, bias, in_q, out_q, cosine, sine, rank_ref, query_ref):
    x = normed[0]
    mask = slot_lanes(adapter, x.shape[0], in_q.shape[0])
    rank = picked(mask, nt(x, in_q[...]))
    rank_ref[0] = rank
    query = nt(x, weight[...]) + bias[...] + adapter_scale * nn(rank, out_q[...])
    cos, sin = cosine[...], sine[...]
    for h in range(query.shape[1] // HEAD_DIM):
        part = slice(h * HEAD_DIM, (h + 1) * HEAD_DIM)
        query_ref[0, :, part] = turn(query[:, part], cos, sin).astype(bf16)


def query_side(adapter_of, normed, weight, bias, adapters, cosine, sine):
    slots, block, width = normed.shape
    shared = (weight, bias, *adapters, cosine, sine)
    outs = (struct((slots, block, adapters[0].shape[0]), bf16), struct(normed.shape, bf16))
    return pl.pallas_call(
        query_kernel,
        grid_spec=pltpu.PrefetchScalarGridSpec(
            num_scalar_prefetch=1,
            grid=(slots,),
            in_specs=[by_slot(normed)] + [whole(a) for a in shared],
            out_specs=[by_slot(o) for o in outs],
        ),
        out_shape=outs,
        compiler_params=params(),
        cost_estimate=cost(2.5 * slots * block * width * width, 12e6),
        name="query_side",
    )(adapter_of, normed, *shared)


def attend_kernel(kv_heads, group, mates, flags, *refs):
    query, own, even, odd = refs[:4]
    mate = refs[4] if mates else None
    context_ref, mixed_ref, log_ref = refs[4 + mates :]
    block = query.shape[1]
    half = even.shape[0]
    kv_width = kv_heads * HEAD_DIM
    rows = lax.broadcasted_iota(jnp.int32, (block, block), 0)
    cols = lax.broadcasted_iota(jnp.int32, (block, block), 1)
    causal = rows <= cols
    bias = [jnp.where(flags[i] != 0, 0.0, masked_score) for i in range(2 * half + mates)]
    for kv in range(kv_heads):
        k_part = slice(kv * HEAD_DIM, (kv + 1) * HEAD_DIM)
        v_part = slice(kv_width + kv * HEAD_DIM, kv_width + (kv + 1) * HEAD_DIM)
        sources = [own[0]] + [even[i, 0] for i in range(half)] + [odd[i, 0] for i in range(half)]
        sources += [mate[0]] if mates else []
        keys = [s[:, k_part] for s in sources]
        values_t = [s[:, v_part].T for s in sources]
        for g in range(group):
            h = kv * group + g
            part = slice(h * HEAD_DIM, (h + 1) * HEAD_DIM)
            q = query[0, :, part]
            scores = [nt(k, q) for k in keys]
            scores[0] = jnp.where(causal, scores[0], masked_score)
            scores = scores[:1] + [s + b for s, b in zip(scores[1:], bias)]
            top = functools.reduce(jnp.maximum, [jnp.max(s, axis=0, keepdims=True) for s in scores])
            shift = top * score_to_log2
            total, mixed = 0.0, 0.0
            for s, v in zip(scores, values_t):
                p = jnp.exp2(s * score_to_log2 - shift)
                total = total + jnp.sum(p, axis=0, keepdims=True)
                mixed = mixed + nn(v, p.astype(bf16))
            mixed = mixed / total
            mixed_ref[0, h] = mixed
            log_ref[0, h : h + 1, :] = shift + jnp.log2(total)
            context_ref[0, :, part] = mixed.T.astype(bf16)


def attend(flags, query, own, even, odd, mate, kv_heads):
    slots, block, width = query.shape
    heads = width // HEAD_DIM
    mates = len(mate)
    operands = (query, own, even, odd, *mate)
    specs = [by_slot(query), by_slot(own), second_by_slot(even), second_by_slot(odd)]
    specs += [by_slot(m) for m in mate]
    outs = (
        struct((slots, block, width), bf16),
        struct((slots, heads, HEAD_DIM, block), f32),
        struct((slots, heads, block), f32),
    )
    return pl.pallas_call(
        functools.partial(attend_kernel, kv_heads, heads // kv_heads, mates),
        grid_spec=pltpu.PrefetchScalarGridSpec(
            num_scalar_prefetch=1, grid=(slots,), in_specs=specs, out_specs=[by_slot(o) for o in outs]
        ),
        out_shape=outs,
        compiler_params=params(),
        cost_estimate=cost(20e9, 20e6, slots * heads * block * (own.shape[1] * 5)),
        name="attend",
    )(flags, *operands)


def attend_back_kernel(kv_heads, group, mates, flags, *refs):
    query, own, even, odd = refs[:4]
    mate = refs[4] if mates else None
    grad, mixed_ref, log_ref, cosine, sine = refs[4 + mates : 9 + mates]
    d_query, d_own, d_even, d_odd = refs[9 + mates : 13 + mates]
    d_mate = refs[13 + mates] if mates else None
    acc = refs[13 + 2 * mates]
    block = query.shape[1]
    half = even.shape[0]
    kv_width = kv_heads * HEAD_DIM
    rows = lax.broadcasted_iota(jnp.int32, (block, block), 0)
    cols = lax.broadcasted_iota(jnp.int32, (block, block), 1)
    causal = rows <= cols
    bias = [jnp.where(flags[i] != 0, 0.0, masked_score) for i in range(2 * half + mates)]
    cos, sin = cosine[...], sine[...]
    for kv in range(kv_heads):
        k_part = slice(kv * HEAD_DIM, (kv + 1) * HEAD_DIM)
        v_part = slice(kv_width + kv * HEAD_DIM, kv_width + (kv + 1) * HEAD_DIM)
        sources = [own[0]] + [even[i, 0] for i in range(half)] + [odd[i, 0] for i in range(half)]
        sources += [mate[0]] if mates else []
        keys = [s[:, k_part] for s in sources]
        keys_t = [k.T for k in keys]
        values = [s[:, v_part] for s in sources]
        for g in range(group):
            h = kv * group + g
            part = slice(h * HEAD_DIM, (h + 1) * HEAD_DIM)
            q = query[0, :, part]
            d_o = grad[0, :, part]
            delta = jnp.sum(d_o.astype(f32).T * mixed_ref[0, h], axis=0, keepdims=True)
            shift = log_ref[0, h : h + 1, :]
            d_q = 0.0
            for i in range(len(sources)):
                s = nt(keys[i], q)
                s = jnp.where(causal, s, masked_score) if i == 0 else s + bias[i - 1]
                p = jnp.exp2(s * score_to_log2 - shift)
                d_p = nt(values[i], d_o)
                d_s = (p * (d_p - delta)).astype(bf16)
                d_value = nn(p.astype(bf16), d_o)
                d_key = nn(d_s, q)
                if g == 0:
                    acc[i, :, v_part] = d_value
                    acc[i, :, k_part] = d_key
                else:
                    acc[i, :, v_part] += d_value
                    acc[i, :, k_part] += d_key
                d_q = d_q + nn(keys_t[i], d_s)
            u = d_q.T * score_scale
            d_query[0, :, part] = (u * cos - pltpu.roll(u, HEAD_DIM // 2, 1) * sin).astype(bf16)
    targets = [(d_own, 0)] + [(d_even, i) for i in range(half)] + [(d_odd, i) for i in range(half)]
    targets += [(d_mate, 0)] if mates else []
    for i, (target, j) in enumerate(targets):
        if target is d_own or target is d_mate:
            target[0, :, :kv_width] = (acc[i, :, :kv_width] * score_scale).astype(target.dtype)
            target[0, :, kv_width:] = acc[i, :, kv_width:].astype(target.dtype)
        else:
            target[j, 0, :, :kv_width] = (acc[i, :, :kv_width] * score_scale).astype(target.dtype)
            target[j, 0, :, kv_width:] = acc[i, :, kv_width:].astype(target.dtype)


def attend_back(flags, query, own, even, odd, mate, grad, mixed, logs, cosine, sine, kv_heads):
    slots, block, width = query.shape
    heads = width // HEAD_DIM
    mates = len(mate)
    operands = (query, own, even, odd, *mate, grad, mixed, logs, cosine, sine)
    specs = [by_slot(query), by_slot(own), second_by_slot(even), second_by_slot(odd)]
    specs += [by_slot(m) for m in mate]
    specs += [by_slot(grad), by_slot(mixed), by_slot(logs), whole(cosine), whole(sine)]
    outs = (
        struct(query.shape, bf16),
        struct(own.shape, f32),
        struct(even.shape, bf16),
        struct(odd.shape, bf16),
        *(struct(m.shape, bf16) for m in mate),
    )
    out_specs = [by_slot(outs[0]), by_slot(outs[1]), second_by_slot(even), second_by_slot(odd)]
    out_specs += [by_slot(m) for m in mate]
    count = 1 + 2 * even.shape[0] + mates
    return pl.pallas_call(
        functools.partial(attend_back_kernel, kv_heads, heads // kv_heads, mates),
        grid_spec=pltpu.PrefetchScalarGridSpec(
            num_scalar_prefetch=1,
            grid=(slots,),
            in_specs=specs,
            out_specs=out_specs,
            scratch_shapes=[pltpu.VMEM((count,) + own.shape[1:], f32)],
        ),
        out_shape=outs,
        compiler_params=params(),
        cost_estimate=cost(50e9, 40e6, slots * heads * block * (own.shape[1] * 5)),
        name="attend_back",
    )(flags, *operands)


def middle_kernel(
    adapter, live, context, tok, cot, weight, in_o, out_o, gain, in_g, in_u, out_d,
    mid_ref, normed_ref, grad_ref, rank_o_ref, rank_g_ref, rank_u_ref, grad_rank_ref,
):
    s = pl.program_id(0)
    ctx = context[0]
    mask = slot_lanes(adapter, ctx.shape[0], in_o.shape[0])
    rank = picked(mask, nt(ctx, in_o[...]))
    rank_o_ref[0] = rank
    mid = tok[0].astype(f32) + nt(ctx, weight[...]) + adapter_scale * nn(rank, out_o[...])
    mid_ref[0] = mid
    inverse = lax.rsqrt(jnp.mean(mid * mid, axis=-1, keepdims=True) + norm_eps)
    normed = (mid * inverse * gain[...]).astype(bf16)
    normed_ref[0] = normed
    rank_g_ref[0] = picked(mask, nt(normed, in_g[...]))
    rank_u_ref[0] = picked(mask, nt(normed, in_u[...]))
    on = jnp.where(live[s] != 0, 1.0, 0.0)
    grad = (cot[0].astype(f32) * on).astype(bf16)
    grad_ref[0] = grad
    grad_rank_ref[0] = picked(mask, adapter_scale * nt(grad, out_d[...]))


def middle_side(adapter_of, live, context, tokens, cotangent, weight, in_o, out_o, gain, in_g, in_u, out_d):
    slots, block, width = tokens.shape
    shared = (weight, in_o, out_o, gain, in_g, in_u, out_d)
    rank = struct((slots, block, in_o.shape[0]), bf16)
    wide = struct(tokens.shape, bf16)
    outs = (struct(tokens.shape, f32), wide, wide, rank, rank, rank, rank)
    return pl.pallas_call(
        middle_kernel,
        grid_spec=pltpu.PrefetchScalarGridSpec(
            num_scalar_prefetch=2,
            grid=(slots,),
            in_specs=[by_slot(a) for a in (context, tokens, cotangent)] + [whole(a) for a in shared],
            out_specs=[by_slot(o) for o in outs],
        ),
        out_shape=outs,
        compiler_params=params(),
        cost_estimate=cost(3 * slots * block * width * width, 28e6),
        name="middle_side",
    )(adapter_of, live, context, tokens, cotangent, *shared)


def weight_copies(core, own, other, gate, up, down, sems):
    copies = []

    def add(source, target):
        copies.append(pltpu.make_async_copy(source, target, sems.at[len(copies)]))

    shards, line, rows, cols = own.shape
    rows //= 3
    for side, half in ((core, own), (1 - core, other)):
        for w in range(shards):
            span = pl.ds(w * cols, cols)
            add(half.at[w, :, pl.ds(0, rows), :], gate.at[side, :, :, span])
            add(half.at[w, :, pl.ds(rows, rows), :], up.at[side, :, :, span])
            for z in range(line):
                add(
                    half.at[w, z, pl.ds(2 * rows, rows), :],
                    down.at[side, w, :, pl.ds(z * cols, cols)],
                )
    return copies


def wide_copies(core, own, other, gate, up, down, sems):
    copies = []
    for side, half in ((core, own), (1 - core, other)):
        for i, target in enumerate((gate, up, down)):
            copies.append(pltpu.make_async_copy(half.at[i], target.at[side], sems.at[len(copies)]))
    return copies


def feed_kernel(first, plan, span, core, own, other, normed, grad, rank_d, rank_g, rank_u,
                in_d, out_g, out_u, *refs):
    if first:
        sums_in = None
    else:
        sums_in, refs = refs[:5], refs[5:]
    y_ref, dx_ref, rd_ref, rg_ref, ru_ref, terms_ref = refs[:6]
    gate_w, up_w, down_w, acc, sems = refs[6:]
    copies = plan(core[0], own, other, gate_w, up_w, down_w, sems)
    s = pl.program_id(0)

    @pl.when(s == 0)
    def _():
        for c in copies:
            c.start()
        acc[...] = jnp.zeros_like(acc)
        for c in copies:
            c.wait()

    _, line, rows, width = gate_w.shape
    hidden = 2 * line * rows
    gate_m = gate_w[...].reshape(hidden, width)
    up_m = up_w[...].reshape(hidden, width)
    down_m = down_w[...].reshape(hidden, width)
    x, g = normed[0], grad[0]
    r_d, r_g, r_u = rank_d[0], rank_g[0], rank_u[0]
    sums = [0.0] * 5 if first else [r[0] for r in sums_in]
    for at in range(0, hidden, span):
        part = slice(at, min(at + span, hidden))
        o_g, o_u, i_d = out_g[part], out_u[part], in_d[part]
        w_g, w_u, w_d = gate_m[part], up_m[part], down_m[part]
        gate = nt(x, w_g) + adapter_scale * nt(r_g, o_g)
        up = nt(x, w_u) + adapter_scale * nt(r_u, o_u)
        d_act = nt(g, w_d) + nt(r_d, i_d)
        sig = 1.0 / (1.0 + jnp.exp(-gate))
        lit = gate * sig
        act = (lit * up).astype(bf16)
        d_gate = (d_act * up * sig * (1.0 + gate * (1.0 - sig))).astype(bf16)
        d_up = (d_act * lit).astype(bf16)
        sums[0] = sums[0] + nn(act, w_d)
        sums[1] = sums[1] + nn(d_gate, w_g) + nn(d_up, w_u)
        sums[2] = sums[2] + nn(act, i_d)
        sums[3] = sums[3] + nn(d_gate, o_g)
        sums[4] = sums[4] + nn(d_up, o_u)
        acc[0, :, part] += tn(r_g, d_gate)
        acc[1, :, part] += tn(r_u, d_up)
        acc[2, :, part] += tn(r_d, act)
    for ref, value in zip((y_ref, dx_ref, rd_ref, rg_ref, ru_ref), sums):
        ref[0] = value

    @pl.when(s == pl.num_programs(0) - 1)
    def _():
        for i, scale in enumerate((adapter_scale, adapter_scale, 1.0)):
            turned = (acc[i] * scale).T.astype(bf16)
            for side in range(2):
                for z in range(line):
                    at = (side * line + z) * rows
                    terms_ref[2 * z + side, i * rows : (i + 1) * rows, :] = turned[at : at + rows]


def feed_part(core, own, other, normed, grad, ranks, adapters, sums):
    slots, block, width = normed.shape
    hidden, rank_width = adapters[0].shape
    first = sums is None
    if own.shape[-1] == width:
        plan, count, line, rows = wide_copies, 6, own.shape[1], own.shape[2]
    else:
        shards, line = own.shape[:2]
        plan, count, rows = weight_copies, 2 * shards * (2 + line), own.shape[2] // 3
    anywhere = pl.BlockSpec(memory_space=pl.ANY)
    operands = (own, other, normed, grad, *ranks, *adapters)
    specs = [anywhere, anywhere, by_slot(normed), by_slot(grad)]
    specs += [by_slot(r) for r in ranks] + [whole(a) for a in adapters]
    aliases = {}
    if not first:
        aliases = {1 + len(operands) + i: i for i in range(len(sums))}
        operands += tuple(sums)
        specs += [by_slot(a) for a in sums]
    rank_sum = struct((slots, block, rank_width), f32)
    wide_sum = struct((slots, block, width), f32)
    terms = struct((2 * line, 3 * rows, rank_width), bf16)
    outs = (wide_sum, wide_sum, rank_sum, rank_sum, rank_sum, terms)
    buffer = pltpu.VMEM((2, line, rows, width), bf16)
    return pl.pallas_call(
        functools.partial(feed_kernel, first, plan, 512),
        grid_spec=pltpu.PrefetchScalarGridSpec(
            num_scalar_prefetch=1,
            grid=(slots,),
            in_specs=specs,
            out_specs=[by_slot(o) for o in outs[:5]] + [whole(terms)],
            scratch_shapes=[
                buffer,
                buffer,
                buffer,
                pltpu.VMEM((3, rank_width, hidden), f32),
                pltpu.SemaphoreType.DMA((count,)),
            ],
        ),
        out_shape=outs,
        input_output_aliases=aliases,
        compiler_params=params(),
        cost_estimate=cost(15 * slots * block * hidden * width, 60e6, slots * block * hidden),
        name="feed_part",
    )(core, *operands)


def rms_back(hidden, gain, grad_normed):
    scaled = grad_normed * gain
    inverse = lax.rsqrt(jnp.mean(hidden * hidden, axis=-1, keepdims=True) + norm_eps)
    return inverse * scaled - hidden * (inverse * inverse * inverse) * jnp.mean(
        scaled * hidden, axis=-1, keepdims=True
    )


def keep_terms(acc, out, terms):
    s = pl.program_id(0)
    total = acc.shape[1]

    @pl.when(s == 0)
    def _():
        at = 0
        for t in terms:
            acc[:, at : at + t.shape[1]] = t
            at += t.shape[1]

    @pl.when(s != 0)
    def _():
        at = 0
        for t in terms:
            acc[:, at : at + t.shape[1]] += t
            at += t.shape[1]

    @pl.when(s == pl.num_programs(0) - 1)
    def _():
        for i in range(out.shape[0]):
            if i * PIECE < total:
                out[i] = acc[:, i * PIECE : (i + 1) * PIECE].astype(bf16)
            else:
                out[i] = jnp.zeros(out.shape[1:], bf16)


def return_kernel(
    adapter, live, y, dx, sum_d, sum_g, sum_u, mid_in, normed, grad, context, rank_o, rank_d, weight,
    in_o, out_o, gain, in_g, in_u, out_d, layer_ref, d_mid_ref, d_ctx_ref, terms_ref, acc,
):
    s = pl.program_id(0)
    on = jnp.where(live[s] != 0, 1.0, 0.0)
    mid = mid_in[0]
    g = grad[0]
    mask = slot_lanes(adapter, g.shape[0], in_o.shape[0])
    rank_down = picked(mask, sum_d[0])
    result = mid + y[0] + adapter_scale * nn(rank_down, out_d[...])
    layer_ref[0] = (result * on).astype(bf16)
    back_g = picked(mask, adapter_scale * sum_g[0])
    back_u = picked(mask, adapter_scale * sum_u[0])
    d_normed = dx[0] + nn(back_g, in_g[...]) + nn(back_u, in_u[...])
    d_mid = g.astype(f32) + rms_back(mid, gain[...], d_normed)
    d_mid_ref[0] = d_mid
    branch = d_mid.astype(bf16)
    back_o = picked(mask, adapter_scale * nt(branch, out_o[...]))
    d_ctx_ref[0] = (nn(branch, weight[...]) + nn(back_o, in_o[...])).astype(bf16)
    x = normed[0]
    keep_terms(
        acc,
        terms_ref,
        (
            tn(back_o, context[0]),
            adapter_scale * tn(rank_o[0], branch),
            tn(back_g, x),
            tn(back_u, x),
            adapter_scale * tn(rank_down, g),
        ),
    )


def piece_count(columns):
    devices = lax.axis_size("ctx") * lax.axis_size("wsh")
    pieces = -(-columns // PIECE)
    return pieces + -pieces % devices


def return_side(adapter_of, live, sums, mid, normed, grad, context, rank_o, rank_d, weight, in_o, out_o,
                gain, in_g, in_u, out_d):
    slots, block, width = mid.shape
    rows = (*sums, mid, normed, grad, context, rank_o, rank_d)
    shared = (weight, in_o, out_o, gain, in_g, in_u, out_d)
    ranks = in_o.shape[0]
    outs = (
        struct(mid.shape, bf16),
        struct(mid.shape, f32),
        struct(mid.shape, bf16),
        struct((piece_count(5 * width), ranks, PIECE), bf16),
    )
    return pl.pallas_call(
        return_kernel,
        grid_spec=pltpu.PrefetchScalarGridSpec(
            num_scalar_prefetch=2,
            grid=(slots,),
            in_specs=[by_slot(r) for r in rows] + [whole(a) for a in shared],
            out_specs=[by_slot(o) for o in outs[:3]] + [whole(outs[3])],
            scratch_shapes=[pltpu.VMEM((ranks, 5 * width), f32)],
        ),
        out_shape=outs,
        compiler_params=params(),
        cost_estimate=cost(4 * slots * block * width * width, 50e6),
        name="return_side",
    )(adapter_of, live, *rows, *shared)


def query_back_kernel(
    adapter, d_query, normed, rank_q, weight, in_q, out_q, d_normed_ref, terms_ref, acc
):
    g, x = d_query[0], normed[0]
    mask = slot_lanes(adapter, g.shape[0], in_q.shape[0])
    rank_back = picked(mask, adapter_scale * nt(g, out_q[...]))
    d_normed_ref[0] = nn(g, weight[...]) + nn(rank_back, in_q[...])
    keep_terms(acc, terms_ref, (tn(rank_back, x), adapter_scale * tn(rank_q[0], g)))


def query_back_side(adapter_of, d_query, normed, rank_q, weight, in_q, out_q):
    slots, block, width = normed.shape
    ranks = in_q.shape[0]
    rows = (d_query, normed, rank_q)
    shared = (weight, in_q, out_q)
    outs = (
        struct(normed.shape, f32),
        struct((piece_count(2 * width), ranks, PIECE), bf16),
    )
    return pl.pallas_call(
        query_back_kernel,
        grid_spec=pltpu.PrefetchScalarGridSpec(
            num_scalar_prefetch=1,
            grid=(slots,),
            in_specs=[by_slot(r) for r in rows] + [whole(a) for a in shared],
            out_specs=[by_slot(outs[0]), whole(outs[1])],
            scratch_shapes=[pltpu.VMEM((ranks, 2 * width), f32)],
        ),
        out_shape=outs,
        compiler_params=params(),
        cost_estimate=cost(3 * slots * block * width * width, 22e6),
        name="query_back_side",
    )(adapter_of, *rows, *shared)


def output_kernel(
    adapter, live, d_kv, d_normed_q, d_mid, normed, rank_k, rank_v, tok, weight, gain, cosine, sine,
    in_k, in_v, out_k, out_v, grad_ref, terms_ref, acc,
):
    s = pl.program_id(0)
    on = jnp.where(live[s] != 0, 1.0, 0.0)
    kv_width = d_kv.shape[-1] // 2
    cos, sin = cosine[...], sine[...]
    back = d_kv[0]
    x = normed[0]
    mask = slot_lanes(adapter, x.shape[0], in_k.shape[0])
    keys = []
    for h in range(kv_width // HEAD_DIM):
        keys.append(turn_back(back[:, h * HEAD_DIM : (h + 1) * HEAD_DIM], cos, sin).astype(bf16))
    g_k, g_v = jnp.concatenate(keys, axis=1), back[:, kv_width:].astype(bf16)
    back_k = picked(mask, adapter_scale * nt(g_k, out_k[...]))
    back_v = picked(mask, adapter_scale * nt(g_v, out_v[...]))
    d_normed = d_normed_q[0] + nn(g_k, weight[:kv_width]) + nn(g_v, weight[kv_width:])
    d_normed = d_normed + nn(back_k, in_k[...]) + nn(back_v, in_v[...])
    hidden = tok[0].astype(f32)
    d_hidden = d_mid[0] + rms_back(hidden, gain[...], d_normed)
    grad_ref[0] = (d_hidden * on).astype(bf16)
    keep_terms(
        acc,
        terms_ref,
        (
            tn(back_k, x),
            tn(back_v, x),
            adapter_scale * tn(rank_k[0], g_k),
            adapter_scale * tn(rank_v[0], g_v),
        ),
    )


def output_side(adapter_of, live, d_kv, d_normed_q, d_mid, normed, rank_k, rank_v, tokens, weight, gain,
                cosine, sine, adapters):
    slots, block, width = tokens.shape
    ranks = adapters[0].shape[0]
    columns = 2 * width + weight.shape[0]
    rows = (d_kv, d_normed_q, d_mid, normed, rank_k, rank_v, tokens)
    shared = (weight, gain, cosine, sine, *adapters)
    outs = (
        struct(tokens.shape, bf16),
        struct((piece_count(columns), ranks, PIECE), bf16),
    )
    return pl.pallas_call(
        output_kernel,
        grid_spec=pltpu.PrefetchScalarGridSpec(
            num_scalar_prefetch=2,
            grid=(slots,),
            in_specs=[by_slot(r) for r in rows] + [whole(a) for a in shared],
            out_specs=[by_slot(outs[0]), whole(outs[1])],
            scratch_shapes=[pltpu.VMEM((ranks, columns), f32)],
        ),
        out_shape=outs,
        compiler_params=params(),
        cost_estimate=cost(3 * slots * block * width * weight.shape[0], 30e6),
        name="output_side",
    )(adapter_of, live, *rows, *shared)


def prompt_blocks(mine, place, line):
    half = line // 2
    from_above = [mine]
    for _ in range(line - 1):
        t = len(from_above)
        pairs = [(z, z - 1) for z in range(1, line) if half <= z + t - 1 < line]
        from_above.append(along_line(from_above[-1], pairs))
    from_below = [mine]
    for _ in range(half - 1):
        t = len(from_below)
        pairs = [(z, z + 1) for z in range(line - 1) if half <= z - t + 1]
        from_below.append(along_line(from_below[-1], pairs))
    blocks = []
    for b in range(half, line):
        out = mine
        for z in range(line):
            if z < b:
                out = jnp.where(place == z, from_above[b - z], out)
            elif z > b:
                out = jnp.where(place == z, from_below[z - b], out)
        blocks.append(out)
    return jnp.stack(blocks)


def return_blocks(parts, place, line):
    half = line // 2

    def chain(parts, sends):
        total = parts
        for pairs, block_of in sends:
            at = jnp.clip(block_of - half, 0, half - 1)
            out = lax.dynamic_index_in_dim(total, at, 0, False)
            came, at_in = along_line(out, pairs[0]), jnp.clip(pairs[1] - half, 0, half - 1)
            old = lax.dynamic_index_in_dim(total, at_in, 0, False)
            total = lax.dynamic_update_index_in_dim(
                total, (old.astype(f32) + came.astype(f32)).astype(total.dtype), at_in, 0
            )
        return total

    up = []
    for t in range(1, line):
        pairs = [(z, z + 1) for z in range(line - 1) if half <= line - t + z < line]
        up.append(((pairs, line - t + place - 1), line - t + place))
    down = []
    for t in range(1, half):
        shift = half - 1 + t - (line - 1)
        pairs = [(z, z - 1) for z in range(1, line) if half <= shift + z < z]
        down.append(((pairs, shift + place + 1), shift + place))
    owned = jnp.clip(place - half, 0, half - 1)
    own = lax.dynamic_index_in_dim(parts, owned, 0, False).astype(f32)
    through_up = lax.dynamic_index_in_dim(chain(parts, up), owned, 0, False).astype(f32)
    if not down:
        return jnp.where(place >= half, through_up, 0.0)
    through_down = lax.dynamic_index_in_dim(chain(parts, down), owned, 0, False).astype(f32)
    return jnp.where(place >= half, through_up + through_down - own, 0.0)


def sum_pieces(pieces, place, core, shard, line):
    shards = lax.axis_size("wsh")
    each = pieces.shape[0] // (2 * line * shards)
    cut = pieces.reshape((2 * line, shards, each) + pieces.shape[1:])
    mine = reduce_wsh(reduce_ctx(cut, place, core, line), shard)
    return gather_all(mine, place, core, shard, line).reshape(pieces.shape)


def lay_out_kernel(widths, *refs):
    pieces, outs = refs[0], refs[1:]
    at = 0
    for out, width in zip(outs, widths):
        for i in range(width // PIECE):
            block = pieces[at].astype(f32)
            out[:, :, i * PIECE : (i + 1) * PIECE] = block.reshape(out.shape[:2] + (PIECE,))
            at += 1


def lay_out(pieces, widths):
    adapters = pieces.shape[1] // RANK
    return pl.pallas_call(
        functools.partial(lay_out_kernel, widths),
        out_shape=tuple(struct((adapters, RANK, w), f32) for w in widths),
        compiler_params=pltpu.CompilerParams(vmem_limit_bytes=VMEM_LIMIT),
        name="lay_out",
    )(pieces)


def turn_kernel(sums, *outs):
    for i, out in enumerate(outs):
        out[...] = sums[i].astype(f32).T.reshape(out.shape)


def turn_over(sums):
    count, hidden, ranks = sums.shape
    step = 1280
    out = struct((ranks // RANK, RANK, hidden), f32)
    return pl.pallas_call(
        turn_kernel,
        grid=(hidden // step,),
        in_specs=[pl.BlockSpec((count, step, ranks), lambda i: (0, i, 0))],
        out_specs=[pl.BlockSpec(out.shape[:2] + (step,), lambda i: (0, 0, i))] * count,
        out_shape=(out,) * count,
        compiler_params=params(),
        name="turn_over",
    )(sums)


def local(
    tokens,
    cotangent,
    group_slot,
    group_adapter,
    attn_gain,
    mlp_gain,
    w_query,
    w_key,
    w_value,
    w_output,
    w_gate,
    w_up,
    w_down,
    query_bias,
    key_bias,
    value_bias,
    adapt_query_in,
    adapt_query_out,
    adapt_key_in,
    adapt_key_out,
    adapt_value_in,
    adapt_value_out,
    adapt_output_in,
    adapt_output_out,
    adapt_gate_in,
    adapt_gate_out,
    adapt_up_in,
    adapt_up_out,
    adapt_down_in,
    adapt_down_out,
):
    slots, block, width = tokens.shape
    ctx_size, shards = lax.axis_size("ctx"), lax.axis_size("wsh")
    line = ctx_size // 2
    ctx_place, shard_place = lax.axis_index("ctx"), lax.axis_index("wsh")
    place, core = ctx_place // 2, ctx_place % 2
    kv_width = key_bias.shape[0]
    kv_heads = kv_width // HEAD_DIM
    hidden = adapt_gate_out.shape[-1]
    if line != shards or (CONTS * CONT) != line * block or CONT // block > 2:
        raise ValueError("unsupported mesh")
    mates = CONT // block - 1

    slot_ids = shard_place * slots + jnp.arange(slots, dtype=jnp.int32)
    matches = group_slot[None, :] == slot_ids[:, None]
    live = jnp.any(matches, axis=1).astype(jnp.int32)
    adapter_of = jnp.sum(jnp.where(matches, group_adapter[None, :], 0), axis=1).astype(jnp.int32)
    index = ctx_place * block + jnp.arange(block, dtype=jnp.int32)
    position = jnp.where(index >= CONTS * CONT, index - CONTS * CONT, PROMPT + index % CONT)
    frequency = rope_base ** (-(jnp.arange(HEAD_DIM // 2, dtype=f32) * 2.0) / HEAD_DIM)
    angles = position.astype(f32)[:, None] * frequency[None, :]
    cosine = jnp.concatenate([jnp.cos(angles), jnp.cos(angles)], axis=-1)
    sine = jnp.concatenate([-jnp.sin(angles), jnp.sin(angles)], axis=-1)

    is_cont = ctx_place < line
    of_side = [2 * (line // 2 + i) + core for i in range(line // 2)]
    of_other = [2 * (line // 2 + i) + 1 - core for i in range(line // 2)]
    flags = [(is_cont | (b < ctx_place)) for b in of_side + of_other]
    flags += [is_cont & (core == 1)] if mates else []
    flags = jnp.stack(flags).astype(jnp.int32)

    def natural(own, other, at, count):
        pair = jnp.stack([own[:, :, at : at + count], other[:, :, at : at + count]])
        pair = jnp.where(core == 0, pair, pair[::-1])
        return jnp.transpose(pair, (2, 0, 3, 1, 4)).reshape(line * 2 * count, width)

    q_rows, kv_rows = w_query.shape[1], w_key.shape[1]
    lined_qkv = line_gather(jnp.concatenate([w_query.T, w_key.T, w_value.T], axis=0), place, line)
    own = shard_gather(lined_qkv)
    other = swap_cores(own)
    (o_piece,) = hold([w_output.T], lined_qkv)
    lined_o = line_gather(o_piece, place, line)
    q_weight = natural(own, other, 0, q_rows)
    kv_weight = jnp.concatenate(
        [natural(own, other, q_rows, kv_rows), natural(own, other, q_rows + kv_rows, kv_rows)], axis=0
    )
    own = shard_gather(lined_o)
    other = swap_cores(own)
    o_weight = natural(own, other, 0, w_output.shape[1])

    shard_hidden = w_gate.shape[1]
    shard_cols = w_gate.shape[0]
    parts = 5
    rows = shard_hidden // parts
    halves = w_down.reshape(2, shard_hidden, w_down.shape[1])
    kept = lax.dynamic_index_in_dim(halves, core, 0, False)
    given = swap_cores(lax.dynamic_index_in_dim(halves, 1 - core, 0, False))
    down_piece = jnp.where(
        core == 0,
        jnp.concatenate([kept, given], axis=1),
        jnp.concatenate([given, kept], axis=1),
    )
    turned = [w_gate.T, w_up.T, down_piece]
    pieces = [
        jnp.concatenate([m[i * rows : (i + 1) * rows] for m in turned], axis=0) for i in range(parts)
    ]
    (pieces[0],) = hold([pieces[0]], lined_o)
    lined = [line_gather(pieces[0], place, line)]
    halves = [shard_gather(lined[0])]

    def widen(half):
        cut = half.reshape(shards, line, 3, rows, shard_cols)
        out_in = jnp.transpose(cut[:, :, :2], (2, 1, 3, 0, 4)).reshape(2, line, rows, width)
        in_out = jnp.transpose(cut[:, :, 2], (0, 2, 1, 3)).reshape(1, shards, rows, width)
        return jnp.concatenate([out_in, in_out], axis=0)

    def flat(adapters):
        return adapters.reshape(-1, adapters.shape[-1])

    def by_part(adapters):
        cut = flat(adapters).T.reshape(line, 2, parts, rows, -1)
        return jnp.transpose(cut, (2, 1, 0, 3, 4)).reshape(parts, hidden // parts, -1)

    query_in, key_in, value_in, output_in, gate_in, up_in = (
        flat(a)
        for a in (adapt_query_in, adapt_key_in, adapt_value_in, adapt_output_in, adapt_gate_in, adapt_up_in)
    )
    query_out, key_out, value_out, output_out, down_out = (
        flat(a)
        for a in (adapt_query_out, adapt_key_out, adapt_value_out, adapt_output_out, adapt_down_out)
    )

    gain_one = attn_gain.astype(f32)[None, :]
    gain_two = mlp_gain.astype(f32)[None, :]
    q_bias = query_bias.astype(f32)[None, :]
    kv_bias = jnp.concatenate([key_bias, value_bias]).astype(f32)[None, :]

    kv_adapters = (key_in, value_in, key_out, value_out)
    normed, rank_k, rank_v, key_value = key_value_side(
        adapter_of, tokens, gain_one, kv_weight, kv_bias, kv_adapters, cosine, sine
    )
    (pieces[1],) = hold([pieces[1]], key_value)
    side = prompt_blocks(key_value, place, line)
    other_side = swap_cores(side)
    mate = (swap_cores(key_value),) if mates else ()
    rank_q, queries = query_side(
        adapter_of, normed, q_weight, q_bias, (query_in, query_out), cosine, sine
    )
    context, mixed, logs = attend(flags, queries, key_value, side, other_side, mate, kv_heads)
    lined.append(line_gather(pieces[1], place, line, (context,)))
    halves.append(shard_gather(lined[1]))
    halves[0], pieces[2] = hold([halves[0], pieces[2]], context, lined[1])
    others = [swap_cores(halves[0])]
    mid, normed2, grad_out, rank_o, rank_g, rank_u, rank_d = middle_side(
        adapter_of, live, context, tokens, cotangent, o_weight, output_in, output_out, gain_two,
        gate_in, up_in, down_out,
    )

    down_in, gate_out, up_out = by_part(adapt_down_in), by_part(adapt_gate_out), by_part(adapt_up_out)
    core_place = core.astype(jnp.int32)[None]
    lined.append(line_gather(pieces[2], place, line, (normed2,)))
    halves.append(shard_gather(lined[2]))
    (normed2, pieces[3]) = hold([normed2, pieces[3]], lined[2])
    sums, hidden_terms = None, []
    for i in range(parts):
        if i:
            ready = list(sums[2:3])
            if i + 2 < parts:
                ready.append(lined[i + 2])
            if i >= 2:
                ready.append(hidden_terms[i - 2])
            (halves[i],) = hold([halves[i]], *ready)
            others.append(swap_cores(halves[i]))
        own, other = halves[i], others[i]
        if shard_cols % 128:
            own, other = widen(own), widen(other)
        *sums, terms = feed_part(
            core_place, own, other, normed2, grad_out, (rank_d, rank_g, rank_u),
            (down_in[i], gate_out[i], up_out[i]), sums,
        )
        if i + 3 < parts:
            lined.append(line_gather(pieces[i + 3], place, line, (terms,)))
            halves.append(shard_gather(lined[i + 3]))
            if i + 4 < parts:
                (pieces[i + 4],) = hold([pieces[i + 4]], terms)
        hidden_terms.append(reduce_ctx(terms, place, core, line))
    (sums[2],) = hold([sums[2]], hidden_terms[parts - 2])
    hidden_terms = [t.reshape(3, rows, -1) for t in hidden_terms]
    layer_out, d_mid, d_context, terms = return_side(
        adapter_of, live, sums, mid, normed2, grad_out, context, rank_o, rank_d, o_weight,
        output_in, output_out, gain_two, gate_in, up_in, down_out,
    )

    hidden_terms = jnp.concatenate(hidden_terms, axis=1)
    hidden_terms = reduce_wsh(
        hidden_terms.reshape(shards, 3 * shard_hidden // shards, -1), shard_place
    )
    hidden_sums = gather_all(hidden_terms, place, core, shard_place, line)
    hidden_sums = hidden_sums.reshape(2 * line, 3, shard_hidden, -1)
    hidden_sums = jnp.transpose(hidden_sums, (1, 0, 2, 3)).reshape(3, hidden, -1)
    g_gate_out, g_up_out, g_down_in = turn_over(hidden_sums)
    g_output_in, g_output_out, g_gate_in, g_up_in, g_down_out = lay_out(
        sum_pieces(terms, place, core, shard_place, line), (width,) * 5
    )

    back = attend_back(
        flags, queries, key_value, side, other_side, mate, d_context, mixed, logs, cosine, sine, kv_heads
    )
    d_query, d_own, d_side, d_other = back[:4]
    d_side = (d_side.astype(f32) + swap_cores(d_other).astype(f32)).astype(bf16)
    d_kv = d_own + return_blocks(d_side, place, line)
    if mates:
        d_kv = d_kv + swap_cores(back[4]).astype(f32)
    d_normed_q, terms = query_back_side(
        adapter_of, d_query, normed, rank_q, q_weight, query_in, query_out
    )
    g_query_in, g_query_out = lay_out(
        sum_pieces(terms, place, core, shard_place, line), (width, width)
    )
    input_grad, terms = output_side(
        adapter_of, live, d_kv, d_normed_q, d_mid, normed, rank_k, rank_v, tokens, kv_weight, gain_one,
        cosine, sine, kv_adapters,
    )
    g_key_in, g_value_in, g_key_out, g_value_out = lay_out(
        sum_pieces(terms, place, core, shard_place, line), (width, width, kv_width, kv_width)
    )
    return (
        layer_out,
        input_grad,
        g_query_in,
        g_query_out,
        g_key_in,
        g_key_out,
        g_value_in,
        g_value_out,
        g_output_in,
        g_output_out,
        g_gate_in,
        g_gate_out,
        g_up_in,
        g_up_out,
        g_down_in,
        g_down_out,
    )


def solution(mesh):
    weight = P("wsh", "ctx")
    rows = P("wsh", "ctx", None)
    return jax.shard_map(
        local,
        mesh=mesh,
        in_specs=(rows, rows) + (P(),) * 4 + (weight,) * 7 + (P(),) * 17,
        out_specs=(rows, rows) + (P(),) * 14,
        check_vma=False,
    )
```

time: 2610 us -> 1280 us (0.49)
  waiting for transfers between devices: 1380 us -> 374 us
  matrix products: 845 us -> 0 us
  Pallas kernels: 0 us -> 502 us
  starting transfers between devices: 3.51 us -> 187 us
  blocking collectives: 84.5 us -> 0 us
  other arithmetic: 92.3 us -> 55.8 us
  local copies, waits for them, and re-layouts: 167 us -> 135 us
    dot_general x126 -> x0, matrix products: 845 us -> none  [the longest x7 141 us: project_back(): jnp.einsum('sbo,io->sbi', incoming_gradient, weight, preferred_element_ty...]
    psum x1 -> x0, waiting for transfers between devices: 709 us -> none  [local(): lax.psum((by_adapter(g_query_in), by_adapter(g_query_out), by_adapter(g_k...]
    pallas_call x0 -> x32, Pallas kernels: none -> 502 us  [the longest x5 285 us: feed_part(): pl.pallas_call(functools.partial(feed_kernel, first, plan, 512), grid_spe...]
    all_gather x8 -> x7, waiting for transfers between devices: 378 us -> 0.1 us  [shard_gather(): return lax.all_gather(lined, 'wsh', axis=0, tiled=False)]
    ppermute x24 -> x111, starting transfers between devices: 3.16 us -> 186 us  [the longest x65 157 us: along_line(): lax.ppermute(array, 'ctx', [(2 * a + c, 2 * b + c) for a, b in pairs for...]
    ppermute x24 -> x111, waiting for transfers between devices: 288 us -> 374 us  [the longest x65 291 us: along_line(): lax.ppermute(array, 'ctx', [(2 * a + c, 2 * b + c) for a, b in pairs for...]
    all_gather x6 -> x0, blocking collectives: 84.5 us -> none  [the longest x1 20.3 us: local(): lax.all_gather(full_rows[2], 'ctx', axis=1, tiled=True)]
    while x123 -> x0, local copies, waits for them, and re-layouts: 47.9 us -> none
  transfers between devices with their start and end apart: 33 -> 118, of which waited for: 27 -> 43; matrix products, arithmetic and copies ran while one was open for 22% -> 13% of each run, Pallas kernels for 0% -> 35%
where the time goes in v1:
time: 1280 us; the launch traced here: 1270 us
  Pallas kernels  502 us (39%)
  waiting for transfers between devices  374 us (29%)
  starting transfers between devices  187 us (15%)
  local copies, waits for them, and re-layouts  135 us (11%)
  other arithmetic  55.8 us (4%)
  between operations  16.7 us (1%)
    ppermute x65, waiting for transfers between devices, along_line(): lax.ppermute(array, 'ctx', [(2 * a + c, 2 * b + c) for a, b in pairs for...  291 us
    pallas_call x5, Pallas kernels, feed_part(): pl.pallas_call(functools.partial(feed_kernel, first, plan, 512), grid_spe...  285 us
    ppermute x65, starting transfers between devices, along_line(): lax.ppermute(array, 'ctx', [(2 * a + c, 2 * b + c) for a, b in pairs for...  157 us
    pallas_call x1, Pallas kernels, attend_back(): pl.pallas_call(functools.partial(attend_back_kernel, kv_heads, heads // k...  61.6 us
    ppermute x22, waiting for transfers between devices, swap_cores(): return lax.ppermute(array, 'ctx', [(i, i ^ 1) for i in range(size)])  44.3 us
    ppermute x24, waiting for transfers between devices, across(): return lax.ppermute(array, 'wsh', [(i, i ^ by) for i in range(size)])  38.9 us
    pallas_call x1, Pallas kernels, attend(): pl.pallas_call(functools.partial(attend_kernel, kv_heads, heads // kv_hea...  34.4 us
    pallas_call x1, Pallas kernels, return_side(): pl.pallas_call(return_kernel, grid_spec=pltpu.PrefetchScalarGridSpec(num_...  31 us
  transfers between devices with their start and end apart: 118, of which 43 were waited for; matrix products, arithmetic and copies ran while one was open for 13% of the time, Pallas kernels for 35%

profile of v1, /device:TPU:0, one launch (start us, length us, event | category | flops | bytes accessed | tf_op | source)
XLA Modules:
  0.0 1271.1 jit_solution(963551328701485905)
XLA Ops:
  20.9 7.6 collective-permute-done.2
  45.9 6.1 collective-permute-done.5
  62.1 11.1 collective-permute-done.7
  73.3 21.3 %collective-permute-done.8 = bf16[672,384]{1,0:T(8,128)(2,1)S(1)} collective-permute-done((bf16[672,384]{1,0:T(8,128)(2,1)}, bf16[672,384]{1,0:T(8,128)(2,1)S(1)}, u32[]{:S(2)}, u32[]{:S(2)}) %collective-permute-start.8) | collective-permute-done | bytes 516128 | tf_op jit(solution)/shard_map/ppermute | solution.py:43
  112.3 10.1 key_value_side.1
  127.0 59.0 %collective-permute-done.13 = bf16[4,256,512]{2,1,0:T(8,128)(2,1)} collective-permute-done((bf16[4,256,512]{2,1,0:T(8,128)(2,1)S(1)}, bf16[4,256,512]{2,1,0:T(8,128)(2,1)}, u32[]{:S(2)}, u32[]{:S(2)}) %collective-permute-start.13) | collective-permute-done | bytes 1048608 | tf_op jit(solution)/shard_map/ppermute | solution.py:43
  199.2 37.2 %collective-permute-done.14 = bf16[4,256,512]{2,1,0:T(8,128)(2,1)} collective-permute-done((bf16[4,256,512]{2,1,0:T(8,128)(2,1)}, bf16[4,256,512]{2,1,0:T(8,128)(2,1)}, u32[]{:S(2)}, u32[]{:S(2)}) %collective-permute-start.14) | collective-permute-done | bytes 1048608 | tf_op jit(solution)/shard_map/ppermute | solution.py:43
  253.9 12.2 query_side.1
  266.1 34.4 %attend.1 = (bf16[4,256,1536]{2,1,0:T(8,128)(2,1)}, f32[4,12,128,256]{3,2,1,0:T(8,128)}, f32[4,12,256]{2,1,0:T(8,128)}) custom-call(s32[4]{0:T(128)} %add_convert_fusion.1.flags, bf16[4,256,1536]{2,1,0:T(8,128)(2,1)} %get-tuple-element.105.refs_0_, bf16[4,256,512]{2,1,0:T(8,128)(2,1)} %get-tuple-element.106.refs_1_, ...), custom_call_target="tpu_custom_call" | custom-call | flops 20000000000 | bytes 20000000 | tf_op jit(solution)/shard_map/attend/pallas_call | solution.py:294
  331.9 5.2 pad_maximum_fusion.2
  347.7 17.9 %middle_side.1 = (f32[4,256,1536]{2,1,0:T(8,128)}, bf16[4,256,1536]{2,1,0:T(8,128)(2,1)}, bf16[4,256,1536]{2,1,0:T(8,128)(2,1)}, bf16[4,256,128]{2,1,0:T(8,128)(...) custom-call(s32[4]{0:T(128)} %fusion.62.adapter, ...), custom_call_target="tpu_custom_call" | custom-call | flops 7247757312 | bytes 28000000 | tf_op jit(solution)/shard_map/middle_side/pallas_call | solution.py:427
  365.9 15.6 %collective-permute-done.22.refs_1_ = bf16[672,384]{1,0:T(8,128)(2,1)S(1)} collective-permute-done((bf16[672,384]{1,0:T(8,128)(2,1)S(1)}, bf16[672,384]{1,0:T(8,128)(2,1)S(1)}, u32[]{:S(2)}, u32[]{:S(2)}) %collective-permute-start.22) | collective-permute-done | bytes 516128 | tf_op jit(solution)/shard_map/ppermute | solution.py:43
  388.0 10.4 collective-permute-start.27
  401.0 57.4 %feed_part.5 = (f32[4,256,1536]{2,1,0:T(8,128)}, f32[4,256,1536]{2,1,0:T(8,128)}, f32[4,256,128]{2,1,0:T(8,128)}, f32[4,256,128]{2,1,0:T(8,128)}, f32[4,256,128]{2,1,0:T(8,128)}, /*index=5*/bf16[8,672,128]{2,1,0:T(8,128)(2,1)}) custom-call(s32[1]{0:T(128)} %bitcast.core, bf16[4,4,672,384]{3,2,1,0:T(8,128)(2,1)} %get-tuple-element.111.own, ...), custom_call_target="tpu_custom_call" | custom-call | flops 42278584320 | bytes 60000000 | tf_op jit(solution)/shard_map/feed_part/pallas_call | solution.py:554
  470.8 7.4 collective-permute-done.31
  482.7 8.4 collective-permute-done.32
  491.1 11.9 collective-permute-start.25
  508.3 56.5 %feed_part.6 = (f32[4,256,1536]{2,1,0:T(8,128)}, f32[4,256,1536]{2,1,0:T(8,128)}, f32[4,256,128]{2,1,0:T(8,128)}, f32[4,256,128]{2,1,0:T(8,128)}, f32[4,256,128]{2,1,0:T(8,128)}, /*index=5*/bf16[8,672,128]{2,1,0:T(8,128)(2,1)}) custom-call(s32[1]{0:T(128)} %bitcast.core, ...), custom_call_target="tpu_custom_call", output_to_operand_aliasing={{0}: (11, {}), {1}: (12, {}), {2}: (13, {}), {3}: (14, {}),... | custom-call | flops 42278584320 | bytes 60000000 | tf_op jit(solution)/shard_map/feed_part/pallas_call | solution.py:554
  572.1 12.5 collective-permute-done.36
  584.8 5.8 collective-permute-start.37
  595.5 5.8 collective-permute-done.38
  602.8 58.1 %feed_part.7 = (f32[4,256,1536]{2,1,0:T(8,128)}, f32[4,256,1536]{2,1,0:T(8,128)}, f32[4,256,128]{2,1,0:T(8,128)}, f32[4,256,128]{2,1,0:T(8,128)}, f32[4,256,128]{2,1,0:T(8,128)}, /*index=5*/bf16[8,672,128]{2,1,0:T(8,128)(2,1)}) custom-call(s32[1]{0:T(128)} %bitcast.core, ...), custom_call_target="tpu_custom_call", output_to_operand_aliasing={{0}: (11, {}), {1}: (12, {}), {2}: (13, {}), {3}: (14, {}),... | custom-call | flops 42278584320 | bytes 60000000 | tf_op jit(solution)/shard_map/feed_part/pallas_call | solution.py:554
  662.4 12.6 collective-permute-done.41
  686.4 6.9 collective-permute-done.43
  694.1 56.4 %feed_part.8 = (f32[4,256,1536]{2,1,0:T(8,128)}, f32[4,256,1536]{2,1,0:T(8,128)}, f32[4,256,128]{2,1,0:T(8,128)}, f32[4,256,128]{2,1,0:T(8,128)}, f32[4,256,128]{2,1,0:T(8,128)}, /*index=5*/bf16[8,672,128]{2,1,0:T(8,128)(2,1)}) custom-call(s32[1]{0:T(128)} %bitcast.core, ...), custom_call_target="tpu_custom_call", output_to_operand_aliasing={{0}: (11, {}), {1}: (12, {}), {2}: (13, {}), {3}: (14, {}),... | custom-call | flops 42278584320 | bytes 60000000 | tf_op jit(solution)/shard_map/feed_part/pallas_call | solution.py:554
  755.1 9.8 collective-permute-done.46
  775.4 6.5 collective-permute-done.48
  782.1 56.7 %feed_part.9 = (f32[4,256,1536]{2,1,0:T(8,128)}, f32[4,256,1536]{2,1,0:T(8,128)}, f32[4,256,128]{2,1,0:T(8,128)}, f32[4,256,128]{2,1,0:T(8,128)}, f32[4,256,128]{2,1,0:T(8,128)}, /*index=5*/bf16[8,672,128]{2,1,0:T(8,128)(2,1)}) custom-call(s32[1]{0:T(128)} %bitcast.core, ...), custom_call_target="tpu_custom_call", output_to_operand_aliasing={{0}: (11, {}), {1}: (12, {}), {2}: (13, {}), {3}: (14, {}),... | custom-call | flops 42278584320 | bytes 60000000 | tf_op jit(solution)/shard_map/feed_part/pallas_call | solution.py:554
  840.9 31.0 %return_side.1 = (bf16[4,256,1536]{2,1,0:T(8,128)(2,1)}, f32[4,256,1536]{2,1,0:T(8,128)}, bf16[4,256,1536]{2,1,0:T(8,128)(2,1)}, bf16[32,128,256]{2,1,0:T(8,128)(2,1)}) custom-call(s32[4]{0:T(128)} %fusion.62.adapter, s32[4]{0:T(128)} %convert_element_type.476.live, f32[4,256,1536]{2,1,0:T(8,128)} %get-tuple-element.152.y, ...), custom_call_target="tpu_custom_call" | custom-call | flops 9663676416 | bytes 50000000 | tf_op jit(solution)/shard_map/return_side/pallas_call | solution.py:664
  873.8 61.6 %attend_back.1 = (bf16[4,256,1536]{2,1,0:T(8,128)(2,1)}, f32[4,256,512]{2,1,0:T(8,128)}, bf16[2,4,256,512]{3,2,1,0:T(8,128)(2,1)}, bf16[2,4,256,512]{3,2,1,0:T(8,128)(2,1)}) custom-call(s32[4]{0:T(128)} %add_convert_fusion.1.flags, bf16[4,256,1536]{2,1,0:T(8,128)(2,1)} %get-tuple-element.105.refs_0_, bf16[4,256,512]{2,1,0:T(8,128)(2,1)} %get-tuple-element.106.refs_1_, ...), custom_call_target="tpu_custom_call" | custom-call | flops 49999998976 | bytes 40000000 | tf_op jit(solution)/shard_map/attend_back/pallas_call | solution.py:383
  935.8 6.6 collective-permute-start.100
  943.1 16.5 %query_back_side.1 = (f32[4,256,1536]{2,1,0:T(8,128)}, bf16[32,128,256]{2,1,0:T(8,128)(2,1)}) custom-call(s32[4]{0:T(128)} %fusion.62.adapter, bf16[4,256,1536]{2,1,0:T(8,128)(2,1)} %get-tuple-element.167.d_query, bf16[4,256,1536]{2,1,0:T(8,128)(2,1)} %get-tuple-element.104.normed, bf16[4,256,128]{2,1,0:T(8,128)(2,1)} %get-tuple-element.168.rank_q, ...), custom_call_target="tpu_custom_call" | custom-call | flops 7247757312 | bytes 22000000 | tf_op jit(solution)/shard_map/query_back_side/pallas_call | solution.py:699
  984.0 12.5 collective-permute-done.104
  996.6 6.6 collective-permute-start.105
  1003.8 8.1 collective-permute-done.105
  1013.5 5.4 collective-permute-done.106
  1030.6 8.6 collective-permute-done.57
  1050.0 4.9 collective-permute-start.51
  1059.1 20.8 %collective-permute-done.90 = bf16[1,128,256]{2,1,0:T(8,128)(2,1)S(1)} collective-permute-done((bf16[1,128,256]{2,1,0:T(8,128)(2,1)S(1)}, bf16[1,128,256]{2,1,0:T(8,128)(2,1)S(1)}, u32[]{:S(2)}, u32[]{:S(2)}) %collective-permute-start.90) | collective-permute-done | bytes 65568 | tf_op jit(solution)/shard_map/ppermute | solution.py:43
  1093.4 16.7 %collective-permute-done.52 = bf16[4,256,512]{2,1,0:T(8,128)(2,1)S(1)} collective-permute-done((bf16[4,256,512]{2,1,0:T(8,128)(2,1)S(1)}, bf16[4,256,512]{2,1,0:T(8,128)(2,1)S(1)}, u32[]{:S(2)}, u32[]{:S(2)}) %collective-permute-start.52) | collective-permute-done | bytes 1048608 | tf_op jit(solution)/shard_map/ppermute | solution.py:43
  1113.9 7.4 collective-permute-done.65
  1128.8 14.7 %output_side.1 = (bf16[4,256,1536]{2,1,0:T(8,128)(2,1)}, bf16[32,128,256]{2,1,0:T(8,128)(2,1)}) custom-call(s32[4]{0:T(128)} %fusion.62.adapter, s32[4]{0:T(128)} %convert_element_type.476.live, f32[4,256,512]{2,1,0:T(8,128)} %fusion.4.d_kv, f32[4,256,1536]{2,1,0:T(8,128)} %get-tuple-element.169.d_normed_q, f32[4,256,1536]{2,1,0:T(8,128)} %get-tuple-element.170.d_mid, ...), custom_call_target="tpu_custom_call" | custom-call | flops 2415919104 | bytes 30000000 | tf_op jit(solution)/shard_map/output_side/pallas_call | solution.py:760
  1145.0 15.4 %collective-permute-done.66 = bf16[4,1,128,256]{3,2,0,1:T(8,128)(2,1)S(1)} collective-permute-done((bf16[4,1,128,256]{3,2,0,1:T(8,128)(2,1)S(1)}, bf16[4,1,128,256]{3,2,0,1:T(8,128)(2,1)S(1)}, u32[]{:S(2)}, u32[]{:S(2)}) %collective-permute-start.66) | collective-permute-done | bytes 262176 | tf_op jit(solution)/shard_map/ppermute | solution.py:103
  1167.1 5.9 collective-permute-start.70
  1181.2 10.6 collective-permute-done.71
  1198.0 6.2 collective-permute-start.76
  1230.5 5.7 collective-permute-done.80
  1247.8 9.8 turn_over.1
  (584 shorter events, 358.7 us)
Async XLA Ops:
  7.2 89.2 %all-gather.16.cloned.1.call-start = ((), (), s32[]{:S(2)}) async-start(), calls=%async_computation.1 | async-start | bytes 3932160 | tf_op jit(solution)/shard_map/all_gather | solution.py:82
  29.4 276.9 %all-gather.14.cloned.1.call-start = ((), (), s32[]{:S(2)}) async-start(), calls=%async_computation | async-start | bytes 10321920 | tf_op jit(solution)/shard_map/all_gather | solution.py:82
  59.5 35.1 %collective-permute-start.8 = (bf16[672,384]{1,0:T(8,128)(2,1)}, bf16[672,384]{1,0:T(8,128)(2,1)S(1)}, u32[]{:S(2)}, u32[]{:S(2)}) collective-permute-start(bf16[672,384]{1,0:T(8,128)(2,1)} %hold.16), channel_id=1, source_target_pairs={{0,16},{4,20},{8,24},{12,28},{16,0},{20,4},{24,8},{28,12},{1,17},{... | collective-permute-start | bytes 1548296 | tf_op jit(solution)/shard_map/ppermute | solution.py:43
  60.8 33.9 %collective-permute-start.9 = (bf16[672,384]{1,0:T(8,128)(2,1)}, bf16[672,384]{1,0:T(8,128)(2,1)S(1)}, u32[]{:S(2)}, u32[]{:S(2)}) collective-permute-start(bf16[672,384]{1,0:T(8,128)(2,1)} %hold.16), channel_id=1, source_target_pairs={{0,24},{4,28},{8,0},{12,4},{16,8},{20,12},{24,16},{28,20},{1,25},{... | collective-permute-start | bytes 1548296 | tf_op jit(solution)/shard_map/ppermute | solution.py:43
  96.1 210.6 %all-gather.18.cloned.1.call-start = ((), (), s32[]{:S(2)}) async-start(), calls=%async_computation.2 | async-start | bytes 2949120 | tf_op jit(solution)/shard_map/all_gather | solution.py:82
  124.1 61.9 %collective-permute-start.13 = (bf16[4,256,512]{2,1,0:T(8,128)(2,1)S(1)}, bf16[4,256,512]{2,1,0:T(8,128)(2,1)}, u32[]{:S(2)}, u32[]{:S(2)}) collective-permute-start(bf16[4,256,512]{2,1,0:T(8,128)(2,1)S(1)} %collective-permute-done.12), channel_id=1, source_target_pairs={{8,0},{12,4},{16,8},{20,12},{9,1},{13,5},{17,9},{21,13},{10,2},{14... | collective-permute-start | bytes 3145736 | tf_op jit(solution)/shard_map/ppermute | solution.py:43
  125.4 73.9 %collective-permute-start.11 = (bf16[4,256,512]{2,1,0:T(8,128)(2,1)}, bf16[4,256,512]{2,1,0:T(8,128)(2,1)}, u32[]{:S(2)}, u32[]{:S(2)}) collective-permute-start(bf16[4,256,512]{2,1,0:T(8,128)(2,1)} %get-tuple-element.106.refs_1_), channel_id=1, source_target_pairs={{16,24},{20,28},{17,25},{21,29},{18,26},{22,30},{19,27},{23,31}} | collective-permute-start | bytes 3145736 | tf_op jit(solution)/shard_map/ppermute | solution.py:43
  186.0 50.4 %collective-permute-start.14 = (bf16[4,256,512]{2,1,0:T(8,128)(2,1)}, bf16[4,256,512]{2,1,0:T(8,128)(2,1)}, u32[]{:S(2)}, u32[]{:S(2)}) collective-permute-start(bf16[4,256,512]{2,1,0:T(8,128)(2,1)} %collective-permute-done.13), channel_id=1, source_target_pairs={{8,0},{12,4},{9,1},{13,5},{10,2},{14,6},{11,3},{15,7}} | collective-permute-start | bytes 3145736 | tf_op jit(solution)/shard_map/ppermute | solution.py:43
  188.6 274.2 %all-gather.20.cloned.1.call-start = ((), (), s32[]{:S(2)}) async-start(), calls=%async_computation.3 | async-start | bytes 10321920 | tf_op jit(solution)/shard_map/all_gather | solution.py:82
  192.8 107.7 %collective-permute-start.16 = (bf16[672,384]{1,0:T(8,128)(2,1)}, bf16[672,384]{1,0:T(8,128)(2,1)}, u32[]{:S(2)}, u32[]{:S(2)}) collective-permute-start(bf16[672,384]{1,0:T(8,128)(2,1)} %hold.17), channel_id=1, source_target_pairs={{0,8},{4,12},{8,16},{12,20},{16,24},{20,28},{24,0},{28,4},{1,9},{5... | collective-permute-start | bytes 1548296 | tf_op jit(solution)/shard_map/ppermute | solution.py:43
  196.5 104.0 %collective-permute-start.17 = (bf16[672,384]{1,0:T(8,128)(2,1)}, bf16[672,384]{1,0:T(8,128)(2,1)}, u32[]{:S(2)}, u32[]{:S(2)}) collective-permute-start(bf16[672,384]{1,0:T(8,128)(2,1)} %hold.17), channel_id=1, source_target_pairs={{0,16},{4,20},{8,24},{12,28},{16,0},{20,4},{24,8},{28,12},{1,17},{... | collective-permute-start | bytes 1548296 | tf_op jit(solution)/shard_map/ppermute | solution.py:43
  196.5 104.0 %collective-permute-start.18 = (bf16[672,384]{1,0:T(8,128)(2,1)}, bf16[672,384]{1,0:T(8,128)(2,1)}, u32[]{:S(2)}, u32[]{:S(2)}) collective-permute-start(bf16[672,384]{1,0:T(8,128)(2,1)} %hold.17), channel_id=1, source_target_pairs={{0,24},{4,28},{8,0},{12,4},{16,8},{20,12},{24,16},{28,20},{1,25},{... | collective-permute-start | bytes 1548296 | tf_op jit(solution)/shard_map/ppermute | solution.py:43
  240.1 26.0 %collective-permute-start.15 = (bf16[2,4,256,512]{3,2,1,0:T(8,128)(2,1)}, bf16[2,4,256,512]{3,2,1,0:T(8,128)(2,1)}, u32[]{:S(2)}, u32[]{:S(2)}) collective-permute-start(bf16[2,4,256,512]{3,2,1,0:T(8,128)(2,1)} %pad_maximum_fusion.3.refs_2_), channel_id=1, source_target_pairs={{0,4},{4,0},{8,12},{12,8},{16,20},{20,16},{24,28},{28,24},{1,5},{5... | collective-permute-start | bytes 6291464 | tf_op jit(solution)/shard_map/ppermute | solution.py:48
  305.4 263.8 %all-gather.26.cloned.1.call-start = ((), (), s32[]{:S(2)}) async-start(), calls=%async_computation.6 | async-start | bytes 10321920 | tf_op jit(solution)/shard_map/all_gather | solution.py:82
  306.3 94.7 %collective-permute-start.19 = (bf16[4,4,672,384]{3,2,1,0:T(8,128)(2,1)}, bf16[4,4,672,384]{3,2,1,0:T(8,128)(2,1)}, u32[]{:S(2)}, u32[]{:S(2)}) collective-permute-start(bf16[4,4,672,384]{3,2,1,0:T(8,128)(2,1)} %get-tuple-element.111.own), channel_id=1, source_target_pairs={{0,4},{4,0},{8,12},{12,8},{16,20},{20,16},{24,28},{28,24},{1,5},{5... | collective-permute-start | bytes 24772616 | tf_op jit(solution)/shard_map/ppermute | solution.py:48
  343.8 37.6 %collective-permute-start.22 = (bf16[672,384]{1,0:T(8,128)(2,1)S(1)}, bf16[672,384]{1,0:T(8,128)(2,1)S(1)}, u32[]{:S(2)}, u32[]{:S(2)}) collective-permute-start(bf16[672,384]{1,0:T(8,128)(2,1)S(1)} %copy-done.12), channel_id=1, source_target_pairs={{0,16},{4,20},{8,24},{12,28},{16,0},{20,4},{24,8},{28,12},{1,17},{... | collective-permute-start | bytes 1548296 | tf_op jit(solution)/shard_map/ppermute | solution.py:43
  343.9 37.6 %collective-permute-start.23 = (bf16[672,384]{1,0:T(8,128)(2,1)S(1)}, bf16[672,384]{1,0:T(8,128)(2,1)}, u32[]{:S(2)}, u32[]{:S(2)}) collective-permute-start(bf16[672,384]{1,0:T(8,128)(2,1)S(1)} %copy-done.12), channel_id=1, source_target_pairs={{0,24},{4,28},{8,0},{12,4},{16,8},{20,12},{24,16},{28,20},{1,25},{... | collective-permute-start | bytes 1548296 | tf_op jit(solution)/shard_map/ppermute | solution.py:43
  387.0 273.9 %all-gather.24.cloned.1.call-start = ((), (), s32[]{:S(2)}) async-start(), calls=%async_computation.5 | async-start | bytes 10321920 | tf_op jit(solution)/shard_map/all_gather | solution.py:82
  388.0 70.5 %collective-permute-start.27 = (bf16[672,384]{1,0:T(8,128)(2,1)}, bf16[672,384]{1,0:T(8,128)(2,1)S(1)}, u32[]{:S(2)}, u32[]{:S(2)}) collective-permute-start(bf16[672,384]{1,0:T(8,128)(2,1)} %get-tuple-element.124), channel_id=1, source_target_pairs={{0,8},{4,12},{8,16},{12,20},{16,24},{20,28},{24,0},{28,4},{1,9},{5... | collective-permute-start | bytes 1548296 | tf_op jit(solution)/shard_map/ppermute | solution.py:43
  398.3 60.1 %collective-permute-start.28 = (bf16[672,384]{1,0:T(8,128)(2,1)}, bf16[672,384]{1,0:T(8,128)(2,1)S(1)}, u32[]{:S(2)}, u32[]{:S(2)}) collective-permute-start(bf16[672,384]{1,0:T(8,128)(2,1)} %get-tuple-element.124), channel_id=1, source_target_pairs={{0,16},{4,20},{8,24},{12,28},{16,0},{20,4},{24,8},{28,12},{1,17},{... | collective-permute-start | bytes 1548296 | tf_op jit(solution)/shard_map/ppermute | solution.py:43
  398.3 60.2 %collective-permute-start.29 = (bf16[672,384]{1,0:T(8,128)(2,1)}, bf16[672,384]{1,0:T(8,128)(2,1)}, u32[]{:S(2)}, u32[]{:S(2)}) collective-permute-start(bf16[672,384]{1,0:T(8,128)(2,1)} %get-tuple-element.124), channel_id=1, source_target_pairs={{0,24},{4,28},{8,0},{12,4},{16,8},{20,12},{24,16},{28,20},{1,25},{... | collective-permute-start | bytes 1548296 | tf_op jit(solution)/shard_map/ppermute | solution.py:43
  464.1 44.2 %collective-permute-start.30 = (bf16[4,4,672,384]{3,2,1,0:T(8,128)(2,1)}, bf16[4,4,672,384]{3,2,1,0:T(8,128)(2,1)}, u32[]{:S(2)}, u32[]{:S(2)}) collective-permute-start(bf16[4,4,672,384]{3,2,1,0:T(8,128)(2,1)} %hold.24.own), channel_id=1, source_target_pairs={{0,4},{4,0},{8,12},{12,8},{16,20},{20,16},{24,28},{28,24},{1,5},{5... | collective-permute-start | bytes 24772616 | tf_op jit(solution)/shard_map/ppermute | solution.py:48
  470.7 94.1 %collective-permute-start.24 = (bf16[672,384]{1,0:T(8,128)(2,1)}, bf16[672,384]{1,0:T(8,128)(2,1)S(1)}, u32[]{:S(2)}, u32[]{:S(2)}) collective-permute-start(bf16[672,384]{1,0:T(8,128)(2,1)} %hold.22), channel_id=1, source_target_pairs={{0,8},{4,12},{8,16},{12,20},{16,24},{20,28},{24,0},{28,4},{1,9},{5... | collective-permute-start | bytes 1548296 | tf_op jit(solution)/shard_map/ppermute | solution.py:43
  470.8 279.7 %all-gather.22.cloned.1.call-start = ((), (), s32[]{:S(2)}) async-start(), calls=%async_computation.4 | async-start | bytes 10321920 | tf_op jit(solution)/shard_map/all_gather | solution.py:82
  481.3 26.2 %collective-permute-start.34 = (bf16[672,128]{1,0:T(8,128)(2,1)S(1)}, bf16[672,128]{1,0:T(8,128)(2,1)S(1)}, u32[]{:S(2)}, u32[]{:S(2)}) collective-permute-start(bf16[672,128]{1,0:T(8,128)(2,1)S(1)} %get-tuple-element.280), channel_id=1, source_target_pairs={{0,24},{4,28},{8,0},{12,4},{16,8},{20,12},{24,16},{28,20},{1,25},{... | collective-permute-start | bytes 516104 | tf_op jit(solution)/shard_map/ppermute | solution.py:43
  491.1 73.7 %collective-permute-start.25 = (bf16[672,384]{1,0:T(8,128)(2,1)S(1)}, bf16[672,384]{1,0:T(8,128)(2,1)S(1)}, u32[]{:S(2)}, u32[]{:S(2)}) collective-permute-start(bf16[672,384]{1,0:T(8,128)(2,1)S(1)} %copy-done.14), channel_id=1, source_target_pairs={{0,16},{4,20},{8,24},{12,28},{16,0},{20,4},{24,8},{28,12},{1,17},{... | collective-permute-start | bytes 1548296 | tf_op jit(solution)/shard_map/ppermute | solution.py:43
  503.0 61.9 %collective-permute-start.26 = (bf16[672,384]{1,0:T(8,128)(2,1)S(1)}, bf16[672,384]{1,0:T(8,128)(2,1)}, u32[]{:S(2)}, u32[]{:S(2)}) collective-permute-start(bf16[672,384]{1,0:T(8,128)(2,1)S(1)} %copy-done.14), channel_id=1, source_target_pairs={{0,24},{4,28},{8,0},{12,4},{16,8},{20,12},{24,16},{28,20},{1,25},{... | collective-permute-start | bytes 1548296 | tf_op jit(solution)/shard_map/ppermute | solution.py:43
  570.6 32.2 %collective-permute-start.35 = (bf16[4,4,672,384]{3,2,1,0:T(8,128)(2,1)}, bf16[4,4,672,384]{3,2,1,0:T(8,128)(2,1)}, u32[]{:S(2)}, u32[]{:S(2)}) collective-permute-start(bf16[4,4,672,384]{3,2,1,0:T(8,128)(2,1)} %hold.26.own), channel_id=1, source_target_pairs={{0,4},{4,0},{8,12},{12,8},{16,20},{20,16},{24,28},{28,24},{1,5},{5... | collective-permute-start | bytes 24772616 | tf_op jit(solution)/shard_map/ppermute | solution.py:48
  661.0 33.1 %collective-permute-start.40 = (bf16[4,4,672,384]{3,2,1,0:T(8,128)(2,1)}, bf16[4,4,672,384]{3,2,1,0:T(8,128)(2,1)}, u32[]{:S(2)}, u32[]{:S(2)}) collective-permute-start(bf16[4,4,672,384]{3,2,1,0:T(8,128)(2,1)} %hold.27.own), channel_id=1, source_target_pairs={{0,4},{4,0},{8,12},{12,8},{16,20},{20,16},{24,28},{28,24},{1,5},{5... | collective-permute-start | bytes 24772616 | tf_op jit(solution)/shard_map/ppermute | solution.py:48
  750.5 31.6 %collective-permute-start.45 = (bf16[4,4,672,384]{3,2,1,0:T(8,128)(2,1)}, bf16[4,4,672,384]{3,2,1,0:T(8,128)(2,1)}, u32[]{:S(2)}, u32[]{:S(2)}) collective-permute-start(bf16[4,4,672,384]{3,2,1,0:T(8,128)(2,1)} %hold.28.own), channel_id=1, source_target_pairs={{0,4},{4,0},{8,12},{12,8},{16,20},{20,16},{24,28},{28,24},{1,5},{5... | collective-permute-start | bytes 24772616 | tf_op jit(solution)/shard_map/ppermute | solution.py:48
  840.9 94.6 %collective-permute-start.97 = (bf16[4,672,128]{2,1,0:T(8,128)(2,1)}, bf16[4,672,128]{2,1,0:T(8,128)(2,1)S(1)}, u32[]{:S(2)}, u32[]{:S(2)}) collective-permute-start(bf16[4,672,128]{2,1,0:T(8,128)(2,1)} %dynamic-slice_bitcast_fusion.7), channel_id=1, source_target_pairs={{0,4},{4,0},{8,12},{12,8},{16,20},{20,16},{24,28},{28,24},{1,5},{5... | collective-permute-start | bytes 2064392 | tf_op jit(solution)/shard_map/ppermute | solution.py:48
  873.2 92.3 %collective-permute-start.83 = (bf16[4,4,1,128,256]{4,3,1,2,0:T(8,128)(2,1)S(1)}, bf16[4,4,1,128,256]{4,3,1,2,0:T(8,128)(2,1)}, u32[]{:S(2)}, u32[]{:S(2)}) collective-permute-start(bf16[4,4,1,128,256]{4,3,1,2,0:T(8,128)(2,1)S(1)} %dynamic-slice_bitcast_fusion), channel_id=1, source_target_pairs={{0,4},{4,0},{8,12},{12,8},{16,20},{20,16},{24,28},{28,24},{1,5},{5... | collective-permute-start | bytes 3145736 | tf_op jit(solution)/shard_map/ppermute | solution.py:48
  935.4 106.0 %collective-permute-start.50 = (bf16[2,4,256,512]{3,2,1,0:T(8,128)(2,1)}, bf16[2,4,256,512]{3,2,1,0:T(8,128)(2,1)}, u32[]{:S(2)}, u32[]{:S(2)}) collective-permute-start(bf16[2,4,256,512]{3,2,1,0:T(8,128)(2,1)} %get-tuple-element.166), channel_id=1, source_target_pairs={{0,4},{4,0},{8,12},{12,8},{16,20},{20,16},{24,28},{28,24},{1,5},{5... | collective-permute-start | bytes 6291464 | tf_op jit(solution)/shard_map/ppermute | solution.py:48
  935.8 25.2 %collective-permute-start.100 = (bf16[672,128]{1,0:T(8,128)(2,1)S(1)}, bf16[672,128]{1,0:T(8,128)(2,1)S(1)}, u32[]{:S(2)}, u32[]{:S(2)}) collective-permute-start(bf16[672,128]{1,0:T(8,128)(2,1)S(1)} %get-tuple-element.268), channel_id=1, source_target_pairs={{0,24},{4,28},{8,0},{12,4},{16,8},{20,12},{24,16},{28,20},{1,25},{... | collective-permute-start | bytes 516104 | tf_op jit(solution)/shard_map/ppermute | solution.py:43
  970.2 51.2 %collective-permute-start.84 = (bf16[4,1,128,256]{3,2,1,0:T(8,128)(2,1)S(1)}, bf16[4,1,128,256]{3,2,1,0:T(8,128)(2,1)S(1)}, u32[]{:S(2)}, u32[]{:S(2)}) collective-permute-start(bf16[4,1,128,256]{3,2,1,0:T(8,128)(2,1)S(1)} %get-tuple-element.238), channel_id=1, source_target_pairs={{0,8},{4,12},{8,16},{12,20},{16,24},{20,28},{24,0},{28,4},{1,9},{5... | collective-permute-start | bytes 786440 | tf_op jit(solution)/shard_map/ppermute | solution.py:43
  976.1 48.0 %collective-permute-start.85 = (bf16[4,1,128,256]{3,2,1,0:T(8,128)(2,1)S(1)}, bf16[4,1,128,256]{3,2,1,0:T(8,128)(2,1)S(1)}, u32[]{:S(2)}, u32[]{:S(2)}) collective-permute-start(bf16[4,1,128,256]{3,2,1,0:T(8,128)(2,1)S(1)} %get-tuple-element.240), channel_id=1, source_target_pairs={{0,16},{4,20},{8,24},{12,28},{16,0},{20,4},{24,8},{28,12},{1,17},{... | collective-permute-start | bytes 786440 | tf_op jit(solution)/shard_map/ppermute | solution.py:43
  978.0 47.4 %collective-permute-start.86 = (bf16[4,1,128,256]{3,2,1,0:T(8,128)(2,1)S(1)}, bf16[4,1,128,256]{3,2,1,0:T(8,128)(2,1)S(1)}, u32[]{:S(2)}, u32[]{:S(2)}) collective-permute-start(bf16[4,1,128,256]{3,2,1,0:T(8,128)(2,1)S(1)} %get-tuple-element.239), channel_id=1, source_target_pairs={{0,24},{4,28},{8,0},{12,4},{16,8},{20,12},{24,16},{28,20},{1,25},{... | collective-permute-start | bytes 786440 | tf_op jit(solution)/shard_map/ppermute | solution.py:43
  1025.3 136.7 %collective-permute-start.107 = (bf16[4,840,128]{2,1,0:T(8,128)(2,1)}, bf16[4,840,128]{2,1,0:T(8,128)(2,1)}, u32[]{:S(2)}, u32[]{:S(2)}) collective-permute-start(bf16[4,840,128]{2,1,0:T(8,128)(2,1)} %bitcast_dynamic-update-slice_fusion.36), channel_id=1, source_target_pairs={{0,1},{1,0},{2,3},{3,2},{4,5},{5,4},{6,7},{7,6},{8,9},{9,8},{10,11... | collective-permute-start | bytes 2580488 | tf_op jit(solution)/shard_map/ppermute | solution.py:103
  1050.0 36.5 %collective-permute-start.51 = (bf16[4,256,512]{2,1,0:T(8,128)(2,1)S(1)}, bf16[4,256,512]{2,1,0:T(8,128)(2,1)S(1)}, u32[]{:S(2)}, u32[]{:S(2)}) collective-permute-start(bf16[4,256,512]{2,1,0:T(8,128)(2,1)S(1)} %get-tuple-element.237), channel_id=1, source_target_pairs={{0,8},{4,12},{1,9},{5,13},{2,10},{6,14},{3,11},{7,15}} | collective-permute-start | bytes 3145736 | tf_op jit(solution)/shard_map/ppermute | solution.py:43
  1055.1 24.8 %collective-permute-start.90 = (bf16[1,128,256]{2,1,0:T(8,128)(2,1)S(1)}, bf16[1,128,256]{2,1,0:T(8,128)(2,1)S(1)}, u32[]{:S(2)}, u32[]{:S(2)}) collective-permute-start(bf16[1,128,256]{2,1,0:T(8,128)(2,1)S(1)} %get-tuple-element.195), channel_id=1, source_target_pairs={{0,8},{4,12},{8,16},{12,20},{16,24},{20,28},{24,0},{28,4},{1,9},{5... | collective-permute-start | bytes 196616 | tf_op jit(solution)/shard_map/ppermute | solution.py:43
  1055.1 27.3 %collective-permute-start.91 = (bf16[1,128,256]{2,1,0:T(8,128)(2,1)S(1)}, bf16[1,128,256]{2,1,0:T(8,128)(2,1)S(1)}, u32[]{:S(2)}, u32[]{:S(2)}) collective-permute-start(bf16[1,128,256]{2,1,0:T(8,128)(2,1)S(1)} %get-tuple-element.195), channel_id=1, source_target_pairs={{0,16},{4,20},{8,24},{12,28},{16,0},{20,4},{24,8},{28,12},{1,17},{... | collective-permute-start | bytes 196616 | tf_op jit(solution)/shard_map/ppermute | solution.py:43
  1055.2 29.1 %collective-permute-start.92 = (bf16[1,128,256]{2,1,0:T(8,128)(2,1)S(1)}, bf16[1,128,256]{2,1,0:T(8,128)(2,1)S(1)}, u32[]{:S(2)}, u32[]{:S(2)}) collective-permute-start(bf16[1,128,256]{2,1,0:T(8,128)(2,1)S(1)} %get-tuple-element.195), channel_id=1, source_target_pairs={{0,24},{4,28},{8,0},{12,4},{16,8},{20,12},{24,16},{28,20},{1,25},{... | collective-permute-start | bytes 196616 | tf_op jit(solution)/shard_map/ppermute | solution.py:43
  1113.5 49.9 %collective-permute-start.108 = (bf16[4,840,128]{2,1,0:T(8,128)(2,1)}, bf16[4,840,128]{2,1,0:T(8,128)(2,1)}, u32[]{:S(2)}, u32[]{:S(2)}) collective-permute-start(bf16[4,840,128]{2,1,0:T(8,128)(2,1)} %bitcast_dynamic-update-slice_fusion.36), channel_id=1, source_target_pairs={{0,2},{1,3},{2,0},{3,1},{4,6},{5,7},{6,4},{7,5},{8,10},{9,11},{10,... | collective-permute-start | bytes 2580488 | tf_op jit(solution)/shard_map/ppermute | solution.py:103
  1121.3 43.5 %collective-permute-start.109 = (bf16[4,840,128]{2,1,0:T(8,128)(2,1)}, bf16[4,840,128]{2,1,0:T(8,128)(2,1)}, u32[]{:S(2)}, u32[]{:S(2)}) collective-permute-start(bf16[4,840,128]{2,1,0:T(8,128)(2,1)} %bitcast_dynamic-update-slice_fusion.36), channel_id=1, source_target_pairs={{0,3},{1,2},{2,1},{3,0},{4,7},{5,6},{6,5},{7,4},{8,11},{9,10},{10,... | collective-permute-start | bytes 2580488 | tf_op jit(solution)/shard_map/ppermute | solution.py:103
  1122.4 38.0 %collective-permute-start.66 = (bf16[4,1,128,256]{3,2,0,1:T(8,128)(2,1)S(1)}, bf16[4,1,128,256]{3,2,0,1:T(8,128)(2,1)S(1)}, u32[]{:S(2)}, u32[]{:S(2)}) collective-permute-start(bf16[4,1,128,256]{3,2,0,1:T(8,128)(2,1)S(1)} %bitcast_dynamic-update-slice_fusion.59), channel_id=1, source_target_pairs={{0,2},{1,3},{2,0},{3,1},{4,6},{5,7},{6,4},{7,5},{8,10},{9,11},{10,... | collective-permute-start | bytes 786440 | tf_op jit(solution)/shard_map/ppermute | solution.py:103
  1125.4 35.1 %collective-permute-start.67 = (bf16[4,1,128,256]{3,2,0,1:T(8,128)(2,1)S(1)}, bf16[4,1,128,256]{3,2,0,1:T(8,128)(2,1)}, u32[]{:S(2)}, u32[]{:S(2)}) collective-permute-start(bf16[4,1,128,256]{3,2,0,1:T(8,128)(2,1)S(1)} %bitcast_dynamic-update-slice_fusion.59), channel_id=1, source_target_pairs={{0,3},{1,2},{2,1},{3,0},{4,7},{5,6},{6,5},{7,4},{8,11},{9,10},{10,... | collective-permute-start | bytes 786440 | tf_op jit(solution)/shard_map/ppermute | solution.py:103
  1162.0 33.5 %collective-permute-start.68 = (bf16[4,4,1,128,256]{4,3,0,1,2:T(8,128)(2,1)S(1)}, bf16[4,4,1,128,256]{4,3,0,1,2:T(8,128)(2,1)S(1)}, u32[]{:S(2)}, u32[]{:S(2)}) collective-permute-start(bf16[4,4,1,128,256]{4,3,0,1,2:T(8,128)(2,1)S(1)} %bitcast_dynamic-update-slice_fusion.31), channel_id=1, source_target_pairs={{0,4},{4,0},{8,12},{12,8},{16,20},{20,16},{24,28},{28,24},{1,5},{5... | collective-permute-start | bytes 3145736 | tf_op jit(solution)/shard_map/ppermute | solution.py:48
  1166.1 71.6 %collective-permute-start.110 = (bf16[4,4,840,128]{3,2,0,1:T(8,128)(2,1)S(1)}, bf16[4,4,840,128]{3,2,0,1:T(8,128)(2,1)}, u32[]{:S(2)}, u32[]{:S(2)}) collective-permute-start(bf16[4,4,840,128]{3,2,0,1:T(8,128)(2,1)S(1)} %bitcast_dynamic-update-slice_fusion.3), channel_id=1, source_target_pairs={{0,4},{4,0},{8,12},{12,8},{16,20},{20,16},{24,28},{28,24},{1,5},{5... | collective-permute-start | bytes 10321928 | tf_op jit(solution)/shard_map/ppermute | solution.py:48
  (141 other events, 1639.5 us)
Sparse Core Ops, SparseCore 0:
  29.5 47.3 all-gather.15
  96.3 96.8 all-gather.13
  195.5 37.4 all-gather.17
  305.6 84.7 all-gather.19
  392.6 89.1 all-gather.25
  483.5 86.5 all-gather.23
  595.6 87.3 all-gather.21

commit v2 on v1

v2 whole, which is shorter than its diff:
```python
import functools
import math

import jax
import jax.numpy as jnp
from jax import lax
from jax.experimental import pallas as pl
from jax.experimental.pallas import tpu as pltpu
from jax.sharding import PartitionSpec as P

HEAD_DIM = 128
PROMPT = 1024
CONTS = 4
CONT = 256
RANK = 16

norm_eps = 1e-06
adapter_scale = 0.5
rope_base = 1000000.0
masked_score = -1e30
score_scale = HEAD_DIM ** (-0.5)
score_to_log2 = score_scale * math.log2(math.e)

f32 = jnp.float32
bf16 = jnp.bfloat16
VMEM_LIMIT = 60 * 2**20


def nt(left, right):
    return lax.dot_general(left, right, (((1,), (1,)), ((), ())), preferred_element_type=f32)


def nn(left, right):
    return lax.dot_general(left, right, (((1,), (0,)), ((), ())), preferred_element_type=f32)


def tn(left, right):
    return lax.dot_general(left, right, (((0,), (0,)), ((), ())), preferred_element_type=f32)


def along_line(array, pairs):
    return lax.ppermute(array, "ctx", [(2 * a + c, 2 * b + c) for a, b in pairs for c in (0, 1)])


def swap_cores(array):
    size = lax.axis_size("ctx")
    return lax.ppermute(array, "ctx", [(i, i ^ 1) for i in range(size)])


def hold_kernel(*refs):
    pass


def hold(arrays, *after):
    anywhere = pl.BlockSpec(memory_space=pl.ANY)
    count = len(arrays)
    held = pl.pallas_call(
        hold_kernel,
        in_specs=[anywhere] * (count + len(after)),
        out_specs=[anywhere] * count,
        out_shape=[jax.ShapeDtypeStruct(a.shape, a.dtype) for a in arrays],
        input_output_aliases={i: i for i in range(count)},
        name="hold",
    )(*arrays, *after)
    return list(held)


def line_moves(piece, line):
    return [
        along_line(piece, [(i, (i + by) % line) for i in range(line)]) for by in range(1, line)
    ]


def in_order(piece, came, place, line):
    out = jnp.zeros((line,) + piece.shape, piece.dtype)
    out = lax.dynamic_update_index_in_dim(out, piece, place, 0)
    for by in range(1, line):
        out = lax.dynamic_update_index_in_dim(out, came[by - 1], (place - by) % line, 0)
    return out


def shard_gather(lined):
    return lax.all_gather(lined, "wsh", axis=0, tiled=False)


def add_up(arrays):
    return functools.reduce(jnp.add, [a.astype(f32) for a in arrays]).astype(bf16)


def line_outs(mine, place, line):
    return [
        lax.dynamic_index_in_dim(mine, (place + by) % line, 0, False) for by in range(1, line)
    ]


def line_send(outs, line):
    return [
        along_line(out, [(i, (i + by + 1) % line) for i in range(line)]) for by, out in enumerate(outs)
    ]


def line_sum(mine, place, came):
    return add_up([lax.dynamic_index_in_dim(mine, place, 0, False)] + came)


def across(array, by):
    size = lax.axis_size("wsh")
    return lax.ppermute(array, "wsh", [(i, i ^ by) for i in range(size)])


def wsh_outs(parts, shard):
    return [
        lax.dynamic_index_in_dim(parts, shard ^ by, 1, False) for by in range(1, parts.shape[1])
    ]


def wsh_send(outs):
    return [across(out, by + 1) for by, out in enumerate(outs)]


def wsh_sum(parts, shard, came):
    return add_up([lax.dynamic_index_in_dim(parts, shard, 1, False)] + came)


def tip(array):
    ends = (1,) * (array.ndim - 2) + (min(16, array.shape[-2]), min(128, array.shape[-1]))
    return lax.slice(array, (0,) * array.ndim, ends)


def gather_wsh(piece, shard, after=()):
    shards = lax.axis_size("wsh")
    came = [across(piece, by) for by in range(1, shards)]
    came = hold(came, *after) if after else came
    out = jnp.zeros((shards,) + piece.shape, piece.dtype)
    out = lax.dynamic_update_index_in_dim(out, piece, shard, 0)
    for by in range(1, shards):
        out = lax.dynamic_update_index_in_dim(out, came[by - 1], shard ^ by, 0)
    return out


def both_cores(half, other, core):
    return jnp.stack([jnp.where(core == 0, half, other), jnp.where(core == 0, other, half)])


def params(**more):
    return pltpu.CompilerParams(
        dimension_semantics=("arbitrary",), vmem_limit_bytes=VMEM_LIMIT, **more
    )


def whole(array):
    return pl.BlockSpec(array.shape, lambda s, *pre: (0,) * array.ndim)


def by_slot(array):
    return pl.BlockSpec((1,) + array.shape[1:], lambda s, *pre: (s,) + (0,) * (array.ndim - 1))


def second_by_slot(array):
    return pl.BlockSpec(
        (array.shape[0], 1) + array.shape[2:], lambda s, *pre: (0, s) + (0,) * (array.ndim - 2)
    )


def half_copies(core, own, other, parts, sems):
    copies = []
    shards, _, _, cols = own.shape
    for side, half in ((core, own), (1 - core, other)):
        for w in range(shards):
            for at, count, buffer in parts:
                copies.append(
                    pltpu.make_async_copy(
                        half.at[w, :, pl.ds(at, count), :],
                        buffer.at[:, side, :, pl.ds(w * cols, cols)],
                        sems.at[len(copies)],
                    )
                )
    return copies


def fetch_once(copies):
    @pl.when(pl.program_id(0) == 0)
    def _():
        for c in copies:
            c.start()
        for c in copies:
            c.wait()


def buffers(own, rows, width):
    line, shards = own.shape[1], own.shape[0]
    held = [pltpu.VMEM((line, 2, n, width), bf16) for n in rows]
    return held + [pltpu.SemaphoreType.DMA((2 * shards * len(rows),))]


def as_matrix(buffer):
    return buffer[...].reshape(-1, buffer.shape[-1])


anywhere = pl.BlockSpec(memory_space=pl.ANY)


def cost(flops, bytes_accessed, exps=0):
    return pl.CostEstimate(flops=int(flops), bytes_accessed=int(bytes_accessed), transcendentals=int(exps))


def slot_lanes(adapter, block, ranks):
    lane = lax.broadcasted_iota(jnp.int32, (block, ranks), 1)
    return lane // RANK == adapter[pl.program_id(0)]


def picked(mask, values):
    return jnp.where(mask, values, 0.0).astype(bf16)


def struct(shape, dtype):
    return jax.ShapeDtypeStruct(shape, dtype)


def turn(u, cos, sin):
    return u * cos + pltpu.roll(u, HEAD_DIM // 2, 1) * sin


def turn_back(u, cos, sin):
    return u * cos - pltpu.roll(u, HEAD_DIM // 2, 1) * sin


def key_value_kernel(
    first, adapter, core, own, other, tok, gain, bias, in_k, in_v, out_k, out_v, cosine, sine,
    normed_ref, rank_k_ref, rank_v_ref, kv_ref, key_w, value_w, sems,
):
    rows = key_w.shape[2]
    parts = ((first, rows, key_w), (first + rows, rows, value_w))
    fetch_once(half_copies(core[0], own, other, parts, sems))
    hidden = tok[0].astype(f32)
    inverse = lax.rsqrt(jnp.mean(hidden * hidden, axis=-1, keepdims=True) + norm_eps)
    normed = (hidden * inverse * gain[...]).astype(bf16)
    normed_ref[0] = normed
    mask = slot_lanes(adapter, normed.shape[0], in_k.shape[0])
    kv_width = kv_ref.shape[-1] // 2
    rank_k = picked(mask, nt(normed, in_k[...]))
    rank_v = picked(mask, nt(normed, in_v[...]))
    rank_k_ref[0], rank_v_ref[0] = rank_k, rank_v
    lin_k = nt(normed, as_matrix(key_w)) + bias[:, :kv_width]
    lin_v = nt(normed, as_matrix(value_w)) + bias[:, kv_width:]
    key = lin_k + adapter_scale * nn(rank_k, out_k[...])
    value = lin_v + adapter_scale * nn(rank_v, out_v[...])
    cos, sin = cosine[...], sine[...]
    for h in range(kv_width // HEAD_DIM):
        part = slice(h * HEAD_DIM, (h + 1) * HEAD_DIM)
        kv_ref[0, :, part] = turn(key[:, part], cos, sin).astype(bf16)
    kv_ref[0, :, kv_width:] = value.astype(bf16)


def key_value_side(adapter_of, core, own, other, first, tokens, gain, bias, adapters, cosine, sine):
    slots, block, width = tokens.shape
    kv_rows = bias.shape[1] // 4 // own.shape[1]
    shared = (gain, bias, *adapters, cosine, sine)
    ranks = struct((slots, block, adapters[0].shape[0]), bf16)
    outs = (struct(tokens.shape, bf16), ranks, ranks, struct((slots, block, bias.shape[1]), bf16))
    return pl.pallas_call(
        functools.partial(key_value_kernel, first),
        grid_spec=pltpu.PrefetchScalarGridSpec(
            num_scalar_prefetch=2,
            grid=(slots,),
            in_specs=[anywhere, anywhere, by_slot(tokens)] + [whole(a) for a in shared],
            out_specs=[by_slot(o) for o in outs],
            scratch_shapes=buffers(own, (kv_rows, kv_rows), width),
        ),
        out_shape=outs,
        compiler_params=params(),
        cost_estimate=cost(3 * slots * block * width * bias.shape[1], 12e6),
        name="key_value_side",
    )(adapter_of, core, own, other, tokens, *shared)


def query_kernel(
    adapter, core, own, other, normed, bias, in_q, out_q, cosine, sine, rank_ref, query_ref, weight, sems
):
    fetch_once(half_copies(core[0], own, other, ((0, weight.shape[2], weight),), sems))
    x = normed[0]
    mask = slot_lanes(adapter, x.shape[0], in_q.shape[0])
    rank = picked(mask, nt(x, in_q[...]))
    rank_ref[0] = rank
    query = nt(x, as_matrix(weight)) + bias[...] + adapter_scale * nn(rank, out_q[...])
    cos, sin = cosine[...], sine[...]
    for h in range(query.shape[1] // HEAD_DIM):
        part = slice(h * HEAD_DIM, (h + 1) * HEAD_DIM)
        query_ref[0, :, part] = turn(query[:, part], cos, sin).astype(bf16)


def query_side(adapter_of, core, own, other, normed, bias, adapters, cosine, sine):
    slots, block, width = normed.shape
    shared = (bias, *adapters, cosine, sine)
    outs = (struct((slots, block, adapters[0].shape[0]), bf16), struct(normed.shape, bf16))
    return pl.pallas_call(
        query_kernel,
        grid_spec=pltpu.PrefetchScalarGridSpec(
            num_scalar_prefetch=2,
            grid=(slots,),
            in_specs=[anywhere, anywhere, by_slot(normed)] + [whole(a) for a in shared],
            out_specs=[by_slot(o) for o in outs],
            scratch_shapes=buffers(own, (width // 2 // own.shape[1],), width),
        ),
        out_shape=outs,
        compiler_params=params(),
        cost_estimate=cost(2.5 * slots * block * width * width, 12e6),
        name="query_side",
    )(adapter_of, core, own, other, normed, *shared)


def attend_kernel(kv_heads, group, mates, flags, *refs):
    query, own, even, odd = refs[:4]
    mate = refs[4] if mates else None
    context_ref, mixed_ref, log_ref = refs[4 + mates :]
    block = query.shape[1]
    half = even.shape[0]
    kv_width = kv_heads * HEAD_DIM
    rows = lax.broadcasted_iota(jnp.int32, (block, block), 0)
    cols = lax.broadcasted_iota(jnp.int32, (block, block), 1)
    causal = rows <= cols
    bias = [jnp.where(flags[i] != 0, 0.0, masked_score) for i in range(2 * half + mates)]
    for kv in range(kv_heads):
        k_part = slice(kv * HEAD_DIM, (kv + 1) * HEAD_DIM)
        v_part = slice(kv_width + kv * HEAD_DIM, kv_width + (kv + 1) * HEAD_DIM)
        sources = [own[0]] + [even[i, 0] for i in range(half)] + [odd[i, 0] for i in range(half)]
        sources += [mate[0]] if mates else []
        keys = [s[:, k_part] for s in sources]
        values_t = [s[:, v_part].T for s in sources]
        for g in range(group):
            h = kv * group + g
            part = slice(h * HEAD_DIM, (h + 1) * HEAD_DIM)
            q = query[0, :, part]
            scores = [nt(k, q) for k in keys]
            scores[0] = jnp.where(causal, scores[0], masked_score)
            scores = scores[:1] + [s + b for s, b in zip(scores[1:], bias)]
            top = functools.reduce(jnp.maximum, [jnp.max(s, axis=0, keepdims=True) for s in scores])
            shift = top * score_to_log2
            total, mixed = 0.0, 0.0
            for s, v in zip(scores, values_t):
                p = jnp.exp2(s * score_to_log2 - shift)
                total = total + jnp.sum(p, axis=0, keepdims=True)
                mixed = mixed + nn(v, p.astype(bf16))
            mixed = mixed / total
            mixed_ref[0, h] = mixed
            log_ref[0, h : h + 1, :] = shift + jnp.log2(total)
            context_ref[0, :, part] = mixed.T.astype(bf16)


def attend(flags, query, own, even, odd, mate, kv_heads):
    slots, block, width = query.shape
    heads = width // HEAD_DIM
    mates = len(mate)
    operands = (query, own, even, odd, *mate)
    specs = [by_slot(query), by_slot(own), second_by_slot(even), second_by_slot(odd)]
    specs += [by_slot(m) for m in mate]
    outs = (
        struct((slots, block, width), bf16),
        struct((slots, heads, HEAD_DIM, block), f32),
        struct((slots, heads, block), f32),
    )
    return pl.pallas_call(
        functools.partial(attend_kernel, kv_heads, heads // kv_heads, mates),
        grid_spec=pltpu.PrefetchScalarGridSpec(
            num_scalar_prefetch=1, grid=(slots,), in_specs=specs, out_specs=[by_slot(o) for o in outs]
        ),
        out_shape=outs,
        compiler_params=params(),
        cost_estimate=cost(20e9, 20e6, slots * heads * block * (own.shape[1] * 5)),
        name="attend",
    )(flags, *operands)


def attend_back_kernel(kv_heads, group, mates, more, flags, *refs):
    refs = refs[more:]
    query, own, even, odd = refs[:4]
    mate = refs[4] if mates else None
    grad, mixed_ref, log_ref, cosine, sine = refs[4 + mates : 9 + mates]
    d_query, d_own, d_even, d_odd = refs[9 + mates : 13 + mates]
    d_mate = refs[13 + mates] if mates else None
    acc = refs[13 + 2 * mates]
    block = query.shape[1]
    half = even.shape[0]
    kv_width = kv_heads * HEAD_DIM
    rows = lax.broadcasted_iota(jnp.int32, (block, block), 0)
    cols = lax.broadcasted_iota(jnp.int32, (block, block), 1)
    causal = rows <= cols
    bias = [jnp.where(flags[i] != 0, 0.0, masked_score) for i in range(2 * half + mates)]
    cos, sin = cosine[...], sine[...]
    for kv in range(kv_heads):
        k_part = slice(kv * HEAD_DIM, (kv + 1) * HEAD_DIM)
        v_part = slice(kv_width + kv * HEAD_DIM, kv_width + (kv + 1) * HEAD_DIM)
        sources = [own[0]] + [even[i, 0] for i in range(half)] + [odd[i, 0] for i in range(half)]
        sources += [mate[0]] if mates else []
        keys = [s[:, k_part] for s in sources]
        keys_t = [k.T for k in keys]
        values = [s[:, v_part] for s in sources]
        for g in range(group):
            h = kv * group + g
            part = slice(h * HEAD_DIM, (h + 1) * HEAD_DIM)
            q = query[0, :, part]
            d_o = grad[0, :, part]
            delta = jnp.sum(d_o.astype(f32).T * mixed_ref[0, h], axis=0, keepdims=True)
            shift = log_ref[0, h : h + 1, :]
            d_q = 0.0
            for i in range(len(sources)):
                s = nt(keys[i], q)
                s = jnp.where(causal, s, masked_score) if i == 0 else s + bias[i - 1]
                p = jnp.exp2(s * score_to_log2 - shift)
                d_p = nt(values[i], d_o)
                d_s = (p * (d_p - delta)).astype(bf16)
                d_value = nn(p.astype(bf16), d_o)
                d_key = nn(d_s, q)
                if g == 0:
                    acc[i, :, v_part] = d_value
                    acc[i, :, k_part] = d_key
                else:
                    acc[i, :, v_part] += d_value
                    acc[i, :, k_part] += d_key
                d_q = d_q + nn(keys_t[i], d_s)
            u = d_q.T * score_scale
            d_query[0, :, part] = (u * cos - pltpu.roll(u, HEAD_DIM // 2, 1) * sin).astype(bf16)
    targets = [(d_own, 0)] + [(d_even, i) for i in range(half)] + [(d_odd, i) for i in range(half)]
    targets += [(d_mate, 0)] if mates else []
    for i, (target, j) in enumerate(targets):
        if target is d_own or target is d_mate:
            target[0, :, :kv_width] = (acc[i, :, :kv_width] * score_scale).astype(target.dtype)
            target[0, :, kv_width:] = acc[i, :, kv_width:].astype(target.dtype)
        else:
            target[j, 0, :, :kv_width] = (acc[i, :, :kv_width] * score_scale).astype(target.dtype)
            target[j, 0, :, kv_width:] = acc[i, :, kv_width:].astype(target.dtype)


def attend_back(flags, query, own, even, odd, mate, grad, mixed, logs, cosine, sine, kv_heads, start, slots, d_query=None):
    _, block, width = query.shape

    def by_slot(array):
        lead = array.ndim - 1
        return pl.BlockSpec((1,) + array.shape[1:], lambda s, *pre: (s + start,) + (0,) * lead)

    def second_by_slot(array):
        lead = array.ndim - 2
        shape = (array.shape[0], 1) + array.shape[2:]
        return pl.BlockSpec(shape, lambda s, *pre: (0, s + start) + (0,) * lead)

    def out_by_slot(array):
        return pl.BlockSpec((1,) + array.shape[1:], lambda s, *pre: (s,) + (0,) * (array.ndim - 1))

    def out_second(array):
        shape = (array.shape[0], 1) + array.shape[2:]
        return pl.BlockSpec(shape, lambda s, *pre: (0, s) + (0,) * (array.ndim - 2))

    heads = width // HEAD_DIM
    mates = len(mate)
    earlier = () if d_query is None else (d_query,)
    operands = (*earlier, query, own, even, odd, *mate, grad, mixed, logs, cosine, sine)
    specs = [anywhere] * len(earlier) + [by_slot(query), by_slot(own), second_by_slot(even), second_by_slot(odd)]
    specs += [by_slot(m) for m in mate]
    specs += [by_slot(grad), by_slot(mixed), by_slot(logs), whole(cosine), whole(sine)]
    outs = (
        struct(query.shape, bf16),
        struct((slots,) + own.shape[1:], f32),
        struct((even.shape[0], slots) + even.shape[2:], bf16),
        struct((odd.shape[0], slots) + odd.shape[2:], bf16),
        *(struct((slots,) + m.shape[1:], bf16) for m in mate),
    )
    out_specs = [by_slot(outs[0]), out_by_slot(outs[1]), out_second(even), out_second(odd)]
    out_specs += [out_by_slot(m) for m in mate]
    count = 1 + 2 * even.shape[0] + mates
    return pl.pallas_call(
        functools.partial(attend_back_kernel, kv_heads, heads // kv_heads, mates, len(earlier)),
        grid_spec=pltpu.PrefetchScalarGridSpec(
            num_scalar_prefetch=1,
            grid=(slots,),
            in_specs=specs,
            out_specs=out_specs,
            scratch_shapes=[pltpu.VMEM((count,) + own.shape[1:], f32)],
        ),
        out_shape=outs,
        input_output_aliases={1: 0} if earlier else {},
        compiler_params=params(),
        cost_estimate=cost(25e9, 20e6, slots * heads * block * (own.shape[1] * 5)),
        name="attend_back",
    )(flags, *operands)


def middle_kernel(
    first, adapter, live, core, own, other, context, tok, cot, in_o, out_o, gain, in_g, in_u, out_d,
    mid_ref, normed_ref, grad_ref, rank_o_ref, rank_g_ref, rank_u_ref, grad_rank_ref, weight, sems,
):
    fetch_once(half_copies(core[0], own, other, ((first, weight.shape[2], weight),), sems))
    s = pl.program_id(0)
    ctx = context[0]
    mask = slot_lanes(adapter, ctx.shape[0], in_o.shape[0])
    rank = picked(mask, nt(ctx, in_o[...]))
    rank_o_ref[0] = rank
    mid = tok[0].astype(f32) + nt(ctx, as_matrix(weight)) + adapter_scale * nn(rank, out_o[...])
    mid_ref[0] = mid
    inverse = lax.rsqrt(jnp.mean(mid * mid, axis=-1, keepdims=True) + norm_eps)
    normed = (mid * inverse * gain[...]).astype(bf16)
    normed_ref[0] = normed
    rank_g_ref[0] = picked(mask, nt(normed, in_g[...]))
    rank_u_ref[0] = picked(mask, nt(normed, in_u[...]))
    on = jnp.where(live[s] != 0, 1.0, 0.0)
    grad = (cot[0].astype(f32) * on).astype(bf16)
    grad_ref[0] = grad
    grad_rank_ref[0] = picked(mask, adapter_scale * nt(grad, out_d[...]))


def middle_side(adapter_of, live, core, own, other, first, context, tokens, cotangent, in_o, out_o, gain,
                in_g, in_u, out_d):
    slots, block, width = tokens.shape
    shared = (in_o, out_o, gain, in_g, in_u, out_d)
    rank = struct((slots, block, in_o.shape[0]), bf16)
    wide = struct(tokens.shape, bf16)
    outs = (struct(tokens.shape, f32), wide, wide, rank, rank, rank, rank)
    return pl.pallas_call(
        functools.partial(middle_kernel, first),
        grid_spec=pltpu.PrefetchScalarGridSpec(
            num_scalar_prefetch=3,
            grid=(slots,),
            in_specs=[anywhere, anywhere]
            + [by_slot(a) for a in (context, tokens, cotangent)]
            + [whole(a) for a in shared],
            out_specs=[by_slot(o) for o in outs],
            scratch_shapes=buffers(own, (width // 2 // own.shape[1],), width),
        ),
        out_shape=outs,
        compiler_params=params(),
        cost_estimate=cost(3 * slots * block * width * width, 28e6),
        name="middle_side",
    )(adapter_of, live, core, own, other, context, tokens, cotangent, *shared)


def feed_copies(half, gate, up, down, sems, base):
    copies = []

    def add(source, target):
        copies.append(pltpu.make_async_copy(source, target, sems.at[base + len(copies)]))

    shards, line, rows, cols = half.shape
    rows //= 3
    for w in range(shards):
        span = pl.ds(w * cols, cols)
        add(half.at[w, :, pl.ds(0, rows), :], gate.at[:, :, span])
        add(half.at[w, :, pl.ds(rows, rows), :], up.at[:, :, span])
    last = pl.ds(2 * rows, rows)
    if shards == 1:
        add(half.at[0, :, last, :], down)
    else:
        for w in range(shards):
            for z in range(line):
                add(half.at[w, z, last, :], down.at[w, :, pl.ds(z * cols, cols)])
    return copies


def feed_kernel(first, count, span, core, *refs):
    halves, refs = refs[:count], refs[count:]
    x_ref, g_ref, rank_d, rank_g, rank_u = refs[:5]
    adapters, refs = refs[5 : 5 + 3 * count], refs[5 + 3 * count :]
    if first:
        sums_in = None
    else:
        sums_in, refs = refs[:5], refs[5:]
    sums_out, terms, refs = refs[:5], refs[5 : 5 + count], refs[5 + count :]
    weights, accs, sems = refs[: 3 * count], refs[3 * count : 4 * count], refs[4 * count]
    s = pl.program_id(0)
    copies, base = [], 0
    for i in range(count):
        copies.append(feed_copies(halves[i], *weights[3 * i : 3 * i + 3], sems, base))
        base += len(copies[-1])

    @pl.when(s == 0)
    def _():
        for group in copies:
            for c in group:
                c.start()
        for acc in accs:
            acc[...] = jnp.zeros_like(acc)

    x, g = x_ref[0], g_ref[0]
    r_d, r_g, r_u = rank_d[0], rank_g[0], rank_u[0]
    sums = [0.0] * 5 if first else [r[0] for r in sums_in]
    for i in range(count):

        @pl.when(s == 0)
        def _(i=i):
            for c in copies[i]:
                c.wait()

        gate_m, up_m, down_m = (as_matrix(b) for b in weights[3 * i : 3 * i + 3])
        in_d, out_g, out_u = (a[0] for a in adapters[3 * i : 3 * i + 3])
        acc = accs[i]
        hidden = gate_m.shape[0]
        for at in range(0, hidden, span):
            part = slice(at, min(at + span, hidden))
            o_g, o_u, i_d = out_g[part], out_u[part], in_d[part]
            w_g, w_u, w_d = gate_m[part], up_m[part], down_m[part]
            gate = nt(x, w_g) + adapter_scale * nt(r_g, o_g)
            up = nt(x, w_u) + adapter_scale * nt(r_u, o_u)
            d_act = nt(g, w_d) + nt(r_d, i_d)
            sig = 1.0 / (1.0 + jnp.exp(-gate))
            lit = gate * sig
            act = (lit * up).astype(bf16)
            d_gate = (d_act * up * sig * (1.0 + gate * (1.0 - sig))).astype(bf16)
            d_up = (d_act * lit).astype(bf16)
            sums[0] = sums[0] + nn(act, w_d)
            sums[1] = sums[1] + nn(d_gate, w_g) + nn(d_up, w_u)
            sums[2] = sums[2] + nn(act, i_d)
            sums[3] = sums[3] + nn(d_gate, o_g)
            sums[4] = sums[4] + nn(d_up, o_u)
            acc[0, :, part] += tn(r_g, d_gate)
            acc[1, :, part] += tn(r_u, d_up)
            acc[2, :, part] += tn(r_d, act)
    for ref, value in zip(sums_out, sums):
        ref[0] = value

    @pl.when(s == pl.num_programs(0) - 1)
    def _():
        for i in range(count):
            line, rows, _ = weights[3 * i].shape
            for j, scale in enumerate((adapter_scale, adapter_scale, 1.0)):
                turned = (accs[i][j] * scale).T.astype(bf16)
                for z in range(line):
                    terms[i][z, j * rows : (j + 1) * rows, :] = turned[z * rows : (z + 1) * rows]


def feed_part(core, halves, normed, grad, ranks, sums):
    slots, block, width = normed.shape
    rank_width = ranks[0].shape[-1]
    count = len(halves)
    first = sums is None
    operands = [h[0] for h in halves] + [normed, grad, *ranks]
    specs = [anywhere] * count + [by_slot(a) for a in (normed, grad, *ranks)]
    for _, of_other, adapters in halves:
        for a in adapters:
            operands.append(a)
            side = (lambda s, c: (1 - c[0], 0, 0)) if of_other else (lambda s, c: (c[0], 0, 0))
            specs.append(pl.BlockSpec((1,) + a.shape[1:], side))
    aliases = {}
    if not first:
        aliases = {1 + len(operands) + i: i for i in range(len(sums))}
        operands += list(sums)
        specs += [by_slot(a) for a in sums]
    rank_sum = struct((slots, block, rank_width), f32)
    wide_sum = struct((slots, block, width), f32)
    outs = [wide_sum, wide_sum, rank_sum, rank_sum, rank_sum]
    out_specs = [by_slot(o) for o in outs]
    scratch, hidden, copies = [], 0, 0
    for half, _, _ in halves:
        shards, line, rows = half.shape[:3]
        terms = struct((line, rows, rank_width), bf16)
        outs.append(terms)
        out_specs.append(whole(terms))
        scratch += [pltpu.VMEM((line, rows // 3, width), bf16)] * 3
        hidden += line * rows // 3
        copies += 2 * shards + (1 if shards == 1 else shards * line)
    for half, _, _ in halves:
        scratch.append(pltpu.VMEM((3, rank_width, half.shape[1] * half.shape[2] // 3), f32))
    return pl.pallas_call(
        functools.partial(feed_kernel, first, count, 512),
        grid_spec=pltpu.PrefetchScalarGridSpec(
            num_scalar_prefetch=1,
            grid=(slots,),
            in_specs=specs,
            out_specs=out_specs,
            scratch_shapes=scratch + [pltpu.SemaphoreType.DMA((copies,))],
        ),
        out_shape=outs,
        input_output_aliases=aliases,
        compiler_params=params(),
        cost_estimate=cost(20 * slots * block * hidden * width, 60e6, slots * block * hidden),
        name="feed_part",
    )(core, *operands)


def rms_back(hidden, gain, grad_normed):
    scaled = grad_normed * gain
    inverse = lax.rsqrt(jnp.mean(hidden * hidden, axis=-1, keepdims=True) + norm_eps)
    return inverse * scaled - hidden * (inverse * inverse * inverse) * jnp.mean(
        scaled * hidden, axis=-1, keepdims=True
    )


def keep_terms(acc, out, core, terms):
    s = pl.program_id(0)

    @pl.when(s == 0)
    def _():
        at = 0
        for t in terms:
            acc[:, at : at + t.shape[1]] = t
            at += t.shape[1]

    @pl.when(s != 0)
    def _():
        at = 0
        for t in terms:
            acc[:, at : at + t.shape[1]] += t
            at += t.shape[1]

    @pl.when(s == pl.num_programs(0) - 1)
    def _():
        line = out.shape[1]
        at, row = 0, 0
        for t in terms:
            n = t.shape[1]
            cut = n // (2 * line)
            turned = acc[:, at : at + n].T.astype(bf16)
            for z in range(line):
                for side in (0, 1):
                    block = turned[(2 * z + side) * cut : (2 * z + side + 1) * cut]
                    out[jnp.where(core == side, 0, 1), z, row : row + cut, :] = block
            at += n
            row += cut


def turned_terms(line, columns, ranks):
    return struct((2, line, columns // (2 * line), ranks), bf16)


def return_kernel(
    first, adapter, live, core, own, other, y, dx, sum_d, sum_g, sum_u, mid_in, normed, grad, context,
    rank_o, in_o, out_o, gain, in_g, in_u, out_d, layer_ref, d_mid_ref, d_ctx_ref, terms_ref, acc,
    weight, sems,
):
    fetch_once(half_copies(core[0], own, other, ((first, weight.shape[2], weight),), sems))
    s = pl.program_id(0)
    on = jnp.where(live[s] != 0, 1.0, 0.0)
    mid = mid_in[0]
    g = grad[0]
    mask = slot_lanes(adapter, g.shape[0], in_o.shape[0])
    rank_down = picked(mask, sum_d[0])
    result = mid + y[0] + adapter_scale * nn(rank_down, out_d[...])
    layer_ref[0] = (result * on).astype(bf16)
    back_g = picked(mask, adapter_scale * sum_g[0])
    back_u = picked(mask, adapter_scale * sum_u[0])
    d_normed = dx[0] + nn(back_g, in_g[...]) + nn(back_u, in_u[...])
    d_mid = g.astype(f32) + rms_back(mid, gain[...], d_normed)
    d_mid_ref[0] = d_mid
    branch = d_mid.astype(bf16)
    back_o = picked(mask, adapter_scale * nt(branch, out_o[...]))
    d_ctx_ref[0] = (nn(branch, as_matrix(weight)) + nn(back_o, in_o[...])).astype(bf16)
    x = normed[0]
    keep_terms(
        acc,
        terms_ref,
        core[0],
        (
            tn(back_o, context[0]),
            adapter_scale * tn(rank_o[0], branch),
            tn(back_g, x),
            tn(back_u, x),
            adapter_scale * tn(rank_down, g),
        ),
    )


def return_side(adapter_of, live, core, own, other, first, sums, mid, normed, grad, context, rank_o, in_o,
                out_o, gain, in_g, in_u, out_d):
    slots, block, width = mid.shape
    rows = (*sums, mid, normed, grad, context, rank_o)
    shared = (in_o, out_o, gain, in_g, in_u, out_d)
    ranks = in_o.shape[0]
    outs = (
        struct(mid.shape, bf16),
        struct(mid.shape, f32),
        struct(mid.shape, bf16),
        turned_terms(own.shape[1], 5 * width, ranks),
    )
    return pl.pallas_call(
        functools.partial(return_kernel, first),
        grid_spec=pltpu.PrefetchScalarGridSpec(
            num_scalar_prefetch=3,
            grid=(slots,),
            in_specs=[anywhere, anywhere] + [by_slot(r) for r in rows] + [whole(a) for a in shared],
            out_specs=[by_slot(o) for o in outs[:3]] + [whole(outs[3])],
            scratch_shapes=[pltpu.VMEM((ranks, 5 * width), f32)]
            + buffers(own, (width // 2 // own.shape[1],), width),
        ),
        out_shape=outs,
        compiler_params=params(),
        cost_estimate=cost(4 * slots * block * width * width, 50e6),
        name="return_side",
    )(adapter_of, live, core, own, other, *rows, *shared)


def query_back_kernel(
    adapter, core, own, other, d_query, normed, rank_q, in_q, out_q, d_normed_ref, terms_ref, acc,
    weight, sems,
):
    fetch_once(half_copies(core[0], own, other, ((0, weight.shape[2], weight),), sems))
    g, x = d_query[0], normed[0]
    mask = slot_lanes(adapter, g.shape[0], in_q.shape[0])
    rank_back = picked(mask, adapter_scale * nt(g, out_q[...]))
    d_normed_ref[0] = nn(g, as_matrix(weight)) + nn(rank_back, in_q[...])
    keep_terms(acc, terms_ref, core[0], (tn(rank_back, x), adapter_scale * tn(rank_q[0], g)))


def query_back_side(adapter_of, core, own, other, d_query, normed, rank_q, in_q, out_q):
    slots, block, width = normed.shape
    ranks = in_q.shape[0]
    rows = (d_query, normed, rank_q)
    shared = (in_q, out_q)
    outs = (struct(normed.shape, f32), turned_terms(own.shape[1], 2 * width, ranks))
    return pl.pallas_call(
        query_back_kernel,
        grid_spec=pltpu.PrefetchScalarGridSpec(
            num_scalar_prefetch=2,
            grid=(slots,),
            in_specs=[anywhere, anywhere] + [by_slot(r) for r in rows] + [whole(a) for a in shared],
            out_specs=[by_slot(outs[0]), whole(outs[1])],
            scratch_shapes=[pltpu.VMEM((ranks, 2 * width), f32)]
            + buffers(own, (width // 2 // own.shape[1],), width),
        ),
        out_shape=outs,
        compiler_params=params(),
        cost_estimate=cost(3 * slots * block * width * width, 22e6),
        name="query_back_side",
    )(adapter_of, core, own, other, *rows, *shared)


def output_kernel(
    first, adapter, live, core, own, other, d_kv, d_normed_q, d_mid, normed, rank_k, rank_v, tok, gain,
    cosine, sine, in_k, in_v, out_k, out_v, grad_ref, terms_ref, acc, key_w, value_w, sems,
):
    count = key_w.shape[2]
    parts = ((first, count, key_w), (first + count, count, value_w))
    fetch_once(half_copies(core[0], own, other, parts, sems))
    s = pl.program_id(0)
    on = jnp.where(live[s] != 0, 1.0, 0.0)
    kv_width = d_kv.shape[-1] // 2
    cos, sin = cosine[...], sine[...]
    back = d_kv[0]
    x = normed[0]
    mask = slot_lanes(adapter, x.shape[0], in_k.shape[0])
    keys = []
    for h in range(kv_width // HEAD_DIM):
        keys.append(turn_back(back[:, h * HEAD_DIM : (h + 1) * HEAD_DIM], cos, sin).astype(bf16))
    g_k, g_v = jnp.concatenate(keys, axis=1), back[:, kv_width:].astype(bf16)
    back_k = picked(mask, adapter_scale * nt(g_k, out_k[...]))
    back_v = picked(mask, adapter_scale * nt(g_v, out_v[...]))
    d_normed = d_normed_q[0] + nn(g_k, as_matrix(key_w)) + nn(g_v, as_matrix(value_w))
    d_normed = d_normed + nn(back_k, in_k[...]) + nn(back_v, in_v[...])
    hidden = tok[0].astype(f32)
    d_hidden = d_mid[0] + rms_back(hidden, gain[...], d_normed)
    grad_ref[0] = (d_hidden * on).astype(bf16)
    keep_terms(
        acc,
        terms_ref,
        core[0],
        (
            tn(back_k, x),
            tn(back_v, x),
            adapter_scale * tn(rank_k[0], g_k),
            adapter_scale * tn(rank_v[0], g_v),
        ),
    )


def output_side(adapter_of, live, core, own, other, first, d_kv, d_normed_q, d_mid, normed, rank_k, rank_v,
                tokens, gain, cosine, sine, adapters):
    slots, block, width = tokens.shape
    ranks = adapters[0].shape[0]
    kv_columns = d_kv.shape[-1]
    columns = 2 * width + kv_columns
    kv_rows = kv_columns // 4 // own.shape[1]
    rows = (d_kv, d_normed_q, d_mid, normed, rank_k, rank_v, tokens)
    shared = (gain, cosine, sine, *adapters)
    outs = (struct(tokens.shape, bf16), turned_terms(own.shape[1], columns, ranks))
    return pl.pallas_call(
        functools.partial(output_kernel, first),
        grid_spec=pltpu.PrefetchScalarGridSpec(
            num_scalar_prefetch=3,
            grid=(slots,),
            in_specs=[anywhere, anywhere] + [by_slot(r) for r in rows] + [whole(a) for a in shared],
            out_specs=[by_slot(outs[0]), whole(outs[1])],
            scratch_shapes=[pltpu.VMEM((ranks, columns), f32)]
            + buffers(own, (kv_rows, kv_rows), width),
        ),
        out_shape=outs,
        compiler_params=params(),
        cost_estimate=cost(3 * slots * block * width * kv_columns, 30e6),
        name="output_side",
    )(adapter_of, live, core, own, other, *rows, *shared)


def hop_up(array, t, line):
    half = line // 2
    return along_line(array, [(z, z - 1) for z in range(1, line) if half <= z + t - 1 < line])


def hops_down(mine, line):
    half = line // 2
    moved = [mine]
    for t in range(1, half):
        pairs = [(z, z + 1) for z in range(line - 1) if half <= z - t + 1]
        moved.append(along_line(moved[-1], pairs))
    return moved


def prompt_blocks(from_above, from_below, place, line):
    half = line // 2
    mine = from_above[0]
    blocks = []
    for b in range(half, line):
        out = mine
        for z in range(line):
            if z < b:
                out = jnp.where(place == z, from_above[b - z], out)
            elif z > b:
                out = jnp.where(place == z, from_below[z - b], out)
        blocks.append(out)
    return jnp.stack(blocks)


def take(blocks, at):
    return lax.dynamic_index_in_dim(blocks, jnp.clip(at, 0, blocks.shape[0] - 1), 0, False)


def fold_blocks(parts, line):
    half = line // 2
    return [along_line(parts, [(z, half - 1)]) for z in range(half - 1)]


def return_blocks(parts, total, place, line):
    half = line // 2
    came = []
    for b in range(half, line):
        came.append(along_line(total[b - half], [(half - 1, b)]))
    for by in range(1, half):
        pairs = [(z, z - by) for z in range(half + by, line)]
        came.append(along_line(take(parts, place - by - half), pairs))
    return came


def owned_blocks(parts, came, place, line):
    half = line // 2
    total = functools.reduce(jnp.add, [c.astype(f32) for c in came])
    total = total + take(parts, place - half).astype(f32)
    return jnp.where(place >= half, total, 0.0)


def finish_kernel(places, segments, core, own, other, *refs):
    count = len(places)
    outs, buffers, sems = refs[:count], refs[count : 2 * count], refs[2 * count]
    shards, line, rows, _ = own.shape
    copies = []
    for side, half in ((core[0], own), (1 - core[0], other)):
        for at, n, to, offset in segments:
            while n:
                w, row = at // rows, at % rows
                take = min(n, rows - row)
                for z in range(line):
                    start = pl.multiple_of((2 * z + side) * places[to] + offset, 16)
                    copies.append(
                        pltpu.make_async_copy(
                            half.at[w, z, pl.ds(row, take), :],
                            buffers[to].at[pl.ds(start, take), :],
                            sems.at[len(copies)],
                        )
                    )
                at, n, offset = at + take, n - take, offset + take
    for c in copies:
        c.start()
    for c in copies:
        c.wait()
    for out, buffer in zip(outs, buffers):
        total = buffer.shape[0]
        step = next(d for d in (1280, 768, 256) if total % d == 0)
        for at in range(0, total, step):
            block = buffer[at : at + step, :].astype(f32).T
            out[:, :, at : at + step] = block.reshape(out.shape[:2] + (step,))


def finish(core, own, other, places, segments):
    shards, line, rows, ranks = own.shape
    outs = [struct((ranks // RANK, RANK, 2 * line * p), f32) for p in places]
    pieces = 0
    for at, n, _, _ in segments:
        pieces += (at + n - 1) // rows - at // rows + 1
    return pl.pallas_call(
        functools.partial(finish_kernel, places, segments),
        grid_spec=pltpu.PrefetchScalarGridSpec(
            num_scalar_prefetch=1,
            grid=(1,),
            in_specs=[anywhere, anywhere],
            out_specs=[whole(o) for o in outs],
            scratch_shapes=[pltpu.VMEM((2 * line * p, ranks), bf16) for p in places]
            + [pltpu.SemaphoreType.DMA((2 * line * pieces,))],
        ),
        out_shape=outs,
        compiler_params=params(),
        name="finish",
    )(core, own, other)


def split_rows(mine, shards):
    n = mine.shape[1]
    padded = jnp.pad(mine, ((0, 0), (0, -n % (16 * shards)), (0, 0)))
    return padded.reshape(mine.shape[0], shards, -1, mine.shape[2])


def late_segments(rows, pitch, shift, counts, first):
    segments, at = [], 0
    for i, n in enumerate(counts):
        done = 0
        while done < n:
            w, row = (at + done) // rows, (at + done) % rows
            take = min(n - done, rows - row)
            segments.append((w * pitch + shift + row, take, first + i, done))
            done += take
        at += n
    return segments


def pack_kernel(spans, core, gate, up, down, given, *outs):
    kept = down[core[0]]
    came = given[...]
    first = jnp.where(core[0] == 0, kept, came)
    second = jnp.where(core[0] == 0, came, kept)
    turned = (gate[...].T, up[...].T, jnp.concatenate([first, second], axis=1))
    for out, (at, n) in zip(outs, spans):
        for i, t in enumerate(turned):
            out[i * n : (i + 1) * n, :] = t[at : at + n]


def pack_weights(spans, core, gate, up, down, given):
    outs = [struct((3 * n, gate.shape[0]), bf16) for _, n in spans]
    return pl.pallas_call(
        functools.partial(pack_kernel, spans),
        grid_spec=pltpu.PrefetchScalarGridSpec(
            num_scalar_prefetch=1,
            grid=(1,),
            in_specs=[whole(a) for a in (gate, up, down, given)],
            out_specs=[whole(o) for o in outs],
        ),
        out_shape=outs,
        compiler_params=params(),
        cost_estimate=cost(0, 12e6),
        name="pack_weights",
    )(core, gate, up, down, given)


def order_kernel(spans, line, wide, *outs):
    scratch = outs[-1]
    hidden = wide.shape[1]
    step = next(d for d in (1280, 256) if hidden % d == 0)
    for at in range(0, hidden, step):
        scratch[at : at + step, :] = wide[:, at : at + step].T
    shard = hidden // (2 * line)
    for out, (at, n) in zip(outs, spans):
        for z in range(line):
            for side in (0, 1):
                start = (2 * z + side) * shard + at
                out[side, z * n : (z + 1) * n, :] = scratch[start : start + n, :]


def order_adapters(spans, line, wide):
    ranks, hidden = wide.shape
    outs = [struct((2, line * n, ranks), bf16) for _, n in spans]
    return pl.pallas_call(
        functools.partial(order_kernel, spans, line),
        out_shape=outs,
        scratch_shapes=[pltpu.VMEM((hidden, ranks), bf16)],
        compiler_params=pltpu.CompilerParams(vmem_limit_bytes=VMEM_LIMIT),
        cost_estimate=cost(0, 5e6),
        name="order_adapters",
    )(wide)


def local(
    tokens,
    cotangent,
    group_slot,
    group_adapter,
    attn_gain,
    mlp_gain,
    w_query,
    w_key,
    w_value,
    w_output,
    w_gate,
    w_up,
    w_down,
    query_bias,
    key_bias,
    value_bias,
    adapt_query_in,
    adapt_query_out,
    adapt_key_in,
    adapt_key_out,
    adapt_value_in,
    adapt_value_out,
    adapt_output_in,
    adapt_output_out,
    adapt_gate_in,
    adapt_gate_out,
    adapt_up_in,
    adapt_up_out,
    adapt_down_in,
    adapt_down_out,
):
    slots, block, width = tokens.shape
    ctx_size, shards = lax.axis_size("ctx"), lax.axis_size("wsh")
    line = ctx_size // 2
    ctx_place, shard_place = lax.axis_index("ctx"), lax.axis_index("wsh")
    place, core = ctx_place // 2, ctx_place % 2
    kv_width = key_bias.shape[0]
    kv_heads = kv_width // HEAD_DIM
    hidden = adapt_gate_out.shape[-1]
    if line != shards or (CONTS * CONT) != line * block or CONT // block > 2:
        raise ValueError("unsupported mesh")
    mates = CONT // block - 1

    slot_ids = shard_place * slots + jnp.arange(slots, dtype=jnp.int32)
    matches = group_slot[None, :] == slot_ids[:, None]
    live = jnp.any(matches, axis=1).astype(jnp.int32)
    adapter_of = jnp.sum(jnp.where(matches, group_adapter[None, :], 0), axis=1).astype(jnp.int32)
    index = ctx_place * block + jnp.arange(block, dtype=jnp.int32)
    position = jnp.where(index >= CONTS * CONT, index - CONTS * CONT, PROMPT + index % CONT)
    frequency = rope_base ** (-(jnp.arange(HEAD_DIM // 2, dtype=f32) * 2.0) / HEAD_DIM)
    angles = position.astype(f32)[:, None] * frequency[None, :]
    cosine = jnp.concatenate([jnp.cos(angles), jnp.cos(angles)], axis=-1)
    sine = jnp.concatenate([-jnp.sin(angles), jnp.sin(angles)], axis=-1)

    is_cont = ctx_place < line
    of_side = [2 * (line // 2 + i) + core for i in range(line // 2)]
    of_other = [2 * (line // 2 + i) + 1 - core for i in range(line // 2)]
    flags = [(is_cont | (b < ctx_place)) for b in of_side + of_other]
    flags += [is_cont & (core == 1)] if mates else []
    flags = jnp.stack(flags).astype(jnp.int32)

    def wide(half):
        if half.shape[-1] % 128 == 0:
            return half
        return jnp.transpose(half, (1, 2, 0, 3)).reshape(1, line, half.shape[2], width)

    def wide_feed(half):
        if half.shape[-1] % 128 == 0:
            return half
        split = half.shape[2] // 3 * 2
        out_in = jnp.transpose(half[:, :, :split], (1, 2, 0, 3)).reshape(1, line, split, width)
        in_out = jnp.transpose(half[:, :, split:], (0, 2, 1, 3)).reshape(1, line, split // 2, width)
        return jnp.concatenate([out_in, in_out], axis=2)

    q_rows = w_query.shape[1]
    o_at = q_rows
    kv_piece = jnp.concatenate([w_key.T, w_value.T], axis=0)
    qo_piece = jnp.concatenate([w_query.T, w_output.T], axis=0)
    kv_moves = line_moves(kv_piece, line)
    qo_moves = line_moves(qo_piece, line)

    shard_hidden = w_gate.shape[1]
    unit = shard_hidden // 35
    part_rows = [5 * unit, 8 * unit, 8 * unit, 8 * unit, 6 * unit]
    part_at = [sum(part_rows[:i]) for i in range(len(part_rows))]
    parts = len(part_rows)
    spans = list(zip(part_at, part_rows))
    core_place = core.astype(jnp.int32)[None]
    down_halves = w_down.reshape(2, shard_hidden, w_down.shape[1])
    given = swap_cores(lax.dynamic_index_in_dim(down_halves, 1 - core, 0, False))
    pieces = pack_weights(spans, core_place, w_gate, w_up, down_halves, given)
    pieces = list(pieces)

    lined_kv = in_order(kv_piece, hold(kv_moves, pieces[0]), place, line)
    down_in, gate_out, up_out = (
        order_adapters(spans, line, a.reshape(-1, a.shape[-1]))
        for a in (adapt_down_in, adapt_gate_out, adapt_up_out)
    )
    kv_half = gather_wsh(lined_kv, shard_place)
    kv_own, kv_other = wide(kv_half), wide(swap_cores(kv_half))
    lined_qo = in_order(qo_piece, qo_moves, place, line)
    qo_half = shard_gather(lined_qo)

    def flat(adapters):
        return adapters.reshape(-1, adapters.shape[-1])

    query_in, key_in, value_in, output_in, gate_in, up_in = (
        flat(a)
        for a in (adapt_query_in, adapt_key_in, adapt_value_in, adapt_output_in, adapt_gate_in, adapt_up_in)
    )
    query_out, key_out, value_out, output_out, down_out = (
        flat(a)
        for a in (adapt_query_out, adapt_key_out, adapt_value_out, adapt_output_out, adapt_down_out)
    )

    gain_one = attn_gain.astype(f32)[None, :]
    gain_two = mlp_gain.astype(f32)[None, :]
    q_bias = query_bias.astype(f32)[None, :]
    kv_bias = jnp.concatenate([key_bias, value_bias]).astype(f32)[None, :]

    lined, halves = [], []

    def take_in(moves, group, *after):
        moves, at = hold(moves, *after), 0
        for i in group:
            n = pieces[i].shape[0]
            came = [m[at : at + n] for m in moves]
            lined.append(in_order(pieces[i], came, place, line))
            halves.append(shard_gather(lined[-1]))
            at += n

    def set_out(group, *after):
        together = hold([pieces[i] for i in group], *after)
        piece = jnp.concatenate(together, axis=0) if len(group) > 1 else together[0]
        return piece, line_moves(piece, line)

    _, moves = set_out([0], lined_qo)
    attn_kv = (core_place, kv_own, kv_other)
    kv_adapters = (key_in, value_in, key_out, value_out)
    normed, rank_k, rank_v, key_value = key_value_side(
        adapter_of, *attn_kv, 0, tokens, gain_one, kv_bias, kv_adapters, cosine, sine
    )
    hops = [key_value, hop_up(key_value, 1, line)]
    below = hops_down(key_value, line)
    mate = (swap_cores(key_value),) if mates else ()
    hops.append(hop_up(hops[1], 2, line))
    for t in range(3, line):
        hops.append(hop_up(hops[-1], t, line))
    take_in(moves, [0], key_value, *down_in, *gate_out, *up_out)
    _, moves = set_out([1], lined[0])
    take_in(moves, [1], tip(hops[2]))
    _, moves = set_out([2], lined[1])
    (qo_half,) = hold([qo_half], tip(hops[2]))
    attn = (core_place, wide(qo_half), wide(swap_cores(qo_half)))
    rank_q, queries = query_side(
        adapter_of, *attn, normed, q_bias, (query_in, query_out), cosine, sine
    )
    side = prompt_blocks(hops, below, place, line)
    other_side = swap_cores(side)
    (queries,) = hold([queries], lined[1])
    context, mixed, logs = attend(flags, queries, key_value, side, other_side, mate, kv_heads)
    take_in(moves, [2], context)
    _, moves = set_out([3], lined[2])
    (context,) = hold([context], lined[2])
    mid, normed2, grad_out, rank_o, rank_g, rank_u, rank_d = middle_side(
        adapter_of, live, *attn, o_at, context, tokens, cotangent, output_in, output_out, gain_two,
        gate_in, up_in, down_out,
    )

    sums, own_terms, other_terms, others = None, [], [], []
    before = normed2
    for i in range(parts + 1):
        if 0 < i < 3:
            take_in(moves, [i + 2], before)
            if i + 3 < parts:
                _, moves = set_out([i + 3], lined[i + 2])
        if i < parts:
            (halves[i],) = hold([halves[i]], before, lined[-1])
            others.append(swap_cores(halves[i]))
        use = []
        if i < parts:
            use.append((wide_feed(halves[i]), False, (down_in[i], gate_out[i], up_out[i])))
        if i:
            j = i - 1
            use.append((wide_feed(others[j]), True, (down_in[j], gate_out[j], up_out[j])))
        done = feed_part(core_place, use, normed2, grad_out, (rank_d, rank_g, rank_u), sums)
        sums, terms = done[:5], done[5:]
        if i < parts:
            own_terms.append(terms[0])
        if i:
            other_terms.append(terms[-1])
        before = sums[2]
    early_keep = jnp.concatenate(own_terms, axis=1)
    early_came = swap_cores(jnp.concatenate(other_terms, axis=1))
    layer_out, d_mid, d_context, terms = return_side(
        adapter_of, live, *attn, o_at, sums, mid, normed2, grad_out, context, rank_o,
        output_in, output_out, gain_two, gate_in, up_in, down_out,
    )

    first_half = slots // 2

    def slots_back(start, count, d_context, d_query=None):
        return attend_back(
            flags, queries, key_value, side, other_side, mate, d_context, mixed, logs, cosine, sine,
            kv_heads, start, count, d_query,
        )

    (early_came,) = hold([early_came], d_context)
    early = split_rows(add_up([early_keep, early_came]), shards)
    early_outs = wsh_outs(early, shard_place)
    late_keep, late_give = terms[0], terms[1]
    (d_context, late_give) = hold([d_context, late_give], *early_outs)
    early_moves = wsh_send(early_outs)
    late_came = swap_cores(late_give)
    back = [slots_back(0, first_half, d_context)]
    sides = [add_up([back[0][2], swap_cores(back[0][3])])]
    late_came, *early_moves = hold([late_came, *early_moves], back[0][1])
    late = split_rows(add_up([late_keep, late_came]), shards)
    late_outs = wsh_outs(late, shard_place)
    early = wsh_sum(early, shard_place, early_moves)
    early_outs = line_outs(early, place, line)
    (d_context,) = hold([d_context], sides[0], *late_outs, *early_outs)
    folded = [fold_blocks(sides[0], line)]
    late_moves = wsh_send(late_outs)
    early_moves = line_send(early_outs, line)
    back.append(slots_back(first_half, slots - first_half, d_context, back[0][0]))
    swapped = swap_cores(back[1][3])
    *late_moves, late = hold([*late_moves, late], back[1][1])
    folded[0] = hold(folded[0], back[1][1]) if folded[0] else []
    sides.append(add_up([back[1][2], swapped]))
    total = add_up([sides[0]] + folded[0])
    late = wsh_sum(late, shard_place, late_moves)
    late_outs = line_outs(late, place, line)
    early_terms = line_sum(early, place, hold(early_moves, back[1][1]))
    (d_query,) = hold([back[1][0]], sides[1], total, *late_outs, early_terms)
    folded.append(fold_blocks(sides[1], line))
    came = [return_blocks(sides[0], total, place, line)]
    late_moves = line_send(late_outs, line)
    early_moves = line_moves(early_terms, line)
    d_normed_q, query_terms = query_back_side(
        adapter_of, *attn, d_query, normed, rank_q, query_in, query_out
    )
    folded[1] = hold(folded[1], query_terms) if folded[1] else []
    total = add_up([sides[1]] + folded[1])
    came.append(return_blocks(sides[1], total, place, line))
    early_lined = in_order(early_terms, hold(early_moves, query_terms, tip(total)), place, line)
    early_half = shard_gather(early_lined)
    came[0] = hold(came[0], query_terms)
    d_kv = jnp.concatenate(
        [b[1] + owned_blocks(p, c, place, line) for b, p, c in zip(back, sides, came)], axis=0
    )
    if mates:
        d_kv = d_kv + swap_cores(jnp.concatenate([b[4] for b in back], axis=0)).astype(f32)
    late_terms = line_sum(late, place, hold(late_moves, query_terms, tip(total)))
    (d_kv,) = hold([d_kv], early_lined)
    input_grad, kv_terms = output_side(
        adapter_of, live, *attn_kv, 0, d_kv, d_normed_q, d_mid, normed, rank_k, rank_v, tokens, gain_one,
        cosine, sine, kv_adapters,
    )

    width_rows = width // (2 * line)
    last_keep = jnp.concatenate([query_terms[0], kv_terms[0]], axis=1)
    last_came = swap_cores(jnp.concatenate([query_terms[1], kv_terms[1]], axis=1))
    last = split_rows(add_up([last_keep, last_came]), shards)
    moves = wsh_send(wsh_outs(last, shard_place))
    last = wsh_sum(last, shard_place, moves)
    moves = line_send(line_outs(last, place, line), line)
    (early_half,) = hold([early_half], tip(last))
    early_other = swap_cores(early_half)
    last_terms = line_sum(last, place, moves)
    last_terms = jnp.concatenate([late_terms, last_terms], axis=0)
    last_lined = in_order(last_terms, line_moves(last_terms, line), place, line)
    last_own = gather_wsh(last_lined, shard_place)
    last_other = swap_cores(last_own)
    segments = [
        (3 * at + i * n, n, i, at) for at, n in spans for i in range(3)
    ]
    g_gate_out, g_up_out, g_down_in = finish(
        core_place, early_half, early_other, (shard_hidden,) * 3, segments
    )
    kv_rows = kv_width // (2 * line)
    segments = late_segments(late_terms.shape[0], last_terms.shape[0], 0, (width_rows,) * 5, 0)
    segments += late_segments(
        last_terms.shape[0] - late_terms.shape[0], last_terms.shape[0], late_terms.shape[0],
        (width_rows,) * 4 + (kv_rows,) * 2, 5,
    )
    (
        g_output_in, g_output_out, g_gate_in, g_up_in, g_down_out,
        g_query_in, g_query_out, g_key_in, g_value_in, g_key_out, g_value_out,
    ) = finish(
        core_place, last_own, last_other, (width_rows,) * 9 + (kv_rows,) * 2, segments
    )
    return (
        layer_out,
        input_grad,
        g_query_in,
        g_query_out,
        g_key_in,
        g_key_out,
        g_value_in,
        g_value_out,
        g_output_in,
        g_output_out,
        g_gate_in,
        g_gate_out,
        g_up_in,
        g_up_out,
        g_down_in,
        g_down_out,
    )


def solution(mesh):
    weight = P("wsh", "ctx")
    rows = P("wsh", "ctx", None)
    return jax.shard_map(
        local,
        mesh=mesh,
        in_specs=(rows, rows) + (P(),) * 4 + (weight,) * 7 + (P(),) * 17,
        out_specs=(rows, rows) + (P(),) * 14,
        check_vma=False,
    )
```

time: 1280 us -> 1070 us (0.84)
  waiting for transfers between devices: 374 us -> 203 us
  local copies, waits for them, and re-layouts: 135 us -> 82.3 us
  Pallas kernels: 502 us -> 537 us
  other arithmetic: 55.8 us -> 37.8 us
    ppermute x65 -> x48, waiting for transfers between devices: 291 us -> 136 us  [along_line(): lax.ppermute(array, 'ctx', [(2 * a + c, 2 * b + c) for a, b in pairs for...]
    ppermute x22 -> x16, waiting for transfers between devices: 44.3 us -> 8.84 us  [swap_cores(): return lax.ppermute(array, 'ctx', [(i, i ^ 1) for i in range(size)])]
    pallas_call x13 -> x16, Pallas kernels: 378 us -> 406 us  [the longest x6 295 us: feed_part(): pl.pallas_call(functools.partial(feed_kernel, first, count, 512), grid_sp...]
    all_gather x7, waiting for transfers between devices: 0.1 us -> 23.1 us  [shard_gather(): return lax.all_gather(lined, 'wsh', axis=0, tiled=False)]
    transpose x9 -> x0, local copies, waits for them, and re-layouts: 21.8 us -> none  [the longest x3 10.3 us: by_part(): cut = flat(adapters).T.reshape(line, 2, parts, rows, -1)]
    another operation x10 -> x0, other arithmetic: 19.9 us -> none  [the longest x6 10.2 us: gather_all(): jnp.stack([jnp.where(core == 0, all_own, other), jnp.where(core == 0, oth...]
    slice x20 -> x3, local copies, waits for them, and re-layouts: 19 us -> 2.46 us  [tip(): return lax.slice(array, (0,) * array.ndim, ends)]
    convert_element_type x16 -> x12, other arithmetic: 7.15 us -> 20.1 us  [add_up(): functools.reduce(jnp.add, [a.astype(f32) for a in arrays]).astype(bf16)]
  transfers between devices with their start and end apart: 118 -> 86, of which waited for: 43 -> 27; matrix products, arithmetic and copies ran while one was open for 13% -> 8% of each run, Pallas kernels for 35% -> 44%
where the time goes in v2:
time: 1070 us; the launch traced here: 1060 us
  Pallas kernels  537 us (50%)
  waiting for transfers between devices  203 us (19%)
  starting transfers between devices  180 us (17%)
  local copies, waits for them, and re-layouts  82.3 us (8%)
  other arithmetic  37.8 us (4%)
  between operations  16.1 us (2%)
    pallas_call x6, Pallas kernels, feed_part(): pl.pallas_call(functools.partial(feed_kernel, first, count, 512), grid_sp...  295 us
    ppermute x48, starting transfers between devices, along_line(): lax.ppermute(array, 'ctx', [(2 * a + c, 2 * b + c) for a, b in pairs for...  161 us
    ppermute x48, waiting for transfers between devices, along_line(): lax.ppermute(array, 'ctx', [(2 * a + c, 2 * b + c) for a, b in pairs for...  136 us
    pallas_call x2, Pallas kernels, attend_back(): pl.pallas_call(functools.partial(attend_back_kernel, kv_heads, heads // k...  66.2 us
    unnamed x171, local copies, waits for them, and re-layouts  34.7 us
    pallas_call x1, Pallas kernels, attend(): pl.pallas_call(functools.partial(attend_kernel, kv_heads, heads // kv_hea...  34.4 us
    ppermute x15, waiting for transfers between devices, across(): return lax.ppermute(array, 'wsh', [(i, i ^ by) for i in range(size)])  34.3 us
    pallas_call x1, Pallas kernels, return_side(): pl.pallas_call(functools.partial(return_kernel, first), grid_spec=pltpu.P...  32.6 us
  transfers between devices with their start and end apart: 86, of which 27 were waited for; matrix products, arithmetic and copies ran while one was open for 8% of the time, Pallas kernels for 44%

profile of v2, /device:TPU:0, one launch (start us, length us, event | category | flops | bytes accessed | tf_op | source)
XLA Modules:
  0.0 1055.7 jit_solution(10079893420009933396)
XLA Ops:
  16.6 4.8 collective-permute-done
  21.4 11.8 %collective-permute-done.1 = bf16[384,384]{1,0:T(8,128)(2,1)S(1)} collective-permute-done((bf16[384,384]{1,0:T(8,128)(2,1)S(1)}, bf16[384,384]{1,0:T(8,128)(2,1)S(1)}, u32[]{:S(2)}, u32[]{:S(2)}) %collective-permute-start.1) | collective-permute-done | bytes 294944 | tf_op jit(solution)/shard_map/ppermute | solution.py:42
  34.4 6.8 collective-permute-start.3
  52.7 4.0 pack_weights.1
  63.5 4.1 collective-permute-done.7
  67.7 5.2 collective-permute-done.8
  80.7 3.9 order_adapters.3
  84.6 3.9 order_adapters.4
  88.5 3.9 order_adapters.5
  93.2 9.7 key_value_side.1
  113.1 34.2 %collective-permute-start.17 = (bf16[768,384]{1,0:T(8,128)(2,1)}, bf16[768,384]{1,0:T(8,128)(2,1)}, u32[]{:S(2)}, u32[]{:S(2)}) collective-permute-start(bf16[768,384]{1,0:T(8,128)(2,1)} %hold.37), channel_id=1, source_target_pairs={{0,8},{4,12},{8,16},{12,20},{16,24},{20,28},{24,0},{28,4},{1,9},{5... | collective-permute-start | bytes 1769480 | tf_op jit(solution)/shard_map/ppermute | solution.py:42
  152.7 27.8 %collective-permute-done.12 = bf16[4,256,512]{2,1,0:T(8,128)(2,1)} collective-permute-done((bf16[4,256,512]{2,1,0:T(8,128)(2,1)}, bf16[4,256,512]{2,1,0:T(8,128)(2,1)}, u32[]{:S(2)}, u32[]{:S(2)}) %collective-permute-start.12) | collective-permute-done | bytes 1048608 | tf_op jit(solution)/shard_map/ppermute | solution.py:42
  181.8 24.0 %collective-permute-done.18.refs_1_ = bf16[768,384]{1,0:T(8,128)(2,1)} collective-permute-done((bf16[768,384]{1,0:T(8,128)(2,1)}, bf16[768,384]{1,0:T(8,128)(2,1)}, u32[]{:S(2)}, u32[]{:S(2)}) %collective-permute-start.18) | collective-permute-done | bytes 589856 | tf_op jit(solution)/shard_map/ppermute | solution.py:42
  212.9 37.1 %collective-permute-done.24 = bf16[4,256,512]{2,1,0:T(8,128)(2,1)S(1)} collective-permute-done((bf16[4,256,512]{2,1,0:T(8,128)(2,1)}, bf16[4,256,512]{2,1,0:T(8,128)(2,1)S(1)}, u32[]{:S(2)}, u32[]{:S(2)}) %collective-permute-start.24) | collective-permute-done | bytes 1048608 | tf_op jit(solution)/shard_map/ppermute | solution.py:42
  255.2 3.7 collective-permute-start.22
  259.0 13.2 %query_side.1 = (bf16[4,256,128]{2,1,0:T(8,128)(2,1)}, bf16[4,256,1536]{2,1,0:T(8,128)(2,1)}) custom-call(s32[4]{0:T(128)} %fusion.24.adapter, s32[1]{0:T(128)} %bitcast.core, bf16[4,4,384,384]{3,2,1,0:T(8,128)(2,1)} %hold.34.own, bf16[4,4,384,384]{3,2,1,0:T(8,128)(2,1)} %collective-permute-done.13.other, bf16[4,256,1536]{2,1,0:T(8,128)(2,1)} %get-tuple-element.192.normed, ...), custom_call_target="tpu_custom_call" | custom-call | flops 6039797760 | bytes 12000000 | tf_op jit(solution)/shard_map/query_side/pallas_call | solution.py:296
  272.2 34.4 %attend.1 = (bf16[4,256,1536]{2,1,0:T(8,128)(2,1)}, f32[4,12,128,256]{3,2,1,0:T(8,128)}, f32[4,12,256]{2,1,0:T(8,128)}) custom-call(s32[4]{0:T(128)} %add_convert_fusion.6.flags, bf16[4,256,1536]{2,1,0:T(8,128)(2,1)} %hold.40.refs_0_.refs_1_, bf16[4,256,512]{2,1,0:T(8,128)(2,1)} %get-tuple-element.166.refs_3_.refs_1_.refs_2_, ...), custom_call_target="tpu_custom_call" | custom-call | flops 20000000000 | bytes 20000000 | tf_op jit(solution)/shard_map/attend/pallas_call | solution.py:362
  320.1 19.5 %middle_side.1 = (f32[4,256,1536]{2,1,0:T(8,128)}, bf16[4,256,1536]{2,1,0:T(8,128)(2,1)}, bf16[4,256,1536]{2,1,0:T(8,128)(2,1)}, bf16[4,256,128]{2,1,0:T(8,128)(...) custom-call(s32[4]{0:T(128)} %fusion.24.adapter, ...), custom_call_target="tpu_custom_call" | custom-call | flops 7247757312 | bytes 28000000 | tf_op jit(solution)/shard_map/middle_side/pallas_call | solution.py:517
  339.6 26.3 %feed_part.6 = (f32[4,256,1536]{2,1,0:T(8,128)}, f32[4,256,1536]{2,1,0:T(8,128)}, f32[4,256,128]{2,1,0:T(8,128)}, f32[4,256,128]{2,1,0:T(8,128)}, f32[4,256,128]{2,1,0:T(8,128)}, /*index=5*/bf16[4,480,128]{2,1,0:T(8,128)(2,1)}) custom-call(s32[1]{0:T(128)} %bitcast.core, bf16[4,4,480,384]{3,2,1,0:T(8,128)(2,1)} %hold.44.refs_0_, ...), custom_call_target="tpu_custom_call" | custom-call | flops 20132659200 | bytes 60000000 | tf_op jit(solution)/shard_map/feed_part/pallas_call | solution.py:660
  381.9 55.8 %feed_part.7 = (f32[4,256,1536]{2,1,0:T(8,128)}, f32[4,256,1536]{2,1,0:T(8,128)}, f32[4,256,128]{2,1,0:T(8,128)}, f32[4,256,128]{2,1,0:T(8,128)}, f32[4,256,128]...) custom-call(s32[1]{0:T(128)} %bitcast.core, ...), custom_call_target="tpu_custom_call", output_to_operand_aliasing={{0}: (14, {}), {1}: (15, {}), {2}: (16, {}), {3}: (17, {}),... | custom-call | flops 52344913920 | bytes 60000000 | tf_op jit(solution)/shard_map/feed_part/pallas_call | solution.py:660
  443.4 63.3 %feed_part.8 = (f32[4,256,1536]{2,1,0:T(8,128)}, f32[4,256,1536]{2,1,0:T(8,128)}, f32[4,256,128]{2,1,0:T(8,128)}, f32[4,256,128]{2,1,0:T(8,128)}, f32[4,256,128]...) custom-call(s32[1]{0:T(128)} %bitcast.core, ...), custom_call_target="tpu_custom_call", output_to_operand_aliasing={{0}: (14, {}), {1}: (15, {}), {2}: (16, {}), {3}: (17, {}),... | custom-call | flops 64424509440 | bytes 60000000 | tf_op jit(solution)/shard_map/feed_part/pallas_call | solution.py:660
  506.7 7.6 all-gather.23.cloned.1.call-done
  514.4 63.6 %feed_part.9 = (f32[4,256,1536]{2,1,0:T(8,128)}, f32[4,256,1536]{2,1,0:T(8,128)}, f32[4,256,128]{2,1,0:T(8,128)}, f32[4,256,128]{2,1,0:T(8,128)}, f32[4,256,128]...) custom-call(s32[1]{0:T(128)} %bitcast.core, ...), custom_call_target="tpu_custom_call", output_to_operand_aliasing={{0}: (14, {}), {1}: (15, {}), {2}: (16, {}), {3}: (17, {}),... | custom-call | flops 64424509440 | bytes 60000000 | tf_op jit(solution)/shard_map/feed_part/pallas_call | solution.py:660
  578.0 15.3 %all-gather.21.cloned.1.call-done = bf16[16,576,384]{2,1,0:T(8,128)(2,1)} async-done(((bf16[4,576,384]{2,1,0:T(8,128)(2,1)}), bf16[16,576,384]{2,1,0:T(8,128)(2,1)}) %all-gather.21.cloned.1.call-update) | async-done | bytes 7077904 | tf_op jit(solution)/shard_map/all_gather | solution.py:83
  597.3 56.7 %feed_part.10 = (f32[4,256,1536]{2,1,0:T(8,128)}, f32[4,256,1536]{2,1,0:T(8,128)}, f32[4,256,128]{2,1,0:T(8,128)}, f32[4,256,128]{2,1,0:T(8,128)}, f32[4,256,128...) custom-call(s32[1]{0:T(128)} %bitcast.core, ...), custom_call_target="tpu_custom_call", output_to_operand_aliasing={{0}: (14, {}), {1}: (15, {}), {2}: (16, {}), {3}: (17, {}),... | custom-call | flops 56371445760 | bytes 60000000 | tf_op jit(solution)/shard_map/feed_part/pallas_call | solution.py:660
  656.1 29.8 %feed_part.11 = (f32[4,256,1536]{2,1,0:T(8,128)}, f32[4,256,1536]{2,1,0:T(8,128)}, f32[4,256,128]{2,1,0:T(8,128)}, f32[4,256,128]{2,1,0:T(8,128)}, f32[4,256,128]{2,1,0:T(8,128)}, /*index=5*/bf16[4,576,128]{2,1,0:T(8,128)(2,1)}) custom-call(s32[1]{0:T(128)} %bitcast.core, ...), custom_call_target="tpu_custom_call", output_to_operand_aliasing={{0}: (10, {}), {1}: (11, {}), {2}: (12, {}), {3}: (13, {}),... | custom-call | flops 24159191040 | bytes 60000000 | tf_op jit(solution)/shard_map/feed_part/pallas_call | solution.py:660
  692.9 32.6 %return_side.1 = (bf16[4,256,1536]{2,1,0:T(8,128)(2,1)}, f32[4,256,1536]{2,1,0:T(8,128)}, bf16[4,256,1536]{2,1,0:T(8,128)(2,1)}, bf16[2,4,960,128]{3,2,1,0:T(8,128)(2,1)}) custom-call(s32[4]{0:T(128)} %fusion.24.adapter, s32[4]{0:T(128)} %convert_element_type.232.live, s32[1]{0:T(128)} %bitcast.core, bf16[4,4,384,384]{3,2,1,0:T(8,128)(2,1)} %hold.34.own, ...), custom_call_target="tpu_custom_call" | custom-call | flops 9663676416 | bytes 50000000 | tf_op jit(solution)/shard_map/return_side/pallas_call | solution.py:771
  729.6 3.9 add_convert_fusion
  738.9 32.8 %attend_back.2 = (bf16[4,256,1536]{2,1,0:T(8,128)(2,1)}, f32[2,256,512]{2,1,0:T(8,128)}, bf16[2,2,256,512]{3,2,1,0:T(8,128)(2,1)}, bf16[2,2,256,512]{3,2,1,0:T(8,128)(2,1)}) custom-call(s32[4]{0:T(128)} %add_convert_fusion.6.flags, bf16[4,256,1536]{2,1,0:T(8,128)(2,1)} %hold.40.refs_0_.refs_1_, ...), custom_call_target="tpu_custom_call" | custom-call | flops 24999999488 | bytes 20000000 | tf_op jit(solution)/shard_map/attend_back/pallas_call | solution.py:470
  772.3 4.9 collective-permute-done.42.refs_2_
  785.6 33.4 %attend_back.3 = (bf16[4,256,1536]{2,1,0:T(8,128)(2,1)}, f32[2,256,512]{2,1,0:T(8,128)}, bf16[2,2,256,512]{3,2,1,0:T(8,128)(2,1)}, bf16[2,2,256,512]{3,2,1,0:T(8,128)(2,1)}) custom-call(s32[4]{0:T(128)} %add_convert_fusion.6.flags, bf16[4,256,1536]{2,1,0:T(8,128)(2,1)} %get-tuple-element.260.refs_0_, ...), custom_call_target="tpu_custom_call", output_to_operand_aliasing={{0}: (1, {})} | custom-call | flops 24999999488 | bytes 20000000 | tf_op jit(solution)/shard_map/attend_back/pallas_call | solution.py:470
  829.8 8.2 collective-permute-done.52.refs_1_
  842.4 4.5 collective-permute-start.58
  846.9 4.3 collective-permute-done.49.refs_1_
  851.3 5.7 collective-permute-start.60
  861.2 3.5 collective-permute-start.54
  868.8 17.4 %query_back_side.1 = (f32[4,256,1536]{2,1,0:T(8,128)}, bf16[2,4,384,128]{3,2,1,0:T(8,128)(2,1)}) custom-call(s32[4]{0:T(128)} %fusion.24.adapter, s32[1]{0:T(128)} %bitcast.core, bf16[4,4,384,384]{3,2,1,0:T(8,128)(2,1)} %hold.34.own, bf16[4,4,384,384]{3,2,1,0:T(8,128)(2,1)} %collective-permute-done.13.other, bf16[4,256,1536]{2,1,0:T(8,128)(2,1)} %hold.59.d_query, ...), custom_call_target="tpu_custom_call" | custom-call | flops 7247757312 | bytes 22000000 | tf_op jit(solution)/shard_map/query_back_side/pallas_call | solution.py:806
  886.2 8.0 collective-permute-done.54.refs_0_
  918.2 16.3 %output_side.1 = (bf16[4,256,1536]{2,1,0:T(8,128)(2,1)}, bf16[2,4,448,128]{3,2,1,0:T(8,128)(2,1)}) custom-call(s32[4]{0:T(128)} %fusion.24.adapter, s32[4]{0:T(128)} %convert_element_type.232.live, s32[1]{0:T(128)} %bitcast.core, bf16[4,4,64,384]{3,2,1,0:T(8,128)(2,1)} %copy-done.22, bf16[4,4,64,384]{3,2,1,0:T(8,128)(2,1)} %collective-permute-done.10.other, ...), custom_call_target="tpu_custom_call" | custom-call | flops 2415919104 | bytes 30000000 | tf_op jit(solution)/shard_map/output_side/pallas_call | solution.py:871
  942.1 36.0 %collective-permute-start.61 = (bf16[240,128]{1,0:T(8,128)(2,1)S(1)}, bf16[240,128]{1,0:T(8,128)(2,1)S(1)}, u32[]{:S(2)}, u32[]{:S(2)}) collective-permute-start(bf16[240,128]{1,0:T(8,128)(2,1)S(1)} %copy-done.64), channel_id=1, source_target_pairs={{0,8},{4,12},{8,16},{12,20},{16,24},{20,28},{24,0},{28,4},{1,9},{5... | collective-permute-start | bytes 184328 | tf_op jit(solution)/shard_map/ppermute | solution.py:42
  978.1 3.4 collective-permute-start.62
  988.3 4.4 collective-permute-start.69
  997.0 4.1 collective-permute-start.72
  1011.2 9.5 collective-permute-done.74
  1020.8 6.1 collective-permute-done.75
  1027.2 3.8 collective-permute-done.77.other
  1032.2 6.4 finish.2
  1038.6 10.0 finish.3
  (469 shorter events, 210.1 us)
Async XLA Ops:
  7.2 203.6 %all-gather.15.cloned.1.call-start = ((), (), s32[]{:S(2)}) async-start(), calls=%async_computation | async-start | bytes 5898240 | tf_op jit(solution)/shard_map/all_gather | solution.py:83
  11.3 21.8 %collective-permute-start.1 = (bf16[384,384]{1,0:T(8,128)(2,1)S(1)}, bf16[384,384]{1,0:T(8,128)(2,1)S(1)}, u32[]{:S(2)}, u32[]{:S(2)}) collective-permute-start(bf16[384,384]{1,0:T(8,128)(2,1)S(1)} %pad_maximum_fusion.3), channel_id=1, source_target_pairs={{0,16},{4,20},{8,24},{12,28},{16,0},{20,4},{24,8},{28,12},{1,17},{... | collective-permute-start | bytes 884744 | tf_op jit(solution)/shard_map/ppermute | solution.py:42
  34.3 305.2 %all-gather.17.cloned.1.call-start = ((), (), s32[]{:S(2)}) async-start(), calls=%async_computation.1 | async-start | bytes 7372800 | tf_op jit(solution)/shard_map/all_gather | solution.py:83
  34.4 22.2 %collective-permute-start.3 = (bf16[64,384]{1,0:T(8,128)(2,1)S(1)}, bf16[64,384]{1,0:T(8,128)(2,1)S(1)}, u32[]{:S(2)}, u32[]{:S(2)}) collective-permute-start(bf16[64,384]{1,0:T(8,128)(2,1)S(1)} %pad_maximum_fusion.7), channel_id=1, source_target_pairs={{0,8},{4,12},{8,16},{12,20},{16,24},{20,28},{24,0},{28,4},{1,9},{5... | collective-permute-start | bytes 147464 | tf_op jit(solution)/shard_map/ppermute | solution.py:42
  73.0 20.3 %collective-permute-start.10 = (bf16[4,4,64,384]{3,2,1,0:T(8,128)(2,1)S(1)}, bf16[4,4,64,384]{3,2,1,0:T(8,128)(2,1)}, u32[]{:S(2)}, u32[]{:S(2)}) collective-permute-start(bf16[4,4,64,384]{3,2,1,0:T(8,128)(2,1)S(1)} %bitcast_dynamic-update-slice_fusion.32.own), channel_id=1, source_target_pairs={{0,4},{4,0},{8,12},{12,8},{16,20},{20,16},{24,28},{28,24},{1,5},{5... | collective-permute-start | bytes 2359304 | tf_op jit(solution)/shard_map/ppermute | solution.py:47
  74.6 28.4 %collective-permute-start.14 = (bf16[480,384]{1,0:T(8,128)(2,1)}, bf16[480,384]{1,0:T(8,128)(2,1)S(1)}, u32[]{:S(2)}, u32[]{:S(2)}) collective-permute-start(bf16[480,384]{1,0:T(8,128)(2,1)} %hold.35), channel_id=1, source_target_pairs={{0,8},{4,12},{8,16},{12,20},{16,24},{20,28},{24,0},{28,4},{1,9},{5... | collective-permute-start | bytes 1105928 | tf_op jit(solution)/shard_map/ppermute | solution.py:42
  75.7 27.8 %collective-permute-start.15 = (bf16[480,384]{1,0:T(8,128)(2,1)}, bf16[480,384]{1,0:T(8,128)(2,1)S(1)}, u32[]{:S(2)}, u32[]{:S(2)}) collective-permute-start(bf16[480,384]{1,0:T(8,128)(2,1)} %hold.35), channel_id=1, source_target_pairs={{0,16},{4,20},{8,24},{12,28},{16,0},{20,4},{24,8},{28,12},{1,17},{... | collective-permute-start | bytes 1105928 | tf_op jit(solution)/shard_map/ppermute | solution.py:42
  78.1 25.4 %collective-permute-start.16 = (bf16[480,384]{1,0:T(8,128)(2,1)}, bf16[480,384]{1,0:T(8,128)(2,1)S(1)}, u32[]{:S(2)}, u32[]{:S(2)}) collective-permute-start(bf16[480,384]{1,0:T(8,128)(2,1)} %hold.35), channel_id=1, source_target_pairs={{0,24},{4,28},{8,0},{12,4},{16,8},{20,12},{24,16},{28,20},{1,25},{... | collective-permute-start | bytes 1105928 | tf_op jit(solution)/shard_map/ppermute | solution.py:42
  108.8 263.2 %all-gather.19.cloned.1.call-start = ((), (), s32[]{:S(2)}) async-start(), calls=%async_computation.2 | async-start | bytes 11796480 | tf_op jit(solution)/shard_map/all_gather | solution.py:83
  110.5 70.0 %collective-permute-start.12 = (bf16[4,256,512]{2,1,0:T(8,128)(2,1)}, bf16[4,256,512]{2,1,0:T(8,128)(2,1)}, u32[]{:S(2)}, u32[]{:S(2)}) collective-permute-start(bf16[4,256,512]{2,1,0:T(8,128)(2,1)} %collective-permute-done.11), channel_id=1, source_target_pairs={{8,0},{12,4},{16,8},{20,12},{9,1},{13,5},{17,9},{21,13},{10,2},{14... | collective-permute-start | bytes 3145736 | tf_op jit(solution)/shard_map/ppermute | solution.py:42
  113.1 68.6 %collective-permute-start.17 = (bf16[768,384]{1,0:T(8,128)(2,1)}, bf16[768,384]{1,0:T(8,128)(2,1)}, u32[]{:S(2)}, u32[]{:S(2)}) collective-permute-start(bf16[768,384]{1,0:T(8,128)(2,1)} %hold.37), channel_id=1, source_target_pairs={{0,8},{4,12},{8,16},{12,20},{16,24},{20,28},{24,0},{28,4},{1,9},{5... | collective-permute-start | bytes 1769480 | tf_op jit(solution)/shard_map/ppermute | solution.py:42
  147.3 58.4 %collective-permute-start.18 = (bf16[768,384]{1,0:T(8,128)(2,1)}, bf16[768,384]{1,0:T(8,128)(2,1)}, u32[]{:S(2)}, u32[]{:S(2)}) collective-permute-start(bf16[768,384]{1,0:T(8,128)(2,1)} %hold.37), channel_id=1, source_target_pairs={{0,16},{4,20},{8,24},{12,28},{16,0},{20,4},{24,8},{28,12},{1,17},{... | collective-permute-start | bytes 1769480 | tf_op jit(solution)/shard_map/ppermute | solution.py:42
  149.9 55.9 %collective-permute-start.19 = (bf16[768,384]{1,0:T(8,128)(2,1)}, bf16[768,384]{1,0:T(8,128)(2,1)}, u32[]{:S(2)}, u32[]{:S(2)}) collective-permute-start(bf16[768,384]{1,0:T(8,128)(2,1)} %hold.37), channel_id=1, source_target_pairs={{0,24},{4,28},{8,0},{12,4},{16,8},{20,12},{24,16},{28,20},{1,25},{... | collective-permute-start | bytes 1769480 | tf_op jit(solution)/shard_map/ppermute | solution.py:42
  210.7 231.3 %all-gather.25.cloned.1.call-start = ((), (), s32[]{:S(2)}) async-start(), calls=%async_computation.5 | async-start | bytes 11796480 | tf_op jit(solution)/shard_map/all_gather | solution.py:83
  210.8 48.2 %collective-permute-start.13 = (bf16[4,4,384,384]{3,2,1,0:T(8,128)(2,1)}, bf16[4,4,384,384]{3,2,1,0:T(8,128)(2,1)}, u32[]{:S(2)}, u32[]{:S(2)}) collective-permute-start(bf16[4,4,384,384]{3,2,1,0:T(8,128)(2,1)} %hold.34.own), channel_id=1, source_target_pairs={{0,4},{4,0},{8,12},{12,8},{16,20},{20,16},{24,28},{28,24},{1,5},{5... | collective-permute-start | bytes 14155784 | tf_op jit(solution)/shard_map/ppermute | solution.py:47
  211.6 38.4 %collective-permute-start.24 = (bf16[4,256,512]{2,1,0:T(8,128)(2,1)}, bf16[4,256,512]{2,1,0:T(8,128)(2,1)S(1)}, u32[]{:S(2)}, u32[]{:S(2)}) collective-permute-start(bf16[4,256,512]{2,1,0:T(8,128)(2,1)} %collective-permute-done.12), channel_id=1, source_target_pairs={{8,0},{12,4},{9,1},{13,5},{10,2},{14,6},{11,3},{15,7}} | collective-permute-start | bytes 3145736 | tf_op jit(solution)/shard_map/ppermute | solution.py:42
  254.9 51.7 %collective-permute-start.20 = (bf16[768,384]{1,0:T(8,128)(2,1)}, bf16[768,384]{1,0:T(8,128)(2,1)S(1)}, u32[]{:S(2)}, u32[]{:S(2)}) collective-permute-start(bf16[768,384]{1,0:T(8,128)(2,1)} %hold.39), channel_id=1, source_target_pairs={{0,8},{4,12},{8,16},{12,20},{16,24},{20,28},{24,0},{28,4},{1,9},{5... | collective-permute-start | bytes 1769480 | tf_op jit(solution)/shard_map/ppermute | solution.py:42
  255.2 51.5 %collective-permute-start.21 = (bf16[768,384]{1,0:T(8,128)(2,1)}, bf16[768,384]{1,0:T(8,128)(2,1)S(1)}, u32[]{:S(2)}, u32[]{:S(2)}) collective-permute-start(bf16[768,384]{1,0:T(8,128)(2,1)} %hold.39), channel_id=1, source_target_pairs={{0,16},{4,20},{8,24},{12,28},{16,0},{20,4},{24,8},{28,12},{1,17},{... | collective-permute-start | bytes 1769480 | tf_op jit(solution)/shard_map/ppermute | solution.py:42
  255.2 51.4 %collective-permute-start.22 = (bf16[768,384]{1,0:T(8,128)(2,1)}, bf16[768,384]{1,0:T(8,128)(2,1)}, u32[]{:S(2)}, u32[]{:S(2)}) collective-permute-start(bf16[768,384]{1,0:T(8,128)(2,1)} %hold.39), channel_id=1, source_target_pairs={{0,24},{4,28},{8,0},{12,4},{16,8},{20,12},{24,16},{28,20},{1,25},{... | collective-permute-start | bytes 1769480 | tf_op jit(solution)/shard_map/ppermute | solution.py:42
  312.6 201.8 %all-gather.23.cloned.1.call-start = ((), (), s32[]{:S(2)}) async-start(), calls=%async_computation.4 | async-start | bytes 11796480 | tf_op jit(solution)/shard_map/all_gather | solution.py:83
  314.3 51.6 %collective-permute-start.26 = (bf16[768,384]{1,0:T(8,128)(2,1)}, bf16[768,384]{1,0:T(8,128)(2,1)S(1)}, u32[]{:S(2)}, u32[]{:S(2)}) collective-permute-start(bf16[768,384]{1,0:T(8,128)(2,1)} %hold.42), channel_id=1, source_target_pairs={{0,8},{4,12},{8,16},{12,20},{16,24},{20,28},{24,0},{28,4},{1,9},{5... | collective-permute-start | bytes 1769480 | tf_op jit(solution)/shard_map/ppermute | solution.py:42
  317.4 48.5 %collective-permute-start.27 = (bf16[768,384]{1,0:T(8,128)(2,1)}, bf16[768,384]{1,0:T(8,128)(2,1)S(1)}, u32[]{:S(2)}, u32[]{:S(2)}) collective-permute-start(bf16[768,384]{1,0:T(8,128)(2,1)} %hold.42), channel_id=1, source_target_pairs={{0,16},{4,20},{8,24},{12,28},{16,0},{20,4},{24,8},{28,12},{1,17},{... | collective-permute-start | bytes 1769480 | tf_op jit(solution)/shard_map/ppermute | solution.py:42
  317.4 48.5 %collective-permute-start.28 = (bf16[768,384]{1,0:T(8,128)(2,1)}, bf16[768,384]{1,0:T(8,128)(2,1)}, u32[]{:S(2)}, u32[]{:S(2)}) collective-permute-start(bf16[768,384]{1,0:T(8,128)(2,1)} %hold.42), channel_id=1, source_target_pairs={{0,24},{4,28},{8,0},{12,4},{16,8},{20,12},{24,16},{28,20},{1,25},{... | collective-permute-start | bytes 1769480 | tf_op jit(solution)/shard_map/ppermute | solution.py:42
  371.8 221.5 %all-gather.21.cloned.1.call-start = ((), (), s32[]{:S(2)}) async-start(), calls=%async_computation.3 | async-start | bytes 8847360 | tf_op jit(solution)/shard_map/all_gather | solution.py:83
  372.0 71.4 %collective-permute-start.33 = (bf16[4,4,768,384]{3,2,1,0:T(8,128)(2,1)}, bf16[4,4,768,384]{3,2,1,0:T(8,128)(2,1)}, u32[]{:S(2)}, u32[]{:S(2)}) collective-permute-start(bf16[4,4,768,384]{3,2,1,0:T(8,128)(2,1)} %hold.47.refs_0_), channel_id=1, source_target_pairs={{0,4},{4,0},{8,12},{12,8},{16,20},{20,16},{24,28},{28,24},{1,5},{5... | collective-permute-start | bytes 28311560 | tf_op jit(solution)/shard_map/ppermute | solution.py:47
  373.1 64.6 %collective-permute-start.29 = (bf16[576,384]{1,0:T(8,128)(2,1)}, bf16[576,384]{1,0:T(8,128)(2,1)S(1)}, u32[]{:S(2)}, u32[]{:S(2)}) collective-permute-start(bf16[576,384]{1,0:T(8,128)(2,1)} %hold.46), channel_id=1, source_target_pairs={{0,8},{4,12},{8,16},{12,20},{16,24},{20,28},{24,0},{28,4},{1,9},{5... | collective-permute-start | bytes 1327112 | tf_op jit(solution)/shard_map/ppermute | solution.py:42
  376.4 61.3 %collective-permute-start.30 = (bf16[576,384]{1,0:T(8,128)(2,1)}, bf16[576,384]{1,0:T(8,128)(2,1)S(1)}, u32[]{:S(2)}, u32[]{:S(2)}) collective-permute-start(bf16[576,384]{1,0:T(8,128)(2,1)} %hold.46), channel_id=1, source_target_pairs={{0,16},{4,20},{8,24},{12,28},{16,0},{20,4},{24,8},{28,12},{1,17},{... | collective-permute-start | bytes 1327112 | tf_op jit(solution)/shard_map/ppermute | solution.py:42
  378.7 59.0 %collective-permute-start.31 = (bf16[576,384]{1,0:T(8,128)(2,1)}, bf16[576,384]{1,0:T(8,128)(2,1)S(1)}, u32[]{:S(2)}, u32[]{:S(2)}) collective-permute-start(bf16[576,384]{1,0:T(8,128)(2,1)} %hold.46), channel_id=1, source_target_pairs={{0,24},{4,28},{8,0},{12,4},{16,8},{20,12},{24,16},{28,20},{1,25},{... | collective-permute-start | bytes 1327112 | tf_op jit(solution)/shard_map/ppermute | solution.py:42
  443.2 71.2 %collective-permute-start.34 = (bf16[4,4,768,384]{3,2,1,0:T(8,128)(2,1)}, bf16[4,4,768,384]{3,2,1,0:T(8,128)(2,1)}, u32[]{:S(2)}, u32[]{:S(2)}) collective-permute-start(bf16[4,4,768,384]{3,2,1,0:T(8,128)(2,1)} %hold.49.refs_0_), channel_id=1, source_target_pairs={{0,4},{4,0},{8,12},{12,8},{16,20},{20,16},{24,28},{28,24},{1,5},{5... | collective-permute-start | bytes 28311560 | tf_op jit(solution)/shard_map/ppermute | solution.py:47
  443.4 560.3 %all-gather.27.cloned.1.call-start = ((), (), s32[]{:S(2)}) async-start(), calls=%async_computation.6 | async-start | bytes 4341760 | tf_op jit(solution)/shard_map/all_gather | solution.py:83
  514.4 82.9 %collective-permute-start.36 = (bf16[4,4,768,384]{3,2,1,0:T(8,128)(2,1)}, bf16[4,4,768,384]{3,2,1,0:T(8,128)(2,1)}, u32[]{:S(2)}, u32[]{:S(2)}) collective-permute-start(bf16[4,4,768,384]{3,2,1,0:T(8,128)(2,1)} %hold.50.refs_0_), channel_id=1, source_target_pairs={{0,4},{4,0},{8,12},{12,8},{16,20},{20,16},{24,28},{28,24},{1,5},{5... | collective-permute-start | bytes 28311560 | tf_op jit(solution)/shard_map/ppermute | solution.py:47
  593.4 62.8 %collective-permute-start.35 = (bf16[4,4,576,384]{3,2,1,0:T(8,128)(2,1)}, bf16[4,4,576,384]{3,2,1,0:T(8,128)(2,1)}, u32[]{:S(2)}, u32[]{:S(2)}) collective-permute-start(bf16[4,4,576,384]{3,2,1,0:T(8,128)(2,1)} %hold.51.refs_0_), channel_id=1, source_target_pairs={{0,4},{4,0},{8,12},{12,8},{16,20},{20,16},{24,28},{28,24},{1,5},{5... | collective-permute-start | bytes 21233672 | tf_op jit(solution)/shard_map/ppermute | solution.py:47
  688.1 39.8 %collective-permute-start.37 = (bf16[4,3360,128]{2,1,0:T(8,128)(2,1)}, bf16[4,3360,128]{2,1,0:T(8,128)(2,1)S(1)}, u32[]{:S(2)}, u32[]{:S(2)}) collective-permute-start(bf16[4,3360,128]{2,1,0:T(8,128)(2,1)} %constant_dynamic-update-slice_fusion.5), channel_id=1, source_target_pairs={{0,4},{4,0},{8,12},{12,8},{16,20},{20,16},{24,28},{28,24},{1,5},{5... | collective-permute-start | bytes 10321928 | tf_op jit(solution)/shard_map/ppermute | solution.py:47
  735.4 36.9 %collective-permute-start.41 = (bf16[4,848,128]{2,1,0:T(8,128)(2,1)}, bf16[4,848,128]{2,1,0:T(8,128)(2,1)}, u32[]{:S(2)}, u32[]{:S(2)}) collective-permute-start(bf16[4,848,128]{2,1,0:T(8,128)(2,1)} %get-tuple-element.312.refs_2_), channel_id=1, source_target_pairs={{0,1},{1,0},{2,3},{3,2},{4,5},{5,4},{6,7},{7,6},{8,9},{9,8},{10,11... | collective-permute-start | bytes 2605064 | tf_op jit(solution)/shard_map/ppermute | solution.py:108
  736.8 40.3 %collective-permute-start.42 = (bf16[4,848,128]{2,1,0:T(8,128)(2,1)}, bf16[4,848,128]{2,1,0:T(8,128)(2,1)}, u32[]{:S(2)}, u32[]{:S(2)}) collective-permute-start(bf16[4,848,128]{2,1,0:T(8,128)(2,1)} %get-tuple-element.311.refs_3_), channel_id=1, source_target_pairs={{0,2},{1,3},{2,0},{3,1},{4,6},{5,7},{6,4},{7,5},{8,10},{9,11},{10,... | collective-permute-start | bytes 2605064 | tf_op jit(solution)/shard_map/ppermute | solution.py:108
  737.4 39.8 %collective-permute-start.43 = (bf16[4,848,128]{2,1,0:T(8,128)(2,1)}, bf16[4,848,128]{2,1,0:T(8,128)(2,1)}, u32[]{:S(2)}, u32[]{:S(2)}) collective-permute-start(bf16[4,848,128]{2,1,0:T(8,128)(2,1)} %get-tuple-element.310.refs_4_), channel_id=1, source_target_pairs={{0,3},{1,2},{2,1},{3,0},{4,7},{5,6},{6,5},{7,4},{8,11},{9,10},{10,... | collective-permute-start | bytes 2605064 | tf_op jit(solution)/shard_map/ppermute | solution.py:108
  738.9 38.3 %collective-permute-start.40 = (bf16[4,960,128]{2,1,0:T(8,128)(2,1)}, bf16[4,960,128]{2,1,0:T(8,128)(2,1)}, u32[]{:S(2)}, u32[]{:S(2)}) collective-permute-start(bf16[4,960,128]{2,1,0:T(8,128)(2,1)} %get-tuple-element.261), channel_id=1, source_target_pairs={{0,4},{4,0},{8,12},{12,8},{16,20},{20,16},{24,28},{28,24},{1,5},{5... | collective-permute-start | bytes 2949128 | tf_op jit(solution)/shard_map/ppermute | solution.py:47
  819.0 39.4 %collective-permute-start.47 = (bf16[2,2,256,512]{3,2,1,0:T(8,128)(2,1)}, bf16[2,2,256,512]{3,2,1,0:T(8,128)(2,1)}, u32[]{:S(2)}, u32[]{:S(2)}) collective-permute-start(bf16[2,2,256,512]{3,2,1,0:T(8,128)(2,1)} %get-tuple-element.269), channel_id=1, source_target_pairs={{0,4},{4,0},{8,12},{12,8},{16,20},{20,16},{24,28},{28,24},{1,5},{5... | collective-permute-start | bytes 3145736 | tf_op jit(solution)/shard_map/ppermute | solution.py:47
  824.5 40.9 %collective-permute-start.39 = (bf16[2,2,256,512]{3,2,1,0:T(8,128)(2,1)S(1)}, bf16[2,2,256,512]{3,2,1,0:T(8,128)(2,1)S(1)}, u32[]{:S(2)}, u32[]{:S(2)}) collective-permute-start(bf16[2,2,256,512]{3,2,1,0:T(8,128)(2,1)S(1)} %copy-done.5), channel_id=1, source_target_pairs={{0,8},{4,12},{1,9},{5,13},{2,10},{6,14},{3,11},{7,15}} | collective-permute-start | bytes 3145736 | tf_op jit(solution)/shard_map/ppermute | solution.py:42
  842.4 55.2 %collective-permute-start.58 = (bf16[848,128]{1,0:T(8,128)(2,1)}, bf16[848,128]{1,0:T(8,128)(2,1)}, u32[]{:S(2)}, u32[]{:S(2)}) collective-permute-start(bf16[848,128]{1,0:T(8,128)(2,1)} %get-tuple-element.309.refs_6_), channel_id=1, source_target_pairs={{0,8},{4,12},{8,16},{12,20},{16,24},{20,28},{24,0},{28,4},{1,9},{5... | collective-permute-start | bytes 651272 | tf_op jit(solution)/shard_map/ppermute | solution.py:42
  851.3 46.3 %collective-permute-start.59 = (bf16[848,128]{1,0:T(8,128)(2,1)}, bf16[848,128]{1,0:T(8,128)(2,1)}, u32[]{:S(2)}, u32[]{:S(2)}) collective-permute-start(bf16[848,128]{1,0:T(8,128)(2,1)} %get-tuple-element.309.refs_6_), channel_id=1, source_target_pairs={{0,16},{4,20},{8,24},{12,28},{16,0},{20,4},{24,8},{28,12},{1,17},{... | collective-permute-start | bytes 651272 | tf_op jit(solution)/shard_map/ppermute | solution.py:42
  851.3 46.3 %collective-permute-start.60 = (bf16[848,128]{1,0:T(8,128)(2,1)}, bf16[848,128]{1,0:T(8,128)(2,1)}, u32[]{:S(2)}, u32[]{:S(2)}) collective-permute-start(bf16[848,128]{1,0:T(8,128)(2,1)} %get-tuple-element.309.refs_6_), channel_id=1, source_target_pairs={{0,24},{4,28},{8,0},{12,4},{16,8},{20,12},{24,16},{28,20},{1,25},{... | collective-permute-start | bytes 651272 | tf_op jit(solution)/shard_map/ppermute | solution.py:42
  861.2 32.9 %collective-permute-start.54 = (bf16[2,2,256,512]{3,2,1,0:T(8,128)(2,1)}, bf16[2,2,256,512]{3,2,1,0:T(8,128)(2,1)}, u32[]{:S(2)}, u32[]{:S(2)}) collective-permute-start(bf16[2,2,256,512]{3,2,1,0:T(8,128)(2,1)} %add_convert_fusion.2.refs_1_), channel_id=1, source_target_pairs={{0,8},{4,12},{1,9},{5,13},{2,10},{6,14},{3,11},{7,15}} | collective-permute-start | bytes 3145736 | tf_op jit(solution)/shard_map/ppermute | solution.py:42
  938.6 49.5 %collective-permute-start.65 = (bf16[4,208,128]{2,1,0:T(8,128)(2,1)S(1)}, bf16[4,208,128]{2,1,0:T(8,128)(2,1)S(1)}, u32[]{:S(2)}, u32[]{:S(2)}) collective-permute-start(bf16[4,208,128]{2,1,0:T(8,128)(2,1)S(1)} %get-tuple-element.327), channel_id=1, source_target_pairs={{0,1},{1,0},{2,3},{3,2},{4,5},{5,4},{6,7},{7,6},{8,9},{9,8},{10,11... | collective-permute-start | bytes 638984 | tf_op jit(solution)/shard_map/ppermute | solution.py:108
  939.2 48.8 %collective-permute-start.66 = (bf16[4,208,128]{2,1,0:T(8,128)(2,1)S(1)}, bf16[4,208,128]{2,1,0:T(8,128)(2,1)S(1)}, u32[]{:S(2)}, u32[]{:S(2)}) collective-permute-start(bf16[4,208,128]{2,1,0:T(8,128)(2,1)S(1)} %get-tuple-element.329), channel_id=1, source_target_pairs={{0,2},{1,3},{2,0},{3,1},{4,6},{5,7},{6,4},{7,5},{8,10},{9,11},{10,... | collective-permute-start | bytes 638984 | tf_op jit(solution)/shard_map/ppermute | solution.py:108
  940.7 47.4 %collective-permute-start.67 = (bf16[4,208,128]{2,1,0:T(8,128)(2,1)S(1)}, bf16[4,208,128]{2,1,0:T(8,128)(2,1)S(1)}, u32[]{:S(2)}, u32[]{:S(2)}) collective-permute-start(bf16[4,208,128]{2,1,0:T(8,128)(2,1)S(1)} %get-tuple-element.328), channel_id=1, source_target_pairs={{0,3},{1,2},{2,1},{3,0},{4,7},{5,6},{6,5},{7,4},{8,11},{9,10},{10,... | collective-permute-start | bytes 638984 | tf_op jit(solution)/shard_map/ppermute | solution.py:108
  942.1 41.1 %collective-permute-start.61 = (bf16[240,128]{1,0:T(8,128)(2,1)S(1)}, bf16[240,128]{1,0:T(8,128)(2,1)S(1)}, u32[]{:S(2)}, u32[]{:S(2)}) collective-permute-start(bf16[240,128]{1,0:T(8,128)(2,1)S(1)} %copy-done.64), channel_id=1, source_target_pairs={{0,8},{4,12},{8,16},{12,20},{16,24},{20,28},{24,0},{28,4},{1,9},{5... | collective-permute-start | bytes 184328 | tf_op jit(solution)/shard_map/ppermute | solution.py:42
  1003.7 34.9 %collective-permute-start.78 = (bf16[4,4,848,128]{3,2,1,0:T(8,128)(2,1)}, bf16[4,4,848,128]{3,2,1,0:T(8,128)(2,1)}, u32[]{:S(2)}, u32[]{:S(2)}) collective-permute-start(bf16[4,4,848,128]{3,2,1,0:T(8,128)(2,1)} %hold.65.own), channel_id=1, source_target_pairs={{0,4},{4,0},{8,12},{12,8},{16,20},{20,16},{24,28},{28,24},{1,5},{5... | collective-permute-start | bytes 10420232 | tf_op jit(solution)/shard_map/ppermute | solution.py:47
  (118 other events, 1057.9 us)
Sparse Core Ops, SparseCore 0:
  34.4 64.2 all-gather.14
  108.9 72.1 all-gather.16
  210.8 106.2 all-gather.18
  319.3 96.3 all-gather.24
  418.0 96.3 all-gather.22
  516.6 76.6 all-gather.20
  901.6 51.6 all-gather.26

commit v3 on v2

--- a/solution.py
+++ b/solution.py
@@ -1153,7 +1153,7 @@
 
     shard_hidden = w_gate.shape[1]
     unit = shard_hidden // 35
-    part_rows = [5 * unit, 8 * unit, 8 * unit, 8 * unit, 6 * unit]
+    part_rows = [8 * unit, 8 * unit, 8 * unit, 6 * unit, 5 * unit]
     part_at = [sum(part_rows[:i]) for i in range(len(part_rows))]
     parts = len(part_rows)
     spans = list(zip(part_at, part_rows))
@@ -1163,14 +1163,14 @@
     pieces = pack_weights(spans, core_place, w_gate, w_up, down_halves, given)
     pieces = list(pieces)
 
-    lined_kv = in_order(kv_piece, hold(kv_moves, pieces[0]), place, line)
+    lined_kv = in_order(kv_piece, kv_moves, place, line)
     down_in, gate_out, up_out = (
         order_adapters(spans, line, a.reshape(-1, a.shape[-1]))
         for a in (adapt_down_in, adapt_gate_out, adapt_up_out)
     )
     kv_half = gather_wsh(lined_kv, shard_place)
     kv_own, kv_other = wide(kv_half), wide(swap_cores(kv_half))
-    lined_qo = in_order(qo_piece, qo_moves, place, line)
+    lined_qo = in_order(qo_piece, hold(qo_moves, pieces[0]), place, line)
     qo_half = shard_gather(lined_qo)
 
     def flat(adapters):
@@ -1207,6 +1207,9 @@
         return piece, line_moves(piece, line)
 
     _, moves = set_out([0], lined_qo)
+    take_in(moves, [0], tip(kv_half))
+    piece, moves = set_out([1], lined[0])
+    (kv_own,) = hold([kv_own], piece)
     attn_kv = (core_place, kv_own, kv_other)
     kv_adapters = (key_in, value_in, key_out, value_out)
     normed, rank_k, rank_v, key_value = key_value_side(
@@ -1218,10 +1221,6 @@
     hops.append(hop_up(hops[1], 2, line))
     for t in range(3, line):
         hops.append(hop_up(hops[-1], t, line))
-    take_in(moves, [0], key_value, *down_in, *gate_out, *up_out)
-    _, moves = set_out([1], lined[0])
-    take_in(moves, [1], tip(hops[2]))
-    _, moves = set_out([2], lined[1])
     (qo_half,) = hold([qo_half], tip(hops[2]))
     attn = (core_place, wide(qo_half), wide(swap_cores(qo_half)))
     rank_q, queries = query_side(
@@ -1229,11 +1228,13 @@
     )
     side = prompt_blocks(hops, below, place, line)
     other_side = swap_cores(side)
-    (queries,) = hold([queries], lined[1])
+    take_in(moves, [1], tip(side), *down_in, *gate_out, *up_out)
+    piece, moves = set_out([2], lined[1])
+    (queries,) = hold([queries], piece)
     context, mixed, logs = attend(flags, queries, key_value, side, other_side, mate, kv_heads)
     take_in(moves, [2], context)
-    _, moves = set_out([3], lined[2])
-    (context,) = hold([context], lined[2])
+    piece, moves = set_out([3], lined[2])
+    (context,) = hold([context], piece)
     mid, normed2, grad_out, rank_o, rank_g, rank_u, rank_d = middle_side(
         adapter_of, live, *attn, o_at, context, tokens, cotangent, output_in, output_out, gain_two,
         gate_in, up_in, down_out,
@@ -1297,59 +1298,56 @@
     early_moves = line_send(early_outs, line)
     back.append(slots_back(first_half, slots - first_half, d_context, back[0][0]))
     swapped = swap_cores(back[1][3])
-    *late_moves, late = hold([*late_moves, late], back[1][1])
     folded[0] = hold(folded[0], back[1][1]) if folded[0] else []
     sides.append(add_up([back[1][2], swapped]))
     total = add_up([sides[0]] + folded[0])
-    late = wsh_sum(late, shard_place, late_moves)
-    late_outs = line_outs(late, place, line)
-    early_terms = line_sum(early, place, hold(early_moves, back[1][1]))
-    (d_query,) = hold([back[1][0]], sides[1], total, *late_outs, early_terms)
+    (d_query,) = hold([back[1][0]], sides[1], total)
     folded.append(fold_blocks(sides[1], line))
     came = [return_blocks(sides[0], total, place, line)]
-    late_moves = line_send(late_outs, line)
-    early_moves = line_moves(early_terms, line)
     d_normed_q, query_terms = query_back_side(
         adapter_of, *attn, d_query, normed, rank_q, query_in, query_out
     )
     folded[1] = hold(folded[1], query_terms) if folded[1] else []
     total = add_up([sides[1]] + folded[1])
     came.append(return_blocks(sides[1], total, place, line))
-    early_lined = in_order(early_terms, hold(early_moves, query_terms, tip(total)), place, line)
-    early_half = shard_gather(early_lined)
+    late = wsh_sum(late, shard_place, hold(late_moves, query_terms, tip(total)))
+    late_moves = line_send(line_outs(late, place, line), line)
+    early_terms = line_sum(early, place, hold(early_moves, query_terms, tip(total)))
     came[0] = hold(came[0], query_terms)
     d_kv = jnp.concatenate(
         [b[1] + owned_blocks(p, c, place, line) for b, p, c in zip(back, sides, came)], axis=0
     )
     if mates:
         d_kv = d_kv + swap_cores(jnp.concatenate([b[4] for b in back], axis=0)).astype(f32)
-    late_terms = line_sum(late, place, hold(late_moves, query_terms, tip(total)))
-    (d_kv,) = hold([d_kv], early_lined)
+    (early_terms,) = hold([early_terms], tip(d_kv))
+    early_moves = line_moves(early_terms, line)
+    (d_kv,) = hold([d_kv], early_terms)
     input_grad, kv_terms = output_side(
         adapter_of, live, *attn_kv, 0, d_kv, d_normed_q, d_mid, normed, rank_k, rank_v, tokens, gain_one,
         cosine, sine, kv_adapters,
     )
 
     width_rows = width // (2 * line)
+    early_lined = in_order(early_terms, hold(early_moves, kv_terms), place, line)
+    early_half = shard_gather(early_lined)
+    late_terms = line_sum(late, place, hold(late_moves, kv_terms))
     last_keep = jnp.concatenate([query_terms[0], kv_terms[0]], axis=1)
     last_came = swap_cores(jnp.concatenate([query_terms[1], kv_terms[1]], axis=1))
     last = split_rows(add_up([last_keep, last_came]), shards)
     moves = wsh_send(wsh_outs(last, shard_place))
     last = wsh_sum(last, shard_place, moves)
     moves = line_send(line_outs(last, place, line), line)
-    (early_half,) = hold([early_half], tip(last))
-    early_other = swap_cores(early_half)
     last_terms = line_sum(last, place, moves)
     last_terms = jnp.concatenate([late_terms, last_terms], axis=0)
     last_lined = in_order(last_terms, line_moves(last_terms, line), place, line)
-    last_own = gather_wsh(last_lined, shard_place)
-    last_other = swap_cores(last_own)
-    segments = [
-        (3 * at + i * n, n, i, at) for at, n in spans for i in range(3)
-    ]
+    (early_half,) = hold([early_half], tip(last_lined))
+    early_other = swap_cores(early_half)
+    segments = [(3 * at + i * n, n, i, at) for at, n in spans for i in range(3)]
     g_gate_out, g_up_out, g_down_in = finish(
         core_place, early_half, early_other, (shard_hidden,) * 3, segments
     )
+    last_own = gather_wsh(last_lined, shard_place, (tip(g_gate_out),))
+    last_other = swap_cores(last_own)
     kv_rows = kv_width // (2 * line)
     segments = late_segments(late_terms.shape[0], last_terms.shape[0], 0, (width_rows,) * 5, 0)
     segments += late_segments(

time: 1070 us -> 1040 us (0.972)
  starting transfers between devices: 180 us -> 136 us
  local copies, waits for them, and re-layouts: 82.3 us -> 100 us
    ppermute x48, starting transfers between devices: 161 us -> 116 us  [along_line(): lax.ppermute(array, 'ctx', [(2 * a + c, 2 * b + c) for a, b in pairs for...]
    ppermute x48, waiting for transfers between devices: 136 us -> 156 us  [along_line(): lax.ppermute(array, 'ctx', [(2 * a + c, 2 * b + c) for a, b in pairs for...]
    unnamed x171 -> x173, local copies, waits for them, and re-layouts: 34.7 us -> 40.3 us
    convert_element_type x12 -> x13, other arithmetic: 20.1 us -> 22.2 us  [add_up(): functools.reduce(jnp.add, [a.astype(f32) for a in arrays]).astype(bf16)]
  transfers between devices with their start and end apart: 86 -> 86, of which waited for: 27 -> 27; matrix products, arithmetic and copies ran while one was open for 8% -> 9% of each run, Pallas kernels for 44% -> 49%
where the time goes in v3:
time: 1040 us; the launch traced here: 1030 us
  Pallas kernels  538 us (52%)
  waiting for transfers between devices  206 us (20%)
  starting transfers between devices  136 us (13%)
  local copies, waits for them, and re-layouts  100 us (10%)
  other arithmetic  38 us (4%)
  between operations  16 us (2%)
    pallas_call x6, Pallas kernels, feed_part(): pl.pallas_call(functools.partial(feed_kernel, first, count, 512), grid_sp...  297 us
    ppermute x48, waiting for transfers between devices, along_line(): lax.ppermute(array, 'ctx', [(2 * a + c, 2 * b + c) for a, b in pairs for...  156 us
    ppermute x48, starting transfers between devices, along_line(): lax.ppermute(array, 'ctx', [(2 * a + c, 2 * b + c) for a, b in pairs for...  116 us
    pallas_call x2, Pallas kernels, attend_back(): pl.pallas_call(functools.partial(attend_back_kernel, kv_heads, heads // k...  66 us
    unnamed x173, local copies, waits for them, and re-layouts  40.3 us
    pallas_call x1, Pallas kernels, attend(): pl.pallas_call(functools.partial(attend_kernel, kv_heads, heads // kv_hea...  34.4 us
    pallas_call x1, Pallas kernels, return_side(): pl.pallas_call(functools.partial(return_kernel, first), grid_spec=pltpu.P...  32.6 us
    ppermute x15, waiting for transfers between devices, across(): return lax.ppermute(array, 'wsh', [(i, i ^ by) for i in range(size)])  30 us
  transfers between devices with their start and end apart: 86, of which 27 were waited for; matrix products, arithmetic and copies ran while one was open for 9% of the time, Pallas kernels for 49%

profile of v3, /device:TPU:0, one launch (start us, length us, event | category | flops | bytes accessed | tf_op | source)
XLA Modules:
  0.0 1033.5 jit_solution(1092881526937915320)
XLA Ops:
  24.6 4.0 pack_weights.1
  28.6 8.1 collective-permute-done.1.refs_1_
  41.6 6.8 collective-permute-start.4
  62.4 4.0 collective-permute-done.7
  69.9 4.1 collective-permute-done.9
  74.7 3.3 collective-permute-done.10.refs_0_
  78.0 22.8 %collective-permute-done.11.refs_1_ = bf16[768,384]{1,0:T(8,128)(2,1)} collective-permute-done((bf16[768,384]{1,0:T(8,128)(2,1)}, bf16[768,384]{1,0:T(8,128)(2,1)}, u32[]{:S(2)}, u32[]{:S(2)}) %collective-permute-start.11) | collective-permute-done | bytes 589856 | tf_op jit(solution)/shard_map/ppermute | solution.py:42
  109.5 9.9 key_value_side.1
  123.1 62.9 %collective-permute-done.15 = bf16[4,256,512]{2,1,0:T(8,128)(2,1)} collective-permute-done((bf16[4,256,512]{2,1,0:T(8,128)(2,1)S(1)}, bf16[4,256,512]{2,1,0:T(8,128)(2,1)}, u32[]{:S(2)}, u32[]{:S(2)}) %collective-permute-start.15) | collective-permute-done | bytes 1048608 | tf_op jit(solution)/shard_map/ppermute | solution.py:42
  187.3 3.6 collective-permute-start.17
  193.4 3.9 order_adapters.3
  197.2 3.9 order_adapters.4
  201.1 4.0 order_adapters.5
  205.1 34.0 %collective-permute-done.24 = bf16[4,256,512]{2,1,0:T(8,128)(2,1)} collective-permute-done((bf16[4,256,512]{2,1,0:T(8,128)(2,1)}, bf16[4,256,512]{2,1,0:T(8,128)(2,1)}, u32[]{:S(2)}, u32[]{:S(2)}) %collective-permute-start.24) | collective-permute-done | bytes 1048608 | tf_op jit(solution)/shard_map/ppermute | solution.py:42
  239.1 3.4 select_bitcast_fusion
  243.1 7.4 collective-permute-done.19.refs_2_
  261.8 3.7 collective-permute-start.23
  265.5 13.3 %query_side.1 = (bf16[4,256,128]{2,1,0:T(8,128)(2,1)}, bf16[4,256,1536]{2,1,0:T(8,128)(2,1)}) custom-call(s32[4]{0:T(128)} %fusion.24.adapter, s32[1]{0:T(128)} %bitcast.core, bf16[4,4,384,384]{3,2,1,0:T(8,128)(2,1)} %hold.41.own, bf16[4,4,384,384]{3,2,1,0:T(8,128)(2,1)} %collective-permute-done.16.other, bf16[4,256,1536]{2,1,0:T(8,128)(2,1)} %get-tuple-element.194.normed, ...), custom_call_target="tpu_custom_call" | custom-call | flops 6039797760 | bytes 12000000 | tf_op jit(solution)/shard_map/query_side/pallas_call | solution.py:296
  278.8 34.4 %attend.1 = (bf16[4,256,1536]{2,1,0:T(8,128)(2,1)}, f32[4,12,128,256]{3,2,1,0:T(8,128)}, f32[4,12,256]{2,1,0:T(8,128)}) custom-call(s32[4]{0:T(128)} %add_convert_fusion.6.flags, bf16[4,256,1536]{2,1,0:T(8,128)(2,1)} %hold.44.refs_0_.refs_1_, bf16[4,256,512]{2,1,0:T(8,128)(2,1)} %get-tuple-element.172.refs_1_.refs_2_, ...), custom_call_target="tpu_custom_call" | custom-call | flops 20000000000 | bytes 20000000 | tf_op jit(solution)/shard_map/attend/pallas_call | solution.py:362
  321.2 19.5 %middle_side.1 = (f32[4,256,1536]{2,1,0:T(8,128)}, bf16[4,256,1536]{2,1,0:T(8,128)(2,1)}, bf16[4,256,1536]{2,1,0:T(8,128)(2,1)}, bf16[4,256,128]{2,1,0:T(8,128)(...) custom-call(s32[4]{0:T(128)} %fusion.24.adapter, ...), custom_call_target="tpu_custom_call" | custom-call | flops 7247757312 | bytes 28000000 | tf_op jit(solution)/shard_map/middle_side/pallas_call | solution.py:517
  341.7 3.1 collective-permute-start.26
  347.2 34.2 %feed_part.6 = (f32[4,256,1536]{2,1,0:T(8,128)}, f32[4,256,1536]{2,1,0:T(8,128)}, f32[4,256,128]{2,1,0:T(8,128)}, f32[4,256,128]{2,1,0:T(8,128)}, f32[4,256,128]{2,1,0:T(8,128)}, /*index=5*/bf16[4,768,128]{2,1,0:T(8,128)(2,1)}) custom-call(s32[1]{0:T(128)} %bitcast.core, bf16[4,4,768,384]{3,2,1,0:T(8,128)(2,1)} %hold.48.refs_0_, ...), custom_call_target="tpu_custom_call" | custom-call | flops 32212254720 | bytes 60000000 | tf_op jit(solution)/shard_map/feed_part/pallas_call | solution.py:660
  392.7 64.6 %feed_part.7 = (f32[4,256,1536]{2,1,0:T(8,128)}, f32[4,256,1536]{2,1,0:T(8,128)}, f32[4,256,128]{2,1,0:T(8,128)}, f32[4,256,128]{2,1,0:T(8,128)}, f32[4,256,128]...) custom-call(s32[1]{0:T(128)} %bitcast.core, ...), custom_call_target="tpu_custom_call", output_to_operand_aliasing={{0}: (14, {}), {1}: (15, {}), {2}: (16, {}), {3}: (17, {}),... | custom-call | flops 64424509440 | bytes 60000000 | tf_op jit(solution)/shard_map/feed_part/pallas_call | solution.py:660
  463.4 63.7 %feed_part.8 = (f32[4,256,1536]{2,1,0:T(8,128)}, f32[4,256,1536]{2,1,0:T(8,128)}, f32[4,256,128]{2,1,0:T(8,128)}, f32[4,256,128]{2,1,0:T(8,128)}, f32[4,256,128]...) custom-call(s32[1]{0:T(128)} %bitcast.core, ...), custom_call_target="tpu_custom_call", output_to_operand_aliasing={{0}: (14, {}), {1}: (15, {}), {2}: (16, {}), {3}: (17, {}),... | custom-call | flops 64424509440 | bytes 60000000 | tf_op jit(solution)/shard_map/feed_part/pallas_call | solution.py:660
  527.9 56.5 %feed_part.9 = (f32[4,256,1536]{2,1,0:T(8,128)}, f32[4,256,1536]{2,1,0:T(8,128)}, f32[4,256,128]{2,1,0:T(8,128)}, f32[4,256,128]{2,1,0:T(8,128)}, f32[4,256,128]...) custom-call(s32[1]{0:T(128)} %bitcast.core, ...), custom_call_target="tpu_custom_call", output_to_operand_aliasing={{0}: (14, {}), {1}: (15, {}), {2}: (16, {}), {3}: (17, {}),... | custom-call | flops 56371445760 | bytes 60000000 | tf_op jit(solution)/shard_map/feed_part/pallas_call | solution.py:660
  584.3 12.7 %all-gather.22.cloned.1.call-done = bf16[16,480,384]{2,1,0:T(8,128)(2,1)} async-done(((bf16[4,480,384]{2,1,0:T(8,128)(2,1)}), bf16[16,480,384]{2,1,0:T(8,128)(2,1)}) %all-gather.22.cloned.1.call-update) | async-done | bytes 5898256 | tf_op jit(solution)/shard_map/all_gather | solution.py:83
  601.2 49.0 %feed_part.10 = (f32[4,256,1536]{2,1,0:T(8,128)}, f32[4,256,1536]{2,1,0:T(8,128)}, f32[4,256,128]{2,1,0:T(8,128)}, f32[4,256,128]{2,1,0:T(8,128)}, f32[4,256,128...) custom-call(s32[1]{0:T(128)} %bitcast.core, ...), custom_call_target="tpu_custom_call", output_to_operand_aliasing={{0}: (14, {}), {1}: (15, {}), {2}: (16, {}), {3}: (17, {}),... | custom-call | flops 44291850240 | bytes 60000000 | tf_op jit(solution)/shard_map/feed_part/pallas_call | solution.py:660
  652.2 29.0 %feed_part.11 = (f32[4,256,1536]{2,1,0:T(8,128)}, f32[4,256,1536]{2,1,0:T(8,128)}, f32[4,256,128]{2,1,0:T(8,128)}, f32[4,256,128]{2,1,0:T(8,128)}, f32[4,256,128]{2,1,0:T(8,128)}, /*index=5*/bf16[4,480,128]{2,1,0:T(8,128)(2,1)}) custom-call(s32[1]{0:T(128)} %bitcast.core, ...), custom_call_target="tpu_custom_call", output_to_operand_aliasing={{0}: (10, {}), {1}: (11, {}), {2}: (12, {}), {3}: (13, {}),... | custom-call | flops 20132659200 | bytes 60000000 | tf_op jit(solution)/shard_map/feed_part/pallas_call | solution.py:660
  689.3 32.6 %return_side.1 = (bf16[4,256,1536]{2,1,0:T(8,128)(2,1)}, f32[4,256,1536]{2,1,0:T(8,128)}, bf16[4,256,1536]{2,1,0:T(8,128)(2,1)}, bf16[2,4,960,128]{3,2,1,0:T(8,128)(2,1)}) custom-call(s32[4]{0:T(128)} %fusion.24.adapter, s32[4]{0:T(128)} %convert_element_type.232.live, s32[1]{0:T(128)} %bitcast.core, bf16[4,4,384,384]{3,2,1,0:T(8,128)(2,1)} %hold.41.own, ...), custom_call_target="tpu_custom_call" | custom-call | flops 9663676416 | bytes 50000000 | tf_op jit(solution)/shard_map/return_side/pallas_call | solution.py:771
  726.0 3.9 add_convert_fusion
  735.3 32.8 %attend_back.2 = (bf16[4,256,1536]{2,1,0:T(8,128)(2,1)}, f32[2,256,512]{2,1,0:T(8,128)}, bf16[2,2,256,512]{3,2,1,0:T(8,128)(2,1)}, bf16[2,2,256,512]{3,2,1,0:T(8,128)(2,1)}) custom-call(s32[4]{0:T(128)} %add_convert_fusion.6.flags, bf16[4,256,1536]{2,1,0:T(8,128)(2,1)} %hold.44.refs_0_.refs_1_, bf16[4,256,512]{2,1,0:T(8,128)(2,1)} %get-tuple-element.172.refs_1_.refs_2_, ...), custom_call_target="tpu_custom_call" | custom-call | flops 24999999488 | bytes 20000000 | tf_op jit(solution)/shard_map/attend_back/pallas_call | solution.py:470
  768.7 4.9 collective-permute-done.42.refs_2_
  781.8 3.4 collective-permute-start.39
  785.2 33.2 %attend_back.3 = (bf16[4,256,1536]{2,1,0:T(8,128)(2,1)}, f32[2,256,512]{2,1,0:T(8,128)}, bf16[2,2,256,512]{3,2,1,0:T(8,128)(2,1)}, bf16[2,2,256,512]{3,2,1,0:T(8,128)(2,1)}) custom-call(s32[4]{0:T(128)} %add_convert_fusion.6.flags, bf16[4,256,1536]{2,1,0:T(8,128)(2,1)} %get-tuple-element.262.refs_0_, ...), custom_call_target="tpu_custom_call", output_to_operand_aliasing={{0}: (1, {})} | custom-call | flops 24999999488 | bytes 20000000 | tf_op jit(solution)/shard_map/attend_back/pallas_call | solution.py:470
  834.7 17.4 %query_back_side.1 = (f32[4,256,1536]{2,1,0:T(8,128)}, bf16[2,4,384,128]{3,2,1,0:T(8,128)(2,1)}) custom-call(s32[4]{0:T(128)} %fusion.24.adapter, s32[1]{0:T(128)} %bitcast.core, bf16[4,4,384,384]{3,2,1,0:T(8,128)(2,1)} %hold.41.own, bf16[4,4,384,384]{3,2,1,0:T(8,128)(2,1)} %collective-permute-done.16.other, bf16[4,256,1536]{2,1,0:T(8,128)(2,1)} %hold.61.d_query, ...), custom_call_target="tpu_custom_call" | custom-call | flops 7247757312 | bytes 22000000 | tf_op jit(solution)/shard_map/query_back_side/pallas_call | solution.py:806
  852.2 7.0 collective-permute-start.54
  873.2 12.4 %collective-permute-start.74 = (bf16[848,128]{1,0:T(8,128)(2,1)}, bf16[848,128]{1,0:T(8,128)(2,1)S(1)}, u32[]{:S(2)}, u32[]{:S(2)}) collective-permute-start(bf16[848,128]{1,0:T(8,128)(2,1)} %hold.65.refs_1_), channel_id=1, source_target_pairs={{0,8},{4,12},{8,16},{12,20},{16,24},{20,28},{24,0},{28,4},{1,9},{5... | collective-permute-start | bytes 651272 | tf_op jit(solution)/shard_map/ppermute | solution.py:42
  892.6 15.8 %output_side.1 = (bf16[4,256,1536]{2,1,0:T(8,128)(2,1)}, bf16[2,4,448,128]{3,2,1,0:T(8,128)(2,1)}) custom-call(s32[4]{0:T(128)} %fusion.24.adapter, s32[4]{0:T(128)} %convert_element_type.232.live, s32[1]{0:T(128)} %bitcast.core, bf16[4,4,64,384]{3,2,1,0:T(8,128)(2,1)} %hold.40.own, bf16[4,4,64,384]{3,2,1,0:T(8,128)(2,1)} %collective-permute-done.13.other, ...), custom_call_target="tpu_custom_call" | custom-call | flops 2415919104 | bytes 30000000 | tf_op jit(solution)/shard_map/output_side/pallas_call | solution.py:871
  918.8 5.3 collective-permute-done.55.refs_0_
  924.0 5.2 collective-permute-done.56.refs_1_
  936.9 19.5 %collective-permute-start.58 = (bf16[240,128]{1,0:T(8,128)(2,1)S(1)}, bf16[240,128]{1,0:T(8,128)(2,1)S(1)}, u32[]{:S(2)}, u32[]{:S(2)}) collective-permute-start(bf16[240,128]{1,0:T(8,128)(2,1)S(1)} %get-tuple-element.336), channel_id=1, source_target_pairs={{0,8},{4,12},{8,16},{12,20},{16,24},{20,28},{24,0},{28,4},{1,9},{5... | collective-permute-start | bytes 184328 | tf_op jit(solution)/shard_map/ppermute | solution.py:42
  956.5 4.3 collective-permute-start.59
  967.5 4.8 collective-permute-start.66
  975.0 3.2 collective-permute-done.67
  994.5 9.9 finish.2
  1005.7 6.3 collective-permute-done.72.refs_1_
  1016.1 3.9 collective-permute-done.78.other
  1020.0 6.4 finish.3
  (479 shorter events, 216.0 us)
Async XLA Ops:
  7.2 249.6 %all-gather.16.cloned.1.call-start = ((), (), s32[]{:S(2)}) async-start(), calls=%async_computation.1 | async-start | bytes 5898240 | tf_op jit(solution)/shard_map/all_gather | solution.py:83
  41.5 299.2 %all-gather.18.cloned.1.call-start = ((), (), s32[]{:S(2)}) async-start(), calls=%async_computation.2 | async-start | bytes 11796480 | tf_op jit(solution)/shard_map/all_gather | solution.py:83
  60.5 40.3 %collective-permute-start.11 = (bf16[768,384]{1,0:T(8,128)(2,1)}, bf16[768,384]{1,0:T(8,128)(2,1)}, u32[]{:S(2)}, u32[]{:S(2)}) collective-permute-start(bf16[768,384]{1,0:T(8,128)(2,1)} %hold.37), channel_id=1, source_target_pairs={{0,16},{4,20},{8,24},{12,28},{16,0},{20,4},{24,8},{28,12},{1,17},{... | collective-permute-start | bytes 1769480 | tf_op jit(solution)/shard_map/ppermute | solution.py:42
  66.4 34.4 %collective-permute-start.12 = (bf16[768,384]{1,0:T(8,128)(2,1)}, bf16[768,384]{1,0:T(8,128)(2,1)}, u32[]{:S(2)}, u32[]{:S(2)}) collective-permute-start(bf16[768,384]{1,0:T(8,128)(2,1)} %hold.37), channel_id=1, source_target_pairs={{0,24},{4,28},{8,0},{12,4},{16,8},{20,12},{24,16},{28,20},{1,25},{... | collective-permute-start | bytes 1769480 | tf_op jit(solution)/shard_map/ppermute | solution.py:42
  105.8 287.0 %all-gather.20.cloned.1.call-start = ((), (), s32[]{:S(2)}) async-start(), calls=%async_computation.3 | async-start | bytes 11796480 | tf_op jit(solution)/shard_map/all_gather | solution.py:83
  120.2 65.8 %collective-permute-start.15 = (bf16[4,256,512]{2,1,0:T(8,128)(2,1)S(1)}, bf16[4,256,512]{2,1,0:T(8,128)(2,1)}, u32[]{:S(2)}, u32[]{:S(2)}) collective-permute-start(bf16[4,256,512]{2,1,0:T(8,128)(2,1)S(1)} %collective-permute-done.14), channel_id=1, source_target_pairs={{8,0},{12,4},{16,8},{20,12},{9,1},{13,5},{17,9},{21,13},{10,2},{14... | collective-permute-start | bytes 3145736 | tf_op jit(solution)/shard_map/ppermute | solution.py:42
  121.5 83.6 %collective-permute-start.20 = (bf16[4,256,512]{2,1,0:T(8,128)(2,1)}, bf16[4,256,512]{2,1,0:T(8,128)(2,1)}, u32[]{:S(2)}, u32[]{:S(2)}) collective-permute-start(bf16[4,256,512]{2,1,0:T(8,128)(2,1)} %get-tuple-element.172.refs_1_.refs_2_), channel_id=1, source_target_pairs={{16,24},{20,28},{17,25},{21,29},{18,26},{22,30},{19,27},{23,31}} | collective-permute-start | bytes 3145736 | tf_op jit(solution)/shard_map/ppermute | solution.py:42
  186.0 53.1 %collective-permute-start.24 = (bf16[4,256,512]{2,1,0:T(8,128)(2,1)}, bf16[4,256,512]{2,1,0:T(8,128)(2,1)}, u32[]{:S(2)}, u32[]{:S(2)}) collective-permute-start(bf16[4,256,512]{2,1,0:T(8,128)(2,1)} %collective-permute-done.15), channel_id=1, source_target_pairs={{8,0},{12,4},{9,1},{13,5},{10,2},{14,6},{11,3},{15,7}} | collective-permute-start | bytes 3145736 | tf_op jit(solution)/shard_map/ppermute | solution.py:42
  187.3 55.8 %collective-permute-start.17 = (bf16[768,384]{1,0:T(8,128)(2,1)S(1)}, bf16[768,384]{1,0:T(8,128)(2,1)S(1)}, u32[]{:S(2)}, u32[]{:S(2)}) collective-permute-start(bf16[768,384]{1,0:T(8,128)(2,1)S(1)} %copy-done.15), channel_id=1, source_target_pairs={{0,8},{4,12},{8,16},{12,20},{16,24},{20,28},{24,0},{28,4},{1,9},{5... | collective-permute-start | bytes 1769480 | tf_op jit(solution)/shard_map/ppermute | solution.py:42
  190.9 52.2 %collective-permute-start.18 = (bf16[768,384]{1,0:T(8,128)(2,1)S(1)}, bf16[768,384]{1,0:T(8,128)(2,1)}, u32[]{:S(2)}, u32[]{:S(2)}) collective-permute-start(bf16[768,384]{1,0:T(8,128)(2,1)S(1)} %copy-done.15), channel_id=1, source_target_pairs={{0,16},{4,20},{8,24},{12,28},{16,0},{20,4},{24,8},{28,12},{1,17},{... | collective-permute-start | bytes 1769480 | tf_op jit(solution)/shard_map/ppermute | solution.py:42
  190.9 59.6 %collective-permute-start.19 = (bf16[768,384]{1,0:T(8,128)(2,1)S(1)}, bf16[768,384]{1,0:T(8,128)(2,1)}, u32[]{:S(2)}, u32[]{:S(2)}) collective-permute-start(bf16[768,384]{1,0:T(8,128)(2,1)S(1)} %copy-done.15), channel_id=1, source_target_pairs={{0,24},{4,28},{8,0},{12,4},{16,8},{20,12},{24,16},{28,20},{1,25},{... | collective-permute-start | bytes 1769480 | tf_op jit(solution)/shard_map/ppermute | solution.py:42
  255.5 206.2 %all-gather.26.cloned.1.call-start = ((), (), s32[]{:S(2)}) async-start(), calls=%async_computation.6 | async-start | bytes 11796480 | tf_op jit(solution)/shard_map/all_gather | solution.py:83
  261.4 51.7 %collective-permute-start.21 = (bf16[768,384]{1,0:T(8,128)(2,1)}, bf16[768,384]{1,0:T(8,128)(2,1)S(1)}, u32[]{:S(2)}, u32[]{:S(2)}) collective-permute-start(bf16[768,384]{1,0:T(8,128)(2,1)} %hold.43.refs_1_), channel_id=1, source_target_pairs={{0,8},{4,12},{8,16},{12,20},{16,24},{20,28},{24,0},{28,4},{1,9},{5... | collective-permute-start | bytes 1769480 | tf_op jit(solution)/shard_map/ppermute | solution.py:42
  261.7 51.5 %collective-permute-start.22 = (bf16[768,384]{1,0:T(8,128)(2,1)}, bf16[768,384]{1,0:T(8,128)(2,1)S(1)}, u32[]{:S(2)}, u32[]{:S(2)}) collective-permute-start(bf16[768,384]{1,0:T(8,128)(2,1)} %hold.43.refs_1_), channel_id=1, source_target_pairs={{0,16},{4,20},{8,24},{12,28},{16,0},{20,4},{24,8},{28,12},{1,17},{... | collective-permute-start | bytes 1769480 | tf_op jit(solution)/shard_map/ppermute | solution.py:42
  261.8 51.4 %collective-permute-start.23 = (bf16[768,384]{1,0:T(8,128)(2,1)}, bf16[768,384]{1,0:T(8,128)(2,1)}, u32[]{:S(2)}, u32[]{:S(2)}) collective-permute-start(bf16[768,384]{1,0:T(8,128)(2,1)} %hold.43.refs_1_), channel_id=1, source_target_pairs={{0,24},{4,28},{8,0},{12,4},{16,8},{20,12},{24,16},{28,20},{1,25},{... | collective-permute-start | bytes 1769480 | tf_op jit(solution)/shard_map/ppermute | solution.py:42
  319.1 208.8 %all-gather.24.cloned.1.call-start = ((), (), s32[]{:S(2)}) async-start(), calls=%async_computation.5 | async-start | bytes 8847360 | tf_op jit(solution)/shard_map/all_gather | solution.py:83
  340.7 52.0 %collective-permute-start.32 = (bf16[4,4,768,384]{3,2,1,0:T(8,128)(2,1)}, bf16[4,4,768,384]{3,2,1,0:T(8,128)(2,1)}, u32[]{:S(2)}, u32[]{:S(2)}) collective-permute-start(bf16[4,4,768,384]{3,2,1,0:T(8,128)(2,1)} %hold.48.refs_0_), channel_id=1, source_target_pairs={{0,4},{4,0},{8,12},{12,8},{16,20},{20,16},{24,28},{28,24},{1,5},{5... | collective-permute-start | bytes 28311560 | tf_op jit(solution)/shard_map/ppermute | solution.py:47
  341.7 39.6 %collective-permute-start.26 = (bf16[576,384]{1,0:T(8,128)(2,1)S(1)}, bf16[576,384]{1,0:T(8,128)(2,1)S(1)}, u32[]{:S(2)}, u32[]{:S(2)}) collective-permute-start(bf16[576,384]{1,0:T(8,128)(2,1)S(1)} %copy-done.24), channel_id=1, source_target_pairs={{0,8},{4,12},{8,16},{12,20},{16,24},{20,28},{24,0},{28,4},{1,9},{5... | collective-permute-start | bytes 1327112 | tf_op jit(solution)/shard_map/ppermute | solution.py:42
  344.8 36.6 %collective-permute-start.27 = (bf16[576,384]{1,0:T(8,128)(2,1)S(1)}, bf16[576,384]{1,0:T(8,128)(2,1)S(1)}, u32[]{:S(2)}, u32[]{:S(2)}) collective-permute-start(bf16[576,384]{1,0:T(8,128)(2,1)S(1)} %copy-done.24), channel_id=1, source_target_pairs={{0,16},{4,20},{8,24},{12,28},{16,0},{20,4},{24,8},{28,12},{1,17},{... | collective-permute-start | bytes 1327112 | tf_op jit(solution)/shard_map/ppermute | solution.py:42
  344.8 36.6 %collective-permute-start.28 = (bf16[576,384]{1,0:T(8,128)(2,1)S(1)}, bf16[576,384]{1,0:T(8,128)(2,1)S(1)}, u32[]{:S(2)}, u32[]{:S(2)}) collective-permute-start(bf16[576,384]{1,0:T(8,128)(2,1)S(1)} %copy-done.24), channel_id=1, source_target_pairs={{0,24},{4,28},{8,0},{12,4},{16,8},{20,12},{24,16},{28,20},{1,25},{... | collective-permute-start | bytes 1327112 | tf_op jit(solution)/shard_map/ppermute | solution.py:42
  387.0 210.1 %all-gather.22.cloned.1.call-start = ((), (), s32[]{:S(2)}) async-start(), calls=%async_computation.4 | async-start | bytes 7372800 | tf_op jit(solution)/shard_map/all_gather | solution.py:83
  387.2 70.1 %collective-permute-start.29 = (bf16[480,384]{1,0:T(8,128)(2,1)}, bf16[480,384]{1,0:T(8,128)(2,1)S(1)}, u32[]{:S(2)}, u32[]{:S(2)}) collective-permute-start(bf16[480,384]{1,0:T(8,128)(2,1)} %hold.50), channel_id=1, source_target_pairs={{0,8},{4,12},{8,16},{12,20},{16,24},{20,28},{24,0},{28,4},{1,9},{5... | collective-permute-start | bytes 1105928 | tf_op jit(solution)/shard_map/ppermute | solution.py:42
  390.3 67.1 %collective-permute-start.30 = (bf16[480,384]{1,0:T(8,128)(2,1)}, bf16[480,384]{1,0:T(8,128)(2,1)S(1)}, u32[]{:S(2)}, u32[]{:S(2)}) collective-permute-start(bf16[480,384]{1,0:T(8,128)(2,1)} %hold.50), channel_id=1, source_target_pairs={{0,16},{4,20},{8,24},{12,28},{16,0},{20,4},{24,8},{28,12},{1,17},{... | collective-permute-start | bytes 1105928 | tf_op jit(solution)/shard_map/ppermute | solution.py:42
  392.0 65.4 %collective-permute-start.31 = (bf16[480,384]{1,0:T(8,128)(2,1)}, bf16[480,384]{1,0:T(8,128)(2,1)S(1)}, u32[]{:S(2)}, u32[]{:S(2)}) collective-permute-start(bf16[480,384]{1,0:T(8,128)(2,1)} %hold.50), channel_id=1, source_target_pairs={{0,24},{4,28},{8,0},{12,4},{16,8},{20,12},{24,16},{28,20},{1,25},{... | collective-permute-start | bytes 1105928 | tf_op jit(solution)/shard_map/ppermute | solution.py:42
  392.7 70.6 %collective-permute-start.33 = (bf16[4,4,768,384]{3,2,1,0:T(8,128)(2,1)}, bf16[4,4,768,384]{3,2,1,0:T(8,128)(2,1)}, u32[]{:S(2)}, u32[]{:S(2)}) collective-permute-start(bf16[4,4,768,384]{3,2,1,0:T(8,128)(2,1)} %hold.51.refs_0_), channel_id=1, source_target_pairs={{0,4},{4,0},{8,12},{12,8},{16,20},{20,16},{24,28},{28,24},{1,5},{5... | collective-permute-start | bytes 28311560 | tf_op jit(solution)/shard_map/ppermute | solution.py:47
  462.8 65.1 %collective-permute-start.34 = (bf16[4,4,768,384]{3,2,1,0:T(8,128)(2,1)}, bf16[4,4,768,384]{3,2,1,0:T(8,128)(2,1)}, u32[]{:S(2)}, u32[]{:S(2)}) collective-permute-start(bf16[4,4,768,384]{3,2,1,0:T(8,128)(2,1)} %hold.53.refs_0_), channel_id=1, source_target_pairs={{0,4},{4,0},{8,12},{12,8},{16,20},{20,16},{24,28},{28,24},{1,5},{5... | collective-permute-start | bytes 28311560 | tf_op jit(solution)/shard_map/ppermute | solution.py:47
  463.3 524.7 %all-gather.14.cloned.1.call-start = ((), (), s32[]{:S(2)}) async-start(), calls=%async_computation | async-start | bytes 4341760 | tf_op jit(solution)/shard_map/all_gather | solution.py:83
  527.9 73.4 %collective-permute-start.36 = (bf16[4,4,576,384]{3,2,1,0:T(8,128)(2,1)}, bf16[4,4,576,384]{3,2,1,0:T(8,128)(2,1)}, u32[]{:S(2)}, u32[]{:S(2)}) collective-permute-start(bf16[4,4,576,384]{3,2,1,0:T(8,128)(2,1)} %hold.54.refs_0_), channel_id=1, source_target_pairs={{0,4},{4,0},{8,12},{12,8},{16,20},{20,16},{24,28},{28,24},{1,5},{5... | collective-permute-start | bytes 21233672 | tf_op jit(solution)/shard_map/ppermute | solution.py:47
  597.1 55.1 %collective-permute-start.35 = (bf16[4,4,480,384]{3,2,1,0:T(8,128)(2,1)}, bf16[4,4,480,384]{3,2,1,0:T(8,128)(2,1)}, u32[]{:S(2)}, u32[]{:S(2)}) collective-permute-start(bf16[4,4,480,384]{3,2,1,0:T(8,128)(2,1)} %hold.55.refs_0_), channel_id=1, source_target_pairs={{0,4},{4,0},{8,12},{12,8},{16,20},{20,16},{24,28},{28,24},{1,5},{5... | collective-permute-start | bytes 17694728 | tf_op jit(solution)/shard_map/ppermute | solution.py:47
  683.3 41.0 %collective-permute-start.37 = (bf16[4,3360,128]{2,1,0:T(8,128)(2,1)}, bf16[4,3360,128]{2,1,0:T(8,128)(2,1)S(1)}, u32[]{:S(2)}, u32[]{:S(2)}) collective-permute-start(bf16[4,3360,128]{2,1,0:T(8,128)(2,1)} %constant_dynamic-update-slice_fusion.5), channel_id=1, source_target_pairs={{0,4},{4,0},{8,12},{12,8},{16,20},{20,16},{24,28},{28,24},{1,5},{5... | collective-permute-start | bytes 10321928 | tf_op jit(solution)/shard_map/ppermute | solution.py:47
  731.8 36.9 %collective-permute-start.41 = (bf16[4,848,128]{2,1,0:T(8,128)(2,1)}, bf16[4,848,128]{2,1,0:T(8,128)(2,1)}, u32[]{:S(2)}, u32[]{:S(2)}) collective-permute-start(bf16[4,848,128]{2,1,0:T(8,128)(2,1)} %get-tuple-element.314.refs_2_), channel_id=1, source_target_pairs={{0,1},{1,0},{2,3},{3,2},{4,5},{5,4},{6,7},{7,6},{8,9},{9,8},{10,11... | collective-permute-start | bytes 2605064 | tf_op jit(solution)/shard_map/ppermute | solution.py:108
  733.2 40.3 %collective-permute-start.42 = (bf16[4,848,128]{2,1,0:T(8,128)(2,1)}, bf16[4,848,128]{2,1,0:T(8,128)(2,1)}, u32[]{:S(2)}, u32[]{:S(2)}) collective-permute-start(bf16[4,848,128]{2,1,0:T(8,128)(2,1)} %get-tuple-element.313.refs_3_), channel_id=1, source_target_pairs={{0,2},{1,3},{2,0},{3,1},{4,6},{5,7},{6,4},{7,5},{8,10},{9,11},{10,... | collective-permute-start | bytes 2605064 | tf_op jit(solution)/shard_map/ppermute | solution.py:108
  733.8 39.8 %collective-permute-start.43 = (bf16[4,848,128]{2,1,0:T(8,128)(2,1)}, bf16[4,848,128]{2,1,0:T(8,128)(2,1)}, u32[]{:S(2)}, u32[]{:S(2)}) collective-permute-start(bf16[4,848,128]{2,1,0:T(8,128)(2,1)} %get-tuple-element.312.refs_4_), channel_id=1, source_target_pairs={{0,3},{1,2},{2,1},{3,0},{4,7},{5,6},{6,5},{7,4},{8,11},{9,10},{10,... | collective-permute-start | bytes 2605064 | tf_op jit(solution)/shard_map/ppermute | solution.py:108
  735.3 38.3 %collective-permute-start.40 = (bf16[4,960,128]{2,1,0:T(8,128)(2,1)}, bf16[4,960,128]{2,1,0:T(8,128)(2,1)}, u32[]{:S(2)}, u32[]{:S(2)}) collective-permute-start(bf16[4,960,128]{2,1,0:T(8,128)(2,1)} %get-tuple-element.263), channel_id=1, source_target_pairs={{0,4},{4,0},{8,12},{12,8},{16,20},{20,16},{24,28},{28,24},{1,5},{5... | collective-permute-start | bytes 2949128 | tf_op jit(solution)/shard_map/ppermute | solution.py:47
  781.8 40.2 %collective-permute-start.39 = (bf16[2,2,256,512]{3,2,1,0:T(8,128)(2,1)}, bf16[2,2,256,512]{3,2,1,0:T(8,128)(2,1)S(1)}, u32[]{:S(2)}, u32[]{:S(2)}) collective-permute-start(bf16[2,2,256,512]{3,2,1,0:T(8,128)(2,1)} %add_convert_fusion.4.refs_1_), channel_id=1, source_target_pairs={{0,8},{4,12},{1,9},{5,13},{2,10},{6,14},{3,11},{7,15}} | collective-permute-start | bytes 3145736 | tf_op jit(solution)/shard_map/ppermute | solution.py:42
  818.6 47.6 %collective-permute-start.52 = (bf16[848,128]{1,0:T(8,128)(2,1)}, bf16[848,128]{1,0:T(8,128)(2,1)S(1)}, u32[]{:S(2)}, u32[]{:S(2)}) collective-permute-start(bf16[848,128]{1,0:T(8,128)(2,1)} %get-tuple-element.328.refs_5_), channel_id=1, source_target_pairs={{0,8},{4,12},{8,16},{12,20},{16,24},{20,28},{24,0},{28,4},{1,9},{5... | collective-permute-start | bytes 651272 | tf_op jit(solution)/shard_map/ppermute | solution.py:42
  820.5 31.5 %collective-permute-start.46 = (bf16[2,256,512]{2,1,0:T(8,128)(2,1)}, bf16[2,256,512]{2,1,0:T(8,128)(2,1)}, u32[]{:S(2)}, u32[]{:S(2)}) collective-permute-start(bf16[2,256,512]{2,1,0:T(8,128)(2,1)} %dynamic-slice_bitcast_fusion.4), channel_id=1, source_target_pairs={{24,16},{28,20},{25,17},{29,21},{26,18},{30,22},{27,19},{31,23}} | collective-permute-start | bytes 1572872 | tf_op jit(solution)/shard_map/ppermute | solution.py:42
  827.1 33.6 %collective-permute-start.48 = (bf16[2,2,256,512]{3,2,1,0:T(8,128)(2,1)}, bf16[2,2,256,512]{3,2,1,0:T(8,128)(2,1)S(1)}, u32[]{:S(2)}, u32[]{:S(2)}) collective-permute-start(bf16[2,2,256,512]{3,2,1,0:T(8,128)(2,1)} %add_convert_fusion.2.refs_1_), channel_id=1, source_target_pairs={{0,8},{4,12},{1,9},{5,13},{2,10},{6,14},{3,11},{7,15}} | collective-permute-start | bytes 3145736 | tf_op jit(solution)/shard_map/ppermute | solution.py:42
  832.1 27.2 %collective-permute-start.45 = (bf16[2,256,512]{2,1,0:T(8,128)(2,1)S(1)}, bf16[2,256,512]{2,1,0:T(8,128)(2,1)S(1)}, u32[]{:S(2)}, u32[]{:S(2)}) collective-permute-start(bf16[2,256,512]{2,1,0:T(8,128)(2,1)S(1)} %get-tuple-element.317), channel_id=1, source_target_pairs={{8,24},{12,28},{9,25},{13,29},{10,26},{14,30},{11,27},{15,31}} | collective-permute-start | bytes 1572872 | tf_op jit(solution)/shard_map/ppermute | solution.py:42
  859.3 27.5 %collective-permute-start.51 = (bf16[2,256,512]{2,1,0:T(8,128)(2,1)}, bf16[2,256,512]{2,1,0:T(8,128)(2,1)}, u32[]{:S(2)}, u32[]{:S(2)}) collective-permute-start(bf16[2,256,512]{2,1,0:T(8,128)(2,1)} %dynamic-slice_bitcast_fusion.3), channel_id=1, source_target_pairs={{24,16},{28,20},{25,17},{29,21},{26,18},{30,22},{27,19},{31,23}} | collective-permute-start | bytes 1572872 | tf_op jit(solution)/shard_map/ppermute | solution.py:42
  864.7 24.5 %collective-permute-start.49 = (bf16[2,256,512]{2,1,0:T(8,128)(2,1)}, bf16[2,256,512]{2,1,0:T(8,128)(2,1)}, u32[]{:S(2)}, u32[]{:S(2)}) collective-permute-start(bf16[2,256,512]{2,1,0:T(8,128)(2,1)} %get-tuple-element.319), channel_id=1, source_target_pairs={{8,16},{12,20},{9,17},{13,21},{10,18},{14,22},{11,19},{15,23}} | collective-permute-start | bytes 1572872 | tf_op jit(solution)/shard_map/ppermute | solution.py:42
  866.2 23.0 %collective-permute-start.50 = (bf16[2,256,512]{2,1,0:T(8,128)(2,1)}, bf16[2,256,512]{2,1,0:T(8,128)(2,1)}, u32[]{:S(2)}, u32[]{:S(2)}) collective-permute-start(bf16[2,256,512]{2,1,0:T(8,128)(2,1)} %get-tuple-element.320), channel_id=1, source_target_pairs={{8,24},{12,28},{9,25},{13,29},{10,26},{14,30},{11,27},{15,31}} | collective-permute-start | bytes 1572872 | tf_op jit(solution)/shard_map/ppermute | solution.py:42
  873.2 35.1 %collective-permute-start.74 = (bf16[848,128]{1,0:T(8,128)(2,1)}, bf16[848,128]{1,0:T(8,128)(2,1)S(1)}, u32[]{:S(2)}, u32[]{:S(2)}) collective-permute-start(bf16[848,128]{1,0:T(8,128)(2,1)} %hold.65.refs_1_), channel_id=1, source_target_pairs={{0,8},{4,12},{8,16},{12,20},{16,24},{20,28},{24,0},{28,4},{1,9},{5... | collective-permute-start | bytes 651272 | tf_op jit(solution)/shard_map/ppermute | solution.py:42
  933.4 33.9 %collective-permute-start.62 = (bf16[4,208,128]{2,1,0:T(8,128)(2,1)S(1)}, bf16[4,208,128]{2,1,0:T(8,128)(2,1)S(1)}, u32[]{:S(2)}, u32[]{:S(2)}) collective-permute-start(bf16[4,208,128]{2,1,0:T(8,128)(2,1)S(1)} %get-tuple-element.329), channel_id=1, source_target_pairs={{0,1},{1,0},{2,3},{3,2},{4,5},{5,4},{6,7},{7,6},{8,9},{9,8},{10,11... | collective-permute-start | bytes 638984 | tf_op jit(solution)/shard_map/ppermute | solution.py:108
  934.9 32.4 %collective-permute-start.63 = (bf16[4,208,128]{2,1,0:T(8,128)(2,1)S(1)}, bf16[4,208,128]{2,1,0:T(8,128)(2,1)S(1)}, u32[]{:S(2)}, u32[]{:S(2)}) collective-permute-start(bf16[4,208,128]{2,1,0:T(8,128)(2,1)S(1)} %get-tuple-element.331), channel_id=1, source_target_pairs={{0,2},{1,3},{2,0},{3,1},{4,6},{5,7},{6,4},{7,5},{8,10},{9,11},{10,... | collective-permute-start | bytes 638984 | tf_op jit(solution)/shard_map/ppermute | solution.py:108
  935.5 31.9 %collective-permute-start.64 = (bf16[4,208,128]{2,1,0:T(8,128)(2,1)S(1)}, bf16[4,208,128]{2,1,0:T(8,128)(2,1)S(1)}, u32[]{:S(2)}, u32[]{:S(2)}) collective-permute-start(bf16[4,208,128]{2,1,0:T(8,128)(2,1)S(1)} %get-tuple-element.330), channel_id=1, source_target_pairs={{0,3},{1,2},{2,1},{3,0},{4,7},{5,6},{6,5},{7,4},{8,11},{9,10},{10,... | collective-permute-start | bytes 638984 | tf_op jit(solution)/shard_map/ppermute | solution.py:108
  936.9 25.5 %collective-permute-start.58 = (bf16[240,128]{1,0:T(8,128)(2,1)S(1)}, bf16[240,128]{1,0:T(8,128)(2,1)S(1)}, u32[]{:S(2)}, u32[]{:S(2)}) collective-permute-start(bf16[240,128]{1,0:T(8,128)(2,1)S(1)} %get-tuple-element.336), channel_id=1, source_target_pairs={{0,8},{4,12},{8,16},{12,20},{16,24},{20,28},{24,0},{28,4},{1,9},{5... | collective-permute-start | bytes 184328 | tf_op jit(solution)/shard_map/ppermute | solution.py:42
  989.0 23.0 %collective-permute-start.72 = (bf16[4,448,128]{2,1,0:T(8,128)(2,1)S(1)}, bf16[4,448,128]{2,1,0:T(8,128)(2,1)S(1)}, u32[]{:S(2)}, u32[]{:S(2)}) collective-permute-start(bf16[4,448,128]{2,1,0:T(8,128)(2,1)S(1)} %bitcast_dynamic-update-slice_fusion.36), channel_id=1, source_target_pairs={{0,2},{1,3},{2,0},{3,1},{4,6},{5,7},{6,4},{7,5},{8,10},{9,11},{10,... | collective-permute-start | bytes 1376264 | tf_op jit(solution)/shard_map/ppermute | solution.py:108
  (119 other events, 912.1 us)
Sparse Core Ops, SparseCore 0:
  41.7 68.7 all-gather.15
  112.8 100.1 all-gather.17
  255.6 94.5 all-gather.19
  352.5 96.3 all-gather.25
  451.1 76.6 all-gather.23
  530.1 66.8 all-gather.21
  914.2 67.5 all-gather.13

commit v4 on v3

--- a/solution.py
+++ b/solution.py
@@ -1153,7 +1153,7 @@
 
     shard_hidden = w_gate.shape[1]
     unit = shard_hidden // 35
-    part_rows = [8 * unit, 8 * unit, 8 * unit, 6 * unit, 5 * unit]
+    part_rows = [8 * unit, 8 * unit, 9 * unit, 6 * unit, 4 * unit]
     part_at = [sum(part_rows[:i]) for i in range(len(part_rows))]
     parts = len(part_rows)
     spans = list(zip(part_at, part_rows))

time: 1040 us -> 1030 us (level)
  waiting for transfers between devices: 206 us -> 193 us
    all_gather x7, waiting for transfers between devices: 13.5 us -> 0.09 us  [shard_gather(): return lax.all_gather(lined, 'wsh', axis=0, tiled=False)]
    unnamed x173 -> x171, local copies, waits for them, and re-layouts: 40.3 us -> 39.1 us
  transfers between devices with their start and end apart: 86 -> 86, of which waited for: 27 -> 26; matrix products, arithmetic and copies ran while one was open for 9% -> 9% of each run, Pallas kernels for 49% -> 50%
where the time goes in v4:
time: 1030 us; the launch traced here: 1020 us
  Pallas kernels  539 us (52%)
  waiting for transfers between devices  193 us (19%)
  starting transfers between devices  138 us (13%)
  local copies, waits for them, and re-layouts  98.6 us (10%)
  other arithmetic  38.1 us (4%)
  between operations  16 us (2%)
    pallas_call x6, Pallas kernels, feed_part(): pl.pallas_call(functools.partial(feed_kernel, first, count, 512), grid_sp...  298 us
    ppermute x48, waiting for transfers between devices, along_line(): lax.ppermute(array, 'ctx', [(2 * a + c, 2 * b + c) for a, b in pairs for...  155 us
    ppermute x48, starting transfers between devices, along_line(): lax.ppermute(array, 'ctx', [(2 * a + c, 2 * b + c) for a, b in pairs for...  117 us
    pallas_call x2, Pallas kernels, attend_back(): pl.pallas_call(functools.partial(attend_back_kernel, kv_heads, heads // k...  66.1 us
    unnamed x171, local copies, waits for them, and re-layouts  39.1 us
    pallas_call x1, Pallas kernels, attend(): pl.pallas_call(functools.partial(attend_kernel, kv_heads, heads // kv_hea...  34.3 us
    pallas_call x1, Pallas kernels, return_side(): pl.pallas_call(functools.partial(return_kernel, first), grid_spec=pltpu.P...  32.6 us
    ppermute x15, waiting for transfers between devices, across(): return lax.ppermute(array, 'wsh', [(i, i ^ by) for i in range(size)])  30.8 us
  transfers between devices with their start and end apart: 86, of which 26 were waited for; matrix products, arithmetic and copies ran while one was open for 9% of the time, Pallas kernels for 50%

profile of v4, /device:TPU:0, one launch (start us, length us, event | category | flops | bytes accessed | tf_op | source)
XLA Modules:
  0.0 1022.8 jit_solution(3716175809703372441)
XLA Ops:
  24.6 4.0 pack_weights.1
  28.6 8.0 collective-permute-done.1.refs_1_
  41.6 6.8 collective-permute-start.4
  62.4 4.0 collective-permute-done.7
  69.9 4.1 collective-permute-done.9
  74.7 3.2 collective-permute-done.10.refs_0_
  78.0 22.8 %collective-permute-done.11.refs_1_ = bf16[768,384]{1,0:T(8,128)(2,1)} collective-permute-done((bf16[768,384]{1,0:T(8,128)(2,1)}, bf16[768,384]{1,0:T(8,128)(2,1)}, u32[]{:S(2)}, u32[]{:S(2)}) %collective-permute-start.11) | collective-permute-done | bytes 589856 | tf_op jit(solution)/shard_map/ppermute | solution.py:42
  109.6 9.9 key_value_side.1
  123.3 62.9 %collective-permute-done.15 = bf16[4,256,512]{2,1,0:T(8,128)(2,1)} collective-permute-done((bf16[4,256,512]{2,1,0:T(8,128)(2,1)S(1)}, bf16[4,256,512]{2,1,0:T(8,128)(2,1)}, u32[]{:S(2)}, u32[]{:S(2)}) %collective-permute-start.15) | collective-permute-done | bytes 1048608 | tf_op jit(solution)/shard_map/ppermute | solution.py:42
  187.5 3.6 collective-permute-start.17
  193.5 3.9 order_adapters.3
  197.4 3.9 order_adapters.4
  201.3 3.9 order_adapters.5
  205.1 34.1 %collective-permute-done.24 = bf16[4,256,512]{2,1,0:T(8,128)(2,1)} collective-permute-done((bf16[4,256,512]{2,1,0:T(8,128)(2,1)}, bf16[4,256,512]{2,1,0:T(8,128)(2,1)}, u32[]{:S(2)}, u32[]{:S(2)}) %collective-permute-start.24) | collective-permute-done | bytes 1048608 | tf_op jit(solution)/shard_map/ppermute | solution.py:42
  239.2 3.4 select_bitcast_fusion
  243.2 7.4 collective-permute-done.19.refs_2_
  261.9 3.7 collective-permute-start.23
  265.7 13.2 %query_side.1 = (bf16[4,256,128]{2,1,0:T(8,128)(2,1)}, bf16[4,256,1536]{2,1,0:T(8,128)(2,1)}) custom-call(s32[4]{0:T(128)} %fusion.24.adapter, s32[1]{0:T(128)} %bitcast.core, bf16[4,4,384,384]{3,2,1,0:T(8,128)(2,1)} %hold.41.own, bf16[4,4,384,384]{3,2,1,0:T(8,128)(2,1)} %collective-permute-done.16.other, bf16[4,256,1536]{2,1,0:T(8,128)(2,1)} %get-tuple-element.194.normed, ...), custom_call_target="tpu_custom_call" | custom-call | flops 6039797760 | bytes 12000000 | tf_op jit(solution)/shard_map/query_side/pallas_call | solution.py:296
  278.9 34.3 %attend.1 = (bf16[4,256,1536]{2,1,0:T(8,128)(2,1)}, f32[4,12,128,256]{3,2,1,0:T(8,128)}, f32[4,12,256]{2,1,0:T(8,128)}) custom-call(s32[4]{0:T(128)} %add_convert_fusion.6.flags, bf16[4,256,1536]{2,1,0:T(8,128)(2,1)} %hold.44.refs_0_.refs_1_, bf16[4,256,512]{2,1,0:T(8,128)(2,1)} %get-tuple-element.172.refs_1_.refs_2_, ...), custom_call_target="tpu_custom_call" | custom-call | flops 20000000000 | bytes 20000000 | tf_op jit(solution)/shard_map/attend/pallas_call | solution.py:362
  321.4 19.5 %middle_side.1 = (f32[4,256,1536]{2,1,0:T(8,128)}, bf16[4,256,1536]{2,1,0:T(8,128)(2,1)}, bf16[4,256,1536]{2,1,0:T(8,128)(2,1)}, bf16[4,256,128]{2,1,0:T(8,128)(...) custom-call(s32[4]{0:T(128)} %fusion.24.adapter, ...), custom_call_target="tpu_custom_call" | custom-call | flops 7247757312 | bytes 28000000 | tf_op jit(solution)/shard_map/middle_side/pallas_call | solution.py:517
  342.0 9.6 collective-permute-start.26
  353.9 34.5 %feed_part.6 = (f32[4,256,1536]{2,1,0:T(8,128)}, f32[4,256,1536]{2,1,0:T(8,128)}, f32[4,256,128]{2,1,0:T(8,128)}, f32[4,256,128]{2,1,0:T(8,128)}, f32[4,256,128]{2,1,0:T(8,128)}, /*index=5*/bf16[4,768,128]{2,1,0:T(8,128)(2,1)}) custom-call(s32[1]{0:T(128)} %bitcast.core, bf16[4,4,768,384]{3,2,1,0:T(8,128)(2,1)} %hold.48.refs_0_, ...), custom_call_target="tpu_custom_call" | custom-call | flops 32212254720 | bytes 60000000 | tf_op jit(solution)/shard_map/feed_part/pallas_call | solution.py:660
  395.3 3.4 collective-permute-start.30
  398.7 64.9 %feed_part.7 = (f32[4,256,1536]{2,1,0:T(8,128)}, f32[4,256,1536]{2,1,0:T(8,128)}, f32[4,256,128]{2,1,0:T(8,128)}, f32[4,256,128]{2,1,0:T(8,128)}, f32[4,256,128]...) custom-call(s32[1]{0:T(128)} %bitcast.core, ...), custom_call_target="tpu_custom_call", output_to_operand_aliasing={{0}: (14, {}), {1}: (15, {}), {2}: (16, {}), {3}: (17, {}),... | custom-call | flops 64424509440 | bytes 60000000 | tf_op jit(solution)/shard_map/feed_part/pallas_call | solution.py:660
  469.2 70.4 %feed_part.8 = (f32[4,256,1536]{2,1,0:T(8,128)}, f32[4,256,1536]{2,1,0:T(8,128)}, f32[4,256,128]{2,1,0:T(8,128)}, f32[4,256,128]{2,1,0:T(8,128)}, f32[4,256,128]...) custom-call(s32[1]{0:T(128)} %bitcast.core, ...), custom_call_target="tpu_custom_call", output_to_operand_aliasing={{0}: (14, {}), {1}: (15, {}), {2}: (16, {}), {3}: (17, {}),... | custom-call | flops 68451041280 | bytes 60000000 | tf_op jit(solution)/shard_map/feed_part/pallas_call | solution.py:660
  539.9 62.9 %feed_part.9 = (f32[4,256,1536]{2,1,0:T(8,128)}, f32[4,256,1536]{2,1,0:T(8,128)}, f32[4,256,128]{2,1,0:T(8,128)}, f32[4,256,128]{2,1,0:T(8,128)}, f32[4,256,128]...) custom-call(s32[1]{0:T(128)} %bitcast.core, ...), custom_call_target="tpu_custom_call", output_to_operand_aliasing={{0}: (14, {}), {1}: (15, {}), {2}: (16, {}), {3}: (17, {}),... | custom-call | flops 60397977600 | bytes 60000000 | tf_op jit(solution)/shard_map/feed_part/pallas_call | solution.py:660
  607.0 42.8 %feed_part.10 = (f32[4,256,1536]{2,1,0:T(8,128)}, f32[4,256,1536]{2,1,0:T(8,128)}, f32[4,256,128]{2,1,0:T(8,128)}, f32[4,256,128]{2,1,0:T(8,128)}, f32[4,256,128...) custom-call(s32[1]{0:T(128)} %bitcast.core, ...), custom_call_target="tpu_custom_call", output_to_operand_aliasing={{0}: (14, {}), {1}: (15, {}), {2}: (16, {}), {3}: (17, {}),... | custom-call | flops 40265318400 | bytes 60000000 | tf_op jit(solution)/shard_map/feed_part/pallas_call | solution.py:660
  651.9 22.8 %feed_part.11 = (f32[4,256,1536]{2,1,0:T(8,128)}, f32[4,256,1536]{2,1,0:T(8,128)}, f32[4,256,128]{2,1,0:T(8,128)}, f32[4,256,128]{2,1,0:T(8,128)}, f32[4,256,128]{2,1,0:T(8,128)}, /*index=5*/bf16[4,384,128]{2,1,0:T(8,128)(2,1)}) custom-call(s32[1]{0:T(128)} %bitcast.core, ...), custom_call_target="tpu_custom_call", output_to_operand_aliasing={{0}: (10, {}), {1}: (11, {}), {2}: (12, {}), {3}: (13, {}),... | custom-call | flops 16106127360 | bytes 60000000 | tf_op jit(solution)/shard_map/feed_part/pallas_call | solution.py:660
  683.1 32.6 %return_side.1 = (bf16[4,256,1536]{2,1,0:T(8,128)(2,1)}, f32[4,256,1536]{2,1,0:T(8,128)}, bf16[4,256,1536]{2,1,0:T(8,128)(2,1)}, bf16[2,4,960,128]{3,2,1,0:T(8,128)(2,1)}) custom-call(s32[4]{0:T(128)} %fusion.24.adapter, s32[4]{0:T(128)} %convert_element_type.232.live, s32[1]{0:T(128)} %bitcast.core, bf16[4,4,384,384]{3,2,1,0:T(8,128)(2,1)} %hold.41.own, ...), custom_call_target="tpu_custom_call" | custom-call | flops 9663676416 | bytes 50000000 | tf_op jit(solution)/shard_map/return_side/pallas_call | solution.py:771
  719.8 3.9 add_convert_fusion
  728.9 32.8 %attend_back.2 = (bf16[4,256,1536]{2,1,0:T(8,128)(2,1)}, f32[2,256,512]{2,1,0:T(8,128)}, bf16[2,2,256,512]{3,2,1,0:T(8,128)(2,1)}, bf16[2,2,256,512]{3,2,1,0:T(8,128)(2,1)}) custom-call(s32[4]{0:T(128)} %add_convert_fusion.6.flags, bf16[4,256,1536]{2,1,0:T(8,128)(2,1)} %hold.44.refs_0_.refs_1_, bf16[4,256,512]{2,1,0:T(8,128)(2,1)} %get-tuple-element.172.refs_1_.refs_2_, ...), custom_call_target="tpu_custom_call" | custom-call | flops 24999999488 | bytes 20000000 | tf_op jit(solution)/shard_map/attend_back/pallas_call | solution.py:470
  762.3 4.6 collective-permute-done.42.refs_2_
  775.2 3.8 collective-permute-start.39
  779.0 33.2 %attend_back.3 = (bf16[4,256,1536]{2,1,0:T(8,128)(2,1)}, f32[2,256,512]{2,1,0:T(8,128)}, bf16[2,2,256,512]{3,2,1,0:T(8,128)(2,1)}, bf16[2,2,256,512]{3,2,1,0:T(8,128)(2,1)}) custom-call(s32[4]{0:T(128)} %add_convert_fusion.6.flags, bf16[4,256,1536]{2,1,0:T(8,128)(2,1)} %get-tuple-element.262.refs_0_, ...), custom_call_target="tpu_custom_call", output_to_operand_aliasing={{0}: (1, {})} | custom-call | flops 24999999488 | bytes 20000000 | tf_op jit(solution)/shard_map/attend_back/pallas_call | solution.py:470
  827.6 17.4 %query_back_side.1 = (f32[4,256,1536]{2,1,0:T(8,128)}, bf16[2,4,384,128]{3,2,1,0:T(8,128)(2,1)}) custom-call(s32[4]{0:T(128)} %fusion.24.adapter, s32[1]{0:T(128)} %bitcast.core, bf16[4,4,384,384]{3,2,1,0:T(8,128)(2,1)} %hold.41.own, bf16[4,4,384,384]{3,2,1,0:T(8,128)(2,1)} %collective-permute-done.16.other, bf16[4,256,1536]{2,1,0:T(8,128)(2,1)} %hold.61.d_query, ...), custom_call_target="tpu_custom_call" | custom-call | flops 7247757312 | bytes 22000000 | tf_op jit(solution)/shard_map/query_back_side/pallas_call | solution.py:806
  845.1 7.9 collective-permute-start.54
  867.1 5.9 collective-permute-start.74
  879.8 15.8 %output_side.1 = (bf16[4,256,1536]{2,1,0:T(8,128)(2,1)}, bf16[2,4,448,128]{3,2,1,0:T(8,128)(2,1)}) custom-call(s32[4]{0:T(128)} %fusion.24.adapter, s32[4]{0:T(128)} %convert_element_type.232.live, s32[1]{0:T(128)} %bitcast.core, bf16[4,4,64,384]{3,2,1,0:T(8,128)(2,1)} %hold.40.own, bf16[4,4,64,384]{3,2,1,0:T(8,128)(2,1)} %collective-permute-done.13.other, ...), custom_call_target="tpu_custom_call" | custom-call | flops 2415919104 | bytes 30000000 | tf_op jit(solution)/shard_map/output_side/pallas_call | solution.py:871
  906.0 5.3 collective-permute-done.55.refs_0_
  911.3 4.3 collective-permute-done.56.refs_1_
  924.2 22.0 %collective-permute-start.58 = (bf16[240,128]{1,0:T(8,128)(2,1)S(1)}, bf16[240,128]{1,0:T(8,128)(2,1)S(1)}, u32[]{:S(2)}, u32[]{:S(2)}) collective-permute-start(bf16[240,128]{1,0:T(8,128)(2,1)S(1)} %get-tuple-element.336), channel_id=1, source_target_pairs={{0,8},{4,12},{8,16},{12,20},{16,24},{20,28},{24,0},{28,4},{1,9},{5... | collective-permute-start | bytes 184328 | tf_op jit(solution)/shard_map/ppermute | solution.py:42
  946.2 4.3 collective-permute-start.59
  957.3 4.4 collective-permute-start.66
  964.5 3.4 collective-permute-done.67
  983.3 9.9 finish.2
  994.5 6.8 collective-permute-done.72.refs_1_
  1005.4 3.9 collective-permute-done.78.other
  1009.3 6.4 finish.3
  (477 shorter events, 210.1 us)
Async XLA Ops:
  7.2 249.7 %all-gather.16.cloned.1.call-start = ((), (), s32[]{:S(2)}) async-start(), calls=%async_computation.1 | async-start | bytes 5898240 | tf_op jit(solution)/shard_map/all_gather | solution.py:83
  14.0 22.7 %collective-permute-start.1 = (bf16[384,384]{1,0:T(8,128)(2,1)}, bf16[384,384]{1,0:T(8,128)(2,1)S(1)}, u32[]{:S(2)}, u32[]{:S(2)}) collective-permute-start(bf16[384,384]{1,0:T(8,128)(2,1)} %pad_maximum_fusion.3), channel_id=1, source_target_pairs={{0,16},{4,20},{8,24},{12,28},{16,0},{20,4},{24,8},{28,12},{1,17},{... | collective-permute-start | bytes 884744 | tf_op jit(solution)/shard_map/ppermute | solution.py:42
  41.5 299.4 %all-gather.18.cloned.1.call-start = ((), (), s32[]{:S(2)}) async-start(), calls=%async_computation.2 | async-start | bytes 11796480 | tf_op jit(solution)/shard_map/all_gather | solution.py:83
  60.5 40.3 %collective-permute-start.11 = (bf16[768,384]{1,0:T(8,128)(2,1)}, bf16[768,384]{1,0:T(8,128)(2,1)}, u32[]{:S(2)}, u32[]{:S(2)}) collective-permute-start(bf16[768,384]{1,0:T(8,128)(2,1)} %hold.37), channel_id=1, source_target_pairs={{0,16},{4,20},{8,24},{12,28},{16,0},{20,4},{24,8},{28,12},{1,17},{... | collective-permute-start | bytes 1769480 | tf_op jit(solution)/shard_map/ppermute | solution.py:42
  66.4 34.4 %collective-permute-start.12 = (bf16[768,384]{1,0:T(8,128)(2,1)}, bf16[768,384]{1,0:T(8,128)(2,1)}, u32[]{:S(2)}, u32[]{:S(2)}) collective-permute-start(bf16[768,384]{1,0:T(8,128)(2,1)} %hold.37), channel_id=1, source_target_pairs={{0,24},{4,28},{8,0},{12,4},{16,8},{20,12},{24,16},{28,20},{1,25},{... | collective-permute-start | bytes 1769480 | tf_op jit(solution)/shard_map/ppermute | solution.py:42
  105.8 292.9 %all-gather.20.cloned.1.call-start = ((), (), s32[]{:S(2)}) async-start(), calls=%async_computation.3 | async-start | bytes 11796480 | tf_op jit(solution)/shard_map/all_gather | solution.py:83
  120.3 65.9 %collective-permute-start.15 = (bf16[4,256,512]{2,1,0:T(8,128)(2,1)S(1)}, bf16[4,256,512]{2,1,0:T(8,128)(2,1)}, u32[]{:S(2)}, u32[]{:S(2)}) collective-permute-start(bf16[4,256,512]{2,1,0:T(8,128)(2,1)S(1)} %collective-permute-done.14), channel_id=1, source_target_pairs={{8,0},{12,4},{16,8},{20,12},{9,1},{13,5},{17,9},{21,13},{10,2},{14... | collective-permute-start | bytes 3145736 | tf_op jit(solution)/shard_map/ppermute | solution.py:42
  121.6 83.5 %collective-permute-start.20 = (bf16[4,256,512]{2,1,0:T(8,128)(2,1)}, bf16[4,256,512]{2,1,0:T(8,128)(2,1)}, u32[]{:S(2)}, u32[]{:S(2)}) collective-permute-start(bf16[4,256,512]{2,1,0:T(8,128)(2,1)} %get-tuple-element.172.refs_1_.refs_2_), channel_id=1, source_target_pairs={{16,24},{20,28},{17,25},{21,29},{18,26},{22,30},{19,27},{23,31}} | collective-permute-start | bytes 3145736 | tf_op jit(solution)/shard_map/ppermute | solution.py:42
  186.2 53.1 %collective-permute-start.24 = (bf16[4,256,512]{2,1,0:T(8,128)(2,1)}, bf16[4,256,512]{2,1,0:T(8,128)(2,1)}, u32[]{:S(2)}, u32[]{:S(2)}) collective-permute-start(bf16[4,256,512]{2,1,0:T(8,128)(2,1)} %collective-permute-done.15), channel_id=1, source_target_pairs={{8,0},{12,4},{9,1},{13,5},{10,2},{14,6},{11,3},{15,7}} | collective-permute-start | bytes 3145736 | tf_op jit(solution)/shard_map/ppermute | solution.py:42
  187.5 55.8 %collective-permute-start.17 = (bf16[768,384]{1,0:T(8,128)(2,1)S(1)}, bf16[768,384]{1,0:T(8,128)(2,1)S(1)}, u32[]{:S(2)}, u32[]{:S(2)}) collective-permute-start(bf16[768,384]{1,0:T(8,128)(2,1)S(1)} %copy-done.15), channel_id=1, source_target_pairs={{0,8},{4,12},{8,16},{12,20},{16,24},{20,28},{24,0},{28,4},{1,9},{5... | collective-permute-start | bytes 1769480 | tf_op jit(solution)/shard_map/ppermute | solution.py:42
  191.1 52.2 %collective-permute-start.18 = (bf16[768,384]{1,0:T(8,128)(2,1)S(1)}, bf16[768,384]{1,0:T(8,128)(2,1)}, u32[]{:S(2)}, u32[]{:S(2)}) collective-permute-start(bf16[768,384]{1,0:T(8,128)(2,1)S(1)} %copy-done.15), channel_id=1, source_target_pairs={{0,16},{4,20},{8,24},{12,28},{16,0},{20,4},{24,8},{28,12},{1,17},{... | collective-permute-start | bytes 1769480 | tf_op jit(solution)/shard_map/ppermute | solution.py:42
  191.1 59.6 %collective-permute-start.19 = (bf16[768,384]{1,0:T(8,128)(2,1)S(1)}, bf16[768,384]{1,0:T(8,128)(2,1)}, u32[]{:S(2)}, u32[]{:S(2)}) collective-permute-start(bf16[768,384]{1,0:T(8,128)(2,1)S(1)} %copy-done.15), channel_id=1, source_target_pairs={{0,24},{4,28},{8,0},{12,4},{16,8},{20,12},{24,16},{28,20},{1,25},{... | collective-permute-start | bytes 1769480 | tf_op jit(solution)/shard_map/ppermute | solution.py:42
  255.6 212.1 %all-gather.26.cloned.1.call-start = ((), (), s32[]{:S(2)}) async-start(), calls=%async_computation.6 | async-start | bytes 13271040 | tf_op jit(solution)/shard_map/all_gather | solution.py:83
  261.6 51.7 %collective-permute-start.21 = (bf16[864,384]{1,0:T(8,128)(2,1)}, bf16[864,384]{1,0:T(8,128)(2,1)S(1)}, u32[]{:S(2)}, u32[]{:S(2)}) collective-permute-start(bf16[864,384]{1,0:T(8,128)(2,1)} %hold.43.refs_1_), channel_id=1, source_target_pairs={{0,8},{4,12},{8,16},{12,20},{16,24},{20,28},{24,0},{28,4},{1,9},{5... | collective-permute-start | bytes 1990664 | tf_op jit(solution)/shard_map/ppermute | solution.py:42
  261.8 51.5 %collective-permute-start.22 = (bf16[864,384]{1,0:T(8,128)(2,1)}, bf16[864,384]{1,0:T(8,128)(2,1)}, u32[]{:S(2)}, u32[]{:S(2)}) collective-permute-start(bf16[864,384]{1,0:T(8,128)(2,1)} %hold.43.refs_1_), channel_id=1, source_target_pairs={{0,16},{4,20},{8,24},{12,28},{16,0},{20,4},{24,8},{28,12},{1,17},{... | collective-permute-start | bytes 1990664 | tf_op jit(solution)/shard_map/ppermute | solution.py:42
  261.9 51.4 %collective-permute-start.23 = (bf16[864,384]{1,0:T(8,128)(2,1)}, bf16[864,384]{1,0:T(8,128)(2,1)}, u32[]{:S(2)}, u32[]{:S(2)}) collective-permute-start(bf16[864,384]{1,0:T(8,128)(2,1)} %hold.43.refs_1_), channel_id=1, source_target_pairs={{0,24},{4,28},{8,0},{12,4},{16,8},{20,12},{24,16},{28,20},{1,25},{... | collective-permute-start | bytes 1990664 | tf_op jit(solution)/shard_map/ppermute | solution.py:42
  319.3 220.4 %all-gather.24.cloned.1.call-start = ((), (), s32[]{:S(2)}) async-start(), calls=%async_computation.5 | async-start | bytes 8847360 | tf_op jit(solution)/shard_map/all_gather | solution.py:83
  341.0 57.8 %collective-permute-start.32 = (bf16[4,4,768,384]{3,2,1,0:T(8,128)(2,1)}, bf16[4,4,768,384]{3,2,1,0:T(8,128)(2,1)}, u32[]{:S(2)}, u32[]{:S(2)}) collective-permute-start(bf16[4,4,768,384]{3,2,1,0:T(8,128)(2,1)} %hold.48.refs_0_), channel_id=1, source_target_pairs={{0,4},{4,0},{8,12},{12,8},{16,20},{20,16},{24,28},{28,24},{1,5},{5... | collective-permute-start | bytes 28311560 | tf_op jit(solution)/shard_map/ppermute | solution.py:47
  342.0 46.5 %collective-permute-start.26 = (bf16[576,384]{1,0:T(8,128)(2,1)S(1)}, bf16[576,384]{1,0:T(8,128)(2,1)S(1)}, u32[]{:S(2)}, u32[]{:S(2)}) collective-permute-start(bf16[576,384]{1,0:T(8,128)(2,1)S(1)} %copy-done.24), channel_id=1, source_target_pairs={{0,8},{4,12},{8,16},{12,20},{16,24},{20,28},{24,0},{28,4},{1,9},{5... | collective-permute-start | bytes 1327112 | tf_op jit(solution)/shard_map/ppermute | solution.py:42
  351.5 36.9 %collective-permute-start.27 = (bf16[576,384]{1,0:T(8,128)(2,1)S(1)}, bf16[576,384]{1,0:T(8,128)(2,1)S(1)}, u32[]{:S(2)}, u32[]{:S(2)}) collective-permute-start(bf16[576,384]{1,0:T(8,128)(2,1)S(1)} %copy-done.24), channel_id=1, source_target_pairs={{0,16},{4,20},{8,24},{12,28},{16,0},{20,4},{24,8},{28,12},{1,17},{... | collective-permute-start | bytes 1327112 | tf_op jit(solution)/shard_map/ppermute | solution.py:42
  351.5 36.9 %collective-permute-start.28 = (bf16[576,384]{1,0:T(8,128)(2,1)S(1)}, bf16[576,384]{1,0:T(8,128)(2,1)S(1)}, u32[]{:S(2)}, u32[]{:S(2)}) collective-permute-start(bf16[576,384]{1,0:T(8,128)(2,1)S(1)} %copy-done.24), channel_id=1, source_target_pairs={{0,24},{4,28},{8,0},{12,4},{16,8},{20,12},{24,16},{28,20},{1,25},{... | collective-permute-start | bytes 1327112 | tf_op jit(solution)/shard_map/ppermute | solution.py:42
  394.0 208.7 %all-gather.22.cloned.1.call-start = ((), (), s32[]{:S(2)}) async-start(), calls=%async_computation.4 | async-start | bytes 5898240 | tf_op jit(solution)/shard_map/all_gather | solution.py:83
  394.3 69.4 %collective-permute-start.29 = (bf16[384,384]{1,0:T(8,128)(2,1)}, bf16[384,384]{1,0:T(8,128)(2,1)S(1)}, u32[]{:S(2)}, u32[]{:S(2)}) collective-permute-start(bf16[384,384]{1,0:T(8,128)(2,1)} %hold.50), channel_id=1, source_target_pairs={{0,8},{4,12},{8,16},{12,20},{16,24},{20,28},{24,0},{28,4},{1,9},{5... | collective-permute-start | bytes 884744 | tf_op jit(solution)/shard_map/ppermute | solution.py:42
  395.3 68.4 %collective-permute-start.30 = (bf16[384,384]{1,0:T(8,128)(2,1)}, bf16[384,384]{1,0:T(8,128)(2,1)S(1)}, u32[]{:S(2)}, u32[]{:S(2)}) collective-permute-start(bf16[384,384]{1,0:T(8,128)(2,1)} %hold.50), channel_id=1, source_target_pairs={{0,16},{4,20},{8,24},{12,28},{16,0},{20,4},{24,8},{28,12},{1,17},{... | collective-permute-start | bytes 884744 | tf_op jit(solution)/shard_map/ppermute | solution.py:42
  398.7 65.0 %collective-permute-start.31 = (bf16[384,384]{1,0:T(8,128)(2,1)}, bf16[384,384]{1,0:T(8,128)(2,1)S(1)}, u32[]{:S(2)}, u32[]{:S(2)}) collective-permute-start(bf16[384,384]{1,0:T(8,128)(2,1)} %hold.50), channel_id=1, source_target_pairs={{0,24},{4,28},{8,0},{12,4},{16,8},{20,12},{24,16},{28,20},{1,25},{... | collective-permute-start | bytes 884744 | tf_op jit(solution)/shard_map/ppermute | solution.py:42
  398.7 70.5 %collective-permute-start.33 = (bf16[4,4,768,384]{3,2,1,0:T(8,128)(2,1)}, bf16[4,4,768,384]{3,2,1,0:T(8,128)(2,1)}, u32[]{:S(2)}, u32[]{:S(2)}) collective-permute-start(bf16[4,4,768,384]{3,2,1,0:T(8,128)(2,1)} %hold.51.refs_0_), channel_id=1, source_target_pairs={{0,4},{4,0},{8,12},{12,8},{16,20},{20,16},{24,28},{28,24},{1,5},{5... | collective-permute-start | bytes 28311560 | tf_op jit(solution)/shard_map/ppermute | solution.py:47
  468.7 71.2 %collective-permute-start.34 = (bf16[4,4,864,384]{3,2,1,0:T(8,128)(2,1)}, bf16[4,4,864,384]{3,2,1,0:T(8,128)(2,1)}, u32[]{:S(2)}, u32[]{:S(2)}) collective-permute-start(bf16[4,4,864,384]{3,2,1,0:T(8,128)(2,1)} %hold.53.refs_0_), channel_id=1, source_target_pairs={{0,4},{4,0},{8,12},{12,8},{16,20},{20,16},{24,28},{28,24},{1,5},{5... | collective-permute-start | bytes 31850504 | tf_op jit(solution)/shard_map/ppermute | solution.py:47
  469.1 507.7 %all-gather.14.cloned.1.call-start = ((), (), s32[]{:S(2)}) async-start(), calls=%async_computation | async-start | bytes 4341760 | tf_op jit(solution)/shard_map/all_gather | solution.py:83
  539.7 67.4 %collective-permute-start.36 = (bf16[4,4,576,384]{3,2,1,0:T(8,128)(2,1)}, bf16[4,4,576,384]{3,2,1,0:T(8,128)(2,1)}, u32[]{:S(2)}, u32[]{:S(2)}) collective-permute-start(bf16[4,4,576,384]{3,2,1,0:T(8,128)(2,1)} %hold.54.refs_0_), channel_id=1, source_target_pairs={{0,4},{4,0},{8,12},{12,8},{16,20},{20,16},{24,28},{28,24},{1,5},{5... | collective-permute-start | bytes 21233672 | tf_op jit(solution)/shard_map/ppermute | solution.py:47
  602.8 49.0 %collective-permute-start.35 = (bf16[4,4,384,384]{3,2,1,0:T(8,128)(2,1)}, bf16[4,4,384,384]{3,2,1,0:T(8,128)(2,1)}, u32[]{:S(2)}, u32[]{:S(2)}) collective-permute-start(bf16[4,4,384,384]{3,2,1,0:T(8,128)(2,1)} %hold.55.refs_0_), channel_id=1, source_target_pairs={{0,4},{4,0},{8,12},{12,8},{16,20},{20,16},{24,28},{28,24},{1,5},{5... | collective-permute-start | bytes 14155784 | tf_op jit(solution)/shard_map/ppermute | solution.py:47
  676.7 41.3 %collective-permute-start.37 = (bf16[4,3360,128]{2,1,0:T(8,128)(2,1)}, bf16[4,3360,128]{2,1,0:T(8,128)(2,1)S(1)}, u32[]{:S(2)}, u32[]{:S(2)}) collective-permute-start(bf16[4,3360,128]{2,1,0:T(8,128)(2,1)} %constant_dynamic-update-slice_fusion.5), channel_id=1, source_target_pairs={{0,4},{4,0},{8,12},{12,8},{16,20},{20,16},{24,28},{28,24},{1,5},{5... | collective-permute-start | bytes 10321928 | tf_op jit(solution)/shard_map/ppermute | solution.py:47
  725.4 36.9 %collective-permute-start.41 = (bf16[4,848,128]{2,1,0:T(8,128)(2,1)}, bf16[4,848,128]{2,1,0:T(8,128)(2,1)}, u32[]{:S(2)}, u32[]{:S(2)}) collective-permute-start(bf16[4,848,128]{2,1,0:T(8,128)(2,1)} %get-tuple-element.314.refs_2_), channel_id=1, source_target_pairs={{0,1},{1,0},{2,3},{3,2},{4,5},{5,4},{6,7},{7,6},{8,9},{9,8},{10,11... | collective-permute-start | bytes 2605064 | tf_op jit(solution)/shard_map/ppermute | solution.py:108
  727.1 39.9 %collective-permute-start.42 = (bf16[4,848,128]{2,1,0:T(8,128)(2,1)}, bf16[4,848,128]{2,1,0:T(8,128)(2,1)}, u32[]{:S(2)}, u32[]{:S(2)}) collective-permute-start(bf16[4,848,128]{2,1,0:T(8,128)(2,1)} %get-tuple-element.313.refs_3_), channel_id=1, source_target_pairs={{0,2},{1,3},{2,0},{3,1},{4,6},{5,7},{6,4},{7,5},{8,10},{9,11},{10,... | collective-permute-start | bytes 2605064 | tf_op jit(solution)/shard_map/ppermute | solution.py:108
  728.6 38.3 %collective-permute-start.43 = (bf16[4,848,128]{2,1,0:T(8,128)(2,1)}, bf16[4,848,128]{2,1,0:T(8,128)(2,1)}, u32[]{:S(2)}, u32[]{:S(2)}) collective-permute-start(bf16[4,848,128]{2,1,0:T(8,128)(2,1)} %get-tuple-element.312.refs_4_), channel_id=1, source_target_pairs={{0,3},{1,2},{2,1},{3,0},{4,7},{5,6},{6,5},{7,4},{8,11},{9,10},{10,... | collective-permute-start | bytes 2605064 | tf_op jit(solution)/shard_map/ppermute | solution.py:108
  728.9 38.0 %collective-permute-start.40 = (bf16[4,960,128]{2,1,0:T(8,128)(2,1)}, bf16[4,960,128]{2,1,0:T(8,128)(2,1)}, u32[]{:S(2)}, u32[]{:S(2)}) collective-permute-start(bf16[4,960,128]{2,1,0:T(8,128)(2,1)} %get-tuple-element.263), channel_id=1, source_target_pairs={{0,4},{4,0},{8,12},{12,8},{16,20},{20,16},{24,28},{28,24},{1,5},{5... | collective-permute-start | bytes 2949128 | tf_op jit(solution)/shard_map/ppermute | solution.py:47
  775.2 40.5 %collective-permute-start.39 = (bf16[2,2,256,512]{3,2,1,0:T(8,128)(2,1)}, bf16[2,2,256,512]{3,2,1,0:T(8,128)(2,1)S(1)}, u32[]{:S(2)}, u32[]{:S(2)}) collective-permute-start(bf16[2,2,256,512]{3,2,1,0:T(8,128)(2,1)} %add_convert_fusion.4.refs_1_), channel_id=1, source_target_pairs={{0,8},{4,12},{1,9},{5,13},{2,10},{6,14},{3,11},{7,15}} | collective-permute-start | bytes 3145736 | tf_op jit(solution)/shard_map/ppermute | solution.py:42
  812.3 47.7 %collective-permute-start.52 = (bf16[848,128]{1,0:T(8,128)(2,1)}, bf16[848,128]{1,0:T(8,128)(2,1)S(1)}, u32[]{:S(2)}, u32[]{:S(2)}) collective-permute-start(bf16[848,128]{1,0:T(8,128)(2,1)} %get-tuple-element.328.refs_5_), channel_id=1, source_target_pairs={{0,8},{4,12},{8,16},{12,20},{16,24},{20,28},{24,0},{28,4},{1,9},{5... | collective-permute-start | bytes 651272 | tf_op jit(solution)/shard_map/ppermute | solution.py:42
  814.3 30.7 %collective-permute-start.46 = (bf16[2,256,512]{2,1,0:T(8,128)(2,1)}, bf16[2,256,512]{2,1,0:T(8,128)(2,1)}, u32[]{:S(2)}, u32[]{:S(2)}) collective-permute-start(bf16[2,256,512]{2,1,0:T(8,128)(2,1)} %dynamic-slice_bitcast_fusion.4), channel_id=1, source_target_pairs={{24,16},{28,20},{25,17},{29,21},{26,18},{30,22},{27,19},{31,23}} | collective-permute-start | bytes 1572872 | tf_op jit(solution)/shard_map/ppermute | solution.py:42
  820.9 33.7 %collective-permute-start.48 = (bf16[2,2,256,512]{3,2,1,0:T(8,128)(2,1)}, bf16[2,2,256,512]{3,2,1,0:T(8,128)(2,1)S(1)}, u32[]{:S(2)}, u32[]{:S(2)}) collective-permute-start(bf16[2,2,256,512]{3,2,1,0:T(8,128)(2,1)} %add_convert_fusion.2.refs_1_), channel_id=1, source_target_pairs={{0,8},{4,12},{1,9},{5,13},{2,10},{6,14},{3,11},{7,15}} | collective-permute-start | bytes 3145736 | tf_op jit(solution)/shard_map/ppermute | solution.py:42
  825.0 28.0 %collective-permute-start.45 = (bf16[2,256,512]{2,1,0:T(8,128)(2,1)S(1)}, bf16[2,256,512]{2,1,0:T(8,128)(2,1)S(1)}, u32[]{:S(2)}, u32[]{:S(2)}) collective-permute-start(bf16[2,256,512]{2,1,0:T(8,128)(2,1)S(1)} %get-tuple-element.317), channel_id=1, source_target_pairs={{8,24},{12,28},{9,25},{13,29},{10,26},{14,30},{11,27},{15,31}} | collective-permute-start | bytes 1572872 | tf_op jit(solution)/shard_map/ppermute | solution.py:42
  867.1 28.6 %collective-permute-start.74 = (bf16[848,128]{1,0:T(8,128)(2,1)}, bf16[848,128]{1,0:T(8,128)(2,1)S(1)}, u32[]{:S(2)}, u32[]{:S(2)}) collective-permute-start(bf16[848,128]{1,0:T(8,128)(2,1)} %hold.65.refs_1_), channel_id=1, source_target_pairs={{0,8},{4,12},{8,16},{12,20},{16,24},{20,28},{24,0},{28,4},{1,9},{5... | collective-permute-start | bytes 651272 | tf_op jit(solution)/shard_map/ppermute | solution.py:42
  872.9 22.7 %collective-permute-start.75 = (bf16[848,128]{1,0:T(8,128)(2,1)}, bf16[848,128]{1,0:T(8,128)(2,1)S(1)}, u32[]{:S(2)}, u32[]{:S(2)}) collective-permute-start(bf16[848,128]{1,0:T(8,128)(2,1)} %hold.65.refs_1_), channel_id=1, source_target_pairs={{0,16},{4,20},{8,24},{12,28},{16,0},{20,4},{24,8},{28,12},{1,17},{... | collective-permute-start | bytes 651272 | tf_op jit(solution)/shard_map/ppermute | solution.py:42
  920.6 36.5 %collective-permute-start.62 = (bf16[4,208,128]{2,1,0:T(8,128)(2,1)S(1)}, bf16[4,208,128]{2,1,0:T(8,128)(2,1)S(1)}, u32[]{:S(2)}, u32[]{:S(2)}) collective-permute-start(bf16[4,208,128]{2,1,0:T(8,128)(2,1)S(1)} %get-tuple-element.329), channel_id=1, source_target_pairs={{0,1},{1,0},{2,3},{3,2},{4,5},{5,4},{6,7},{7,6},{8,9},{9,8},{10,11... | collective-permute-start | bytes 638984 | tf_op jit(solution)/shard_map/ppermute | solution.py:108
  922.1 35.0 %collective-permute-start.63 = (bf16[4,208,128]{2,1,0:T(8,128)(2,1)S(1)}, bf16[4,208,128]{2,1,0:T(8,128)(2,1)S(1)}, u32[]{:S(2)}, u32[]{:S(2)}) collective-permute-start(bf16[4,208,128]{2,1,0:T(8,128)(2,1)S(1)} %get-tuple-element.331), channel_id=1, source_target_pairs={{0,2},{1,3},{2,0},{3,1},{4,6},{5,7},{6,4},{7,5},{8,10},{9,11},{10,... | collective-permute-start | bytes 638984 | tf_op jit(solution)/shard_map/ppermute | solution.py:108
  923.7 33.4 %collective-permute-start.64 = (bf16[4,208,128]{2,1,0:T(8,128)(2,1)S(1)}, bf16[4,208,128]{2,1,0:T(8,128)(2,1)S(1)}, u32[]{:S(2)}, u32[]{:S(2)}) collective-permute-start(bf16[4,208,128]{2,1,0:T(8,128)(2,1)S(1)} %get-tuple-element.330), channel_id=1, source_target_pairs={{0,3},{1,2},{2,1},{3,0},{4,7},{5,6},{6,5},{7,4},{8,11},{9,10},{10,... | collective-permute-start | bytes 638984 | tf_op jit(solution)/shard_map/ppermute | solution.py:108
  924.2 28.1 %collective-permute-start.58 = (bf16[240,128]{1,0:T(8,128)(2,1)S(1)}, bf16[240,128]{1,0:T(8,128)(2,1)S(1)}, u32[]{:S(2)}, u32[]{:S(2)}) collective-permute-start(bf16[240,128]{1,0:T(8,128)(2,1)S(1)} %get-tuple-element.336), channel_id=1, source_target_pairs={{0,8},{4,12},{8,16},{12,20},{16,24},{20,28},{24,0},{28,4},{1,9},{5... | collective-permute-start | bytes 184328 | tf_op jit(solution)/shard_map/ppermute | solution.py:42
  978.8 22.5 %collective-permute-start.72 = (bf16[4,448,128]{2,1,0:T(8,128)(2,1)S(1)}, bf16[4,448,128]{2,1,0:T(8,128)(2,1)S(1)}, u32[]{:S(2)}, u32[]{:S(2)}) collective-permute-start(bf16[4,448,128]{2,1,0:T(8,128)(2,1)S(1)} %bitcast_dynamic-update-slice_fusion.36), channel_id=1, source_target_pairs={{0,2},{1,3},{2,0},{3,1},{4,6},{5,7},{6,4},{7,5},{8,10},{9,11},{10,... | collective-permute-start | bytes 1376264 | tf_op jit(solution)/shard_map/ppermute | solution.py:108
  979.2 22.1 %collective-permute-start.73 = (bf16[4,448,128]{2,1,0:T(8,128)(2,1)S(1)}, bf16[4,448,128]{2,1,0:T(8,128)(2,1)}, u32[]{:S(2)}, u32[]{:S(2)}) collective-permute-start(bf16[4,448,128]{2,1,0:T(8,128)(2,1)S(1)} %bitcast_dynamic-update-slice_fusion.36), channel_id=1, source_target_pairs={{0,3},{1,2},{2,1},{3,0},{4,7},{5,6},{6,5},{7,4},{8,11},{9,10},{10,... | collective-permute-start | bytes 1376264 | tf_op jit(solution)/shard_map/ppermute | solution.py:108
  (118 other events, 896.4 us)
Sparse Core Ops, SparseCore 0:
  41.7 68.7 all-gather.15
  112.8 100.1 all-gather.17
  255.7 94.5 all-gather.19
  352.6 106.1 all-gather.25
  461.1 76.6 all-gather.23
  540.1 57.0 all-gather.21
  901.5 69.6 all-gather.13
